TPU v7x, 256 devices: a whole 4x4x8 slice. The times are simulated.
256 devices in a mesh: ctx: 16 (over y, x_lo, core), tp: 16 (over z, x_hi).
Axes of the slice: x: 4 (x_hi: 2, x_lo: 2; x = x_hi * 2 + x_lo), y: 4, z: 8, core: 2. Of those that a mesh axis runs over, the one named last changes fastest.
Arguments:
- residual: bfloat16 [16384, 8192], P('ctx', 'tp'), may hold values from -6 to 6
- queries: bfloat16 [16, 256, 8192], P('ctx', 'tp'), may hold values from -36 to 36
- keys_values: bfloat16 [16, 256, 2048], P('ctx', 'tp'), may hold values from -6 to 6
- kept_local: int32 [16, 256], replicated, may hold values from 0 to 1024, as said below
- router_weight: bfloat16 [16, 256], P('ctx'), may hold values from 0.25 to 1
Outputs:
- layer_out: bfloat16 [16384, 8192], P('ctx', 'tp')
Inputs may be any that keep to these rules, and one draw needn't show every extreme that they name: `kept_local`: row j lists in rising order the distinct positions of block j's kept tokens, then 1024 in the remaining slots. All blocks together keep exactly 2048 tokens, every block keeps 2 or more, and some block keeps exactly 256.
All inputs are finite; a program needn't handle non-finite values.
Results may differ from a plain program's by a relative error of at most 0.0011.
Values may be sent and summed in bfloat16 or wider, within the bound.
No kernel may reach another device: no remote copies, remote signals or barrier semaphores. Data moves between devices by JAX's collectives and lax.ppermute only.
A program may use at most 64 MiB of HBM per device.

v0:
```python
import math

import jax
import jax.numpy as jnp
from jax import lax
from jax.sharding import PartitionSpec as P

H = 64
KVH = 8
HD = 128
TOK_DEV = 1024
RATIO = 8


def passed_along(block, axis, distance):
    devices = range(lax.axis_size(axis))
    route = [((i - distance) % len(devices), i) for i in devices]
    return lax.ppermute(block, axis, route)


def table_read(table_values, where_at):
    matches = where_at[..., None] == jnp.arange(table_values.shape[0], dtype=jnp.int32)
    return jnp.sum(jnp.where(matches, table_values, 0), axis=-1)


def rank_of(shard_index, slot_in, cycle_size):
    return slot_in * cycle_size + shard_index


def shard_of(rank_value, cycle_size):
    return rank_value % cycle_size


def ranks_below(limit, shard_index, cycle_size):
    return jnp.maximum(0, (limit - shard_index + cycle_size - 1) // cycle_size)


def attend(running, arrived, key_rank, grouped, query_rank, score_scale):
    running_max, running_sum, summed = running
    key_count = arrived.shape[0]
    kv_groups = grouped.shape[1]
    split_pairs = arrived.reshape(key_count, kv_groups, 2, grouped.shape[3])
    scores = (
        jnp.einsum(
            "qgnd,kgd->gnqk", grouped, split_pairs[:, :, 0], preferred_element_type=jnp.float32
        )
        * score_scale
    )
    visible = key_rank[None, :] <= query_rank[:, None]
    scores = jnp.where(visible, scores, -jnp.inf)
    newest = jnp.maximum(running_max, jnp.max(scores, axis=-1))
    anchor = jnp.where(jnp.isfinite(newest), newest, 0.0)
    factor = jnp.exp(running_max - anchor)
    weights = jnp.exp(scores - anchor[..., None])
    running_sum = running_sum * factor + jnp.sum(weights, axis=-1)
    product = jnp.einsum(
        "gnqk,kgd->qgnd",
        weights.astype(jnp.bfloat16),
        split_pairs[:, :, 1],
        preferred_element_type=jnp.float32,
    )
    summed = summed * jnp.transpose(factor, (2, 0, 1))[..., None] + product
    return (newest, running_sum, summed)


def shards(residual, queries, keys_values, kept_local, router_weight):
    cycle_size = lax.axis_size("ctx")
    tp_size = lax.axis_size("tp")
    own_index = lax.axis_index("ctx")
    capacity = kept_local.shape[1]
    rows_tp = queries.shape[1]
    shard_rows = TOK_DEV // RATIO
    heads_dev = H // tp_size
    copies = max(1, tp_size // KVH)
    kv_groups = max(1, KVH // tp_size)
    per_group = heads_dev // kv_groups
    score_scale = 1.0 / math.sqrt(HD)
    counts = jnp.sum((kept_local < TOK_DEV).astype(jnp.int32), axis=1)
    block_ends = jnp.cumsum(counts)
    starts = block_ends - counts
    own_count = table_read(counts, own_index)
    own_start = table_read(starts, own_index)
    query_rows = queries.reshape(rows_tp, tp_size, heads_dev * HD)
    pair_rows = jnp.repeat(keys_values.reshape(rows_tp, KVH, 2 * HD), copies, axis=1)
    own_queries, own_pairs = (
        lax.all_to_all(query_rows, "tp", split_axis=1, concat_axis=0, tiled=True),
        lax.all_to_all(pair_rows, "tp", split_axis=1, concat_axis=0, tiled=True),
    )
    own_queries = own_queries.reshape(capacity, heads_dev * HD)
    own_pairs = own_pairs.reshape(capacity, kv_groups * 2 * HD)
    own_router = router_weight[0]
    slot_index = jnp.arange(capacity, dtype=jnp.int32)
    own_rank = own_start + slot_index
    live_slot = slot_index < own_count
    pair_cap = capacity // cycle_size
    slots_all = cycle_size * pair_cap
    target = shard_of(own_rank, cycle_size)
    pair_slot = ranks_below(own_rank, target, cycle_size) - ranks_below(
        own_start, target, cycle_size
    )
    destination = jnp.where(live_slot, target * pair_cap + pair_slot, slots_all)
    source_of = (
        jnp.full((slots_all,), capacity, jnp.int32).at[destination].set(slot_index, mode="drop")
    )
    taken_mask = source_of < capacity
    picked = jnp.minimum(source_of, capacity - 1)
    send_queries = jnp.where(taken_mask[:, None], own_queries[picked], 0)
    send_pairs = jnp.where(taken_mask[:, None], own_pairs[picked], 0)
    send_router = jnp.where(taken_mask, own_router[picked], 0)
    send_queries = send_queries.reshape(cycle_size, pair_cap, heads_dev * HD)
    send_pairs = send_pairs.reshape(cycle_size, pair_cap, kv_groups * 2 * HD)
    send_router = send_router.reshape(cycle_size, pair_cap)
    got_queries, got_pairs, got_router = (
        lax.all_to_all(send_queries, "ctx", split_axis=0, concat_axis=0, tiled=True),
        lax.all_to_all(send_pairs, "ctx", split_axis=0, concat_axis=0, tiled=True),
        lax.all_to_all(send_router, "ctx", split_axis=0, concat_axis=0, tiled=True),
    )
    shard_slots = jnp.arange(shard_rows, dtype=jnp.int32)
    query_rank = rank_of(own_index, shard_slots, cycle_size)
    sender = jnp.sum((block_ends[None, :] <= query_rank[:, None]).astype(jnp.int32), axis=1)
    sender_start = table_read(starts, sender)
    pair_in = shard_slots - ranks_below(sender_start, own_index, cycle_size)
    flat_index = sender * pair_cap + pair_in
    query_block = got_queries.reshape(slots_all, heads_dev * HD)[flat_index]
    local_pairs = got_pairs.reshape(slots_all, kv_groups * 2 * HD)[flat_index]
    query_router = got_router.reshape(slots_all)[flat_index]

    def key_rank_of(global_rows):
        return rank_of(global_rows // shard_rows, global_rows % shard_rows, cycle_size)

    grouped = query_block.reshape(shard_rows, kv_groups, per_group, HD)
    start_state = (
        jnp.full((kv_groups, per_group, shard_rows), -jnp.inf, jnp.float32),
        jnp.zeros((kv_groups, per_group, shard_rows), jnp.float32),
        jnp.zeros((shard_rows, kv_groups, per_group, HD), jnp.float32),
    )

    def absorb(running, arrived, first_row):
        global_rows = first_row + jnp.arange(arrived.shape[0], dtype=jnp.int32)
        return attend(running, arrived, key_rank_of(global_rows), grouped, query_rank, score_scale)

    running = absorb(start_state, local_pairs, own_index * shard_rows)

    def cycle_turn(turn_index, carried):
        running_now, moving = carried
        moving = passed_along(moving, "ctx", 1)
        source = (own_index - turn_index - 1) % cycle_size
        return (absorb(running_now, moving, source * shard_rows), moving)

    running, _ = lax.fori_loop(0, cycle_size - 1, cycle_turn, (running, local_pairs))
    _, running_sum, summed = running
    attention = (summed / jnp.transpose(running_sum, (2, 0, 1))[..., None]).reshape(
        shard_rows, heads_dev * HD
    )
    update = (query_router.astype(jnp.float32)[:, None] * attention).astype(jnp.bfloat16)
    send_back = jnp.zeros((slots_all, heads_dev * HD), jnp.bfloat16).at[flat_index].set(update)
    send_back = send_back.reshape(cycle_size, pair_cap, heads_dev * HD)
    returned_rows = lax.all_to_all(send_back, "ctx", split_axis=0, concat_axis=0, tiled=True)
    own_update = returned_rows.reshape(slots_all, heads_dev * HD)[
        jnp.minimum(destination, slots_all - 1)
    ]
    own_rows = lax.dynamic_index_in_dim(kept_local, own_index, 0, keepdims=False)
    kept_update = lax.optimization_barrier(own_update).astype(jnp.float32)
    layer_out = residual.astype(jnp.float32).at[own_rows].add(kept_update, mode="drop")
    return layer_out.astype(jnp.bfloat16)


def solution(mesh):
    placed = (P("ctx", "tp"), P("ctx", "tp", None), P("ctx", "tp", None), P(), P("ctx", None))
    return jax.shard_map(
        shards, mesh=mesh, in_specs=placed, out_specs=P("ctx", "tp"), check_vma=False
    )
```

profile of v0, /device:TPU:1, one launch (start us, length us, event | category | flops | bytes accessed | tf_op | source)
XLA Modules:
  0.0 194.6 jit_solution(2949798560507999358)
XLA Ops:
  1.5 11.6 %all-to-all-start.1 = ((bf16[16,16,256]{2,0,1:T(8,128)(2,1)}), bf16[16,16,256]{2,0,1:T(8,128)(2,1)S(1)}, u32[]{:S(2)}, u32[]{:S(2)}) async-start(bf16[16,16,256]{2,0,1:T(8,128)(2,1)} %bitcast.7), calls=%async_computation.1 | async-start | bytes 262144 | tf_op jit(solution)/shard_map/all_to_all | solution.py:87
  16.1 1.4 scatter_custom_fusion
  19.4 1.9 gather_fusion
  21.3 1.8 all-to-all-done.1
  23.1 7.3 %all-to-all-start.3 = ((bf16[16,16,512]{2,0,1:T(8,128)(2,1)}), bf16[16,16,512]{2,0,1:T(8,128)(2,1)S(1)}, u32[]{:S(2)}, u32[]{:S(2)}) async-start(bf16[16,16,512]{2,0,1:T(8,128)(2,1)} %copy.68), calls=%async_computation.3 | async-start | bytes 524288 | tf_op jit(solution)/shard_map/all_to_all | solution.py:86
  32.6 9.2 %all-to-all-done.3 = bf16[16,16,512]{2,0,1:T(8,128)(2,1)S(1)} async-done(((bf16[16,16,512]{2,0,1:T(8,128)(2,1)}), bf16[16,16,512]{2,0,1:T(8,128)(2,1)S(1)}, u32[]{:S(2)}, u32[]{:S(2)}) %all-to-all-start.3) | async-done | bytes 262176 | tf_op jit(solution)/shard_map/all_to_all | solution.py:86
  41.7 7.8 %all-to-all-start = ((bf16[16,1,16]{2,1,0:T(2,128)(2,1)}), bf16[16,1,16]{2,1,0:T(2,128)(2,1)S(1)}, u32[]{:S(2)}, u32[]{:S(2)}) async-start(bf16[16,1,16]{2,1,0:T(2,128)(2,1)} %all_to_all.48), calls=%async_computation | async-start | bytes 16384 | tf_op jit(solution)/shard_map/all_to_all | solution.py:116
  51.4 3.6 %all-to-all-done = bf16[16,1,16]{2,1,0:T(2,128)(2,1)S(1)} async-done(((bf16[16,1,16]{2,1,0:T(2,128)(2,1)}), bf16[16,1,16]{2,1,0:T(2,128)(2,1)S(1)}, u32[]{:S(2)}, u32[]{:S(2)}) %all-to-all-start) | async-done | bytes 544 | tf_op jit(solution)/shard_map/all_to_all | solution.py:116
  55.0 4.0 %all-to-all-start.2 = ((bf16[16,16,256]{2,1,0:T(8,128)(2,1)}), bf16[16,16,256]{2,1,0:T(8,128)(2,1)S(1)}, u32[]{:S(2)}, u32[]{:S(2)}) async-start(bf16[16,16,256]{2,1,0:T(8,128)(2,1)} %broadcast_select_fusion.1), calls=%async_computation.2 | async-start | bytes 262144 | tf_op jit(solution)/shard_map/all_to_all | solution.py:115
  59.8 5.4 %all-to-all-done.2 = bf16[16,16,256]{2,1,0:T(8,128)(2,1)S(1)} async-done(((bf16[16,16,256]{2,1,0:T(8,128)(2,1)}), bf16[16,16,256]{2,1,0:T(8,128)(2,1)S(1)}, u32[]{:S(2)}, u32[]{:S(2)}) %all-to-all-start.2) | async-done | bytes 131104 | tf_op jit(solution)/shard_map/all_to_all | solution.py:115
  65.2 4.0 %all-to-all-start.4 = ((bf16[16,16,512]{2,1,0:T(8,128)(2,1)}), bf16[16,16,512]{2,1,0:T(8,128)(2,1)S(1)}, u32[]{:S(2)}, u32[]{:S(2)}) async-start(bf16[16,16,512]{2,1,0:T(8,128)(2,1)} %broadcast_select_fusion), calls=%async_computation.4 | async-start | bytes 524288 | tf_op jit(solution)/shard_map/all_to_all | solution.py:114
  71.7 4.8 %all-to-all-done.4 = bf16[16,16,512]{2,1,0:T(8,128)(2,1)S(1)} async-done(((bf16[16,16,512]{2,1,0:T(8,128)(2,1)}), bf16[16,16,512]{2,1,0:T(8,128)(2,1)S(1)}, u32[]{:S(2)}, u32[]{:S(2)}) %all-to-all-start.4) | async-done | bytes 262176 | tf_op jit(solution)/shard_map/all_to_all | solution.py:114
  78.0 93.7 %while.24 = (s32[]{:T(128)}, f32[1,4,128]{2,1,0:T(4,128)S(1)}, f32[1,4,128]{2,1,0:T(4,128)S(1)}, f32[128,1,4,128]{3,0,2,1:T(8,128)S(1)}, bf16[128,256]{0,1:T(8,1...) while((s32[]{:T(128)}, f32[1,4,128]{2,1,0:T(4,128)S(1)}, ...), condition=%wide.region_12.13_spmd.clone.clone, body=%wide.region_9.12_spmd.clone.clone.sunk | while | flops 34168336 | bytes 1972542 | solution.py:150
  81.3 2.4 %collective-permute-start = (bf16[128,256]{0,1:T(8,128)(2,1)S(1)}, bf16[128,256]{0,1:T(8,128)(2,1)S(1)}, u32[]{:S(2)}, u32[]{:S(2)}) collective-permute-start(bf16[128,256]{0,1:T(8,128)(2,1)S(1)} %get-tuple-element.420), channel_id=1, source_target_pairs={{240,0},{0,16},{16,32},{32,48},{48,64},{64,80},{80,96},{96,112},{1... | collective-permute-start | bytes 196616 | tf_op jit(solution)/shard_map/while/body/eval_jaxpr/ppermute | solution.py:18
  83.9 2.5 %collective-permute-done = bf16[128,256]{0,1:T(8,128)(2,1)S(1)} collective-permute-done((bf16[128,256]{0,1:T(8,128)(2,1)S(1)}, bf16[128,256]{0,1:T(8,128)(2,1)S(1)}, u32[]{:S(2)}, u32[]{:S(2)}) %collective-permute-start) | collective-permute-done | bytes 65568 | tf_op jit(solution)/shard_map/while/body/eval_jaxpr/ppermute | solution.py:18
  88.3 4.6 %collective-permute-done = bf16[128,256]{0,1:T(8,128)(2,1)S(1)} collective-permute-done((bf16[128,256]{0,1:T(8,128)(2,1)S(1)}, bf16[128,256]{0,1:T(8,128)(2,1)S(1)}, u32[]{:S(2)}, u32[]{:S(2)}) %collective-permute-start) | collective-permute-done | bytes 65568 | tf_op jit(solution)/shard_map/while/body/eval_jaxpr/ppermute | solution.py:18
  93.8 5.7 %collective-permute-done = bf16[128,256]{0,1:T(8,128)(2,1)S(1)} collective-permute-done((bf16[128,256]{0,1:T(8,128)(2,1)S(1)}, bf16[128,256]{0,1:T(8,128)(2,1)S(1)}, u32[]{:S(2)}, u32[]{:S(2)}) %collective-permute-start) | collective-permute-done | bytes 65568 | tf_op jit(solution)/shard_map/while/body/eval_jaxpr/ppermute | solution.py:18
  100.3 5.7 %collective-permute-done = bf16[128,256]{0,1:T(8,128)(2,1)S(1)} collective-permute-done((bf16[128,256]{0,1:T(8,128)(2,1)S(1)}, bf16[128,256]{0,1:T(8,128)(2,1)S(1)}, u32[]{:S(2)}, u32[]{:S(2)}) %collective-permute-start) | collective-permute-done | bytes 65568 | tf_op jit(solution)/shard_map/while/body/eval_jaxpr/ppermute | solution.py:18
  106.8 5.7 %collective-permute-done = bf16[128,256]{0,1:T(8,128)(2,1)S(1)} collective-permute-done((bf16[128,256]{0,1:T(8,128)(2,1)S(1)}, bf16[128,256]{0,1:T(8,128)(2,1)S(1)}, u32[]{:S(2)}, u32[]{:S(2)}) %collective-permute-start) | collective-permute-done | bytes 65568 | tf_op jit(solution)/shard_map/while/body/eval_jaxpr/ppermute | solution.py:18
  113.3 5.7 %collective-permute-done = bf16[128,256]{0,1:T(8,128)(2,1)S(1)} collective-permute-done((bf16[128,256]{0,1:T(8,128)(2,1)S(1)}, bf16[128,256]{0,1:T(8,128)(2,1)S(1)}, u32[]{:S(2)}, u32[]{:S(2)}) %collective-permute-start) | collective-permute-done | bytes 65568 | tf_op jit(solution)/shard_map/while/body/eval_jaxpr/ppermute | solution.py:18
  119.8 5.7 %collective-permute-done = bf16[128,256]{0,1:T(8,128)(2,1)S(1)} collective-permute-done((bf16[128,256]{0,1:T(8,128)(2,1)S(1)}, bf16[128,256]{0,1:T(8,128)(2,1)S(1)}, u32[]{:S(2)}, u32[]{:S(2)}) %collective-permute-start) | collective-permute-done | bytes 65568 | tf_op jit(solution)/shard_map/while/body/eval_jaxpr/ppermute | solution.py:18
  126.4 5.7 %collective-permute-done = bf16[128,256]{0,1:T(8,128)(2,1)S(1)} collective-permute-done((bf16[128,256]{0,1:T(8,128)(2,1)S(1)}, bf16[128,256]{0,1:T(8,128)(2,1)S(1)}, u32[]{:S(2)}, u32[]{:S(2)}) %collective-permute-start) | collective-permute-done | bytes 65568 | tf_op jit(solution)/shard_map/while/body/eval_jaxpr/ppermute | solution.py:18
  132.9 5.7 %collective-permute-done = bf16[128,256]{0,1:T(8,128)(2,1)S(1)} collective-permute-done((bf16[128,256]{0,1:T(8,128)(2,1)S(1)}, bf16[128,256]{0,1:T(8,128)(2,1)S(1)}, u32[]{:S(2)}, u32[]{:S(2)}) %collective-permute-start) | collective-permute-done | bytes 65568 | tf_op jit(solution)/shard_map/while/body/eval_jaxpr/ppermute | solution.py:18
  139.4 5.7 %collective-permute-done = bf16[128,256]{0,1:T(8,128)(2,1)S(1)} collective-permute-done((bf16[128,256]{0,1:T(8,128)(2,1)S(1)}, bf16[128,256]{0,1:T(8,128)(2,1)S(1)}, u32[]{:S(2)}, u32[]{:S(2)}) %collective-permute-start) | collective-permute-done | bytes 65568 | tf_op jit(solution)/shard_map/while/body/eval_jaxpr/ppermute | solution.py:18
  145.9 5.7 %collective-permute-done = bf16[128,256]{0,1:T(8,128)(2,1)S(1)} collective-permute-done((bf16[128,256]{0,1:T(8,128)(2,1)S(1)}, bf16[128,256]{0,1:T(8,128)(2,1)S(1)}, u32[]{:S(2)}, u32[]{:S(2)}) %collective-permute-start) | collective-permute-done | bytes 65568 | tf_op jit(solution)/shard_map/while/body/eval_jaxpr/ppermute | solution.py:18
  152.4 5.7 %collective-permute-done = bf16[128,256]{0,1:T(8,128)(2,1)S(1)} collective-permute-done((bf16[128,256]{0,1:T(8,128)(2,1)S(1)}, bf16[128,256]{0,1:T(8,128)(2,1)S(1)}, u32[]{:S(2)}, u32[]{:S(2)}) %collective-permute-start) | collective-permute-done | bytes 65568 | tf_op jit(solution)/shard_map/while/body/eval_jaxpr/ppermute | solution.py:18
  159.0 5.7 %collective-permute-done = bf16[128,256]{0,1:T(8,128)(2,1)S(1)} collective-permute-done((bf16[128,256]{0,1:T(8,128)(2,1)S(1)}, bf16[128,256]{0,1:T(8,128)(2,1)S(1)}, u32[]{:S(2)}, u32[]{:S(2)}) %collective-permute-start) | collective-permute-done | bytes 65568 | tf_op jit(solution)/shard_map/while/body/eval_jaxpr/ppermute | solution.py:18
  165.5 5.7 %collective-permute-done = bf16[128,256]{0,1:T(8,128)(2,1)S(1)} collective-permute-done((bf16[128,256]{0,1:T(8,128)(2,1)S(1)}, bf16[128,256]{0,1:T(8,128)(2,1)S(1)}, u32[]{:S(2)}, u32[]{:S(2)}) %collective-permute-start) | collective-permute-done | bytes 65568 | tf_op jit(solution)/shard_map/while/body/eval_jaxpr/ppermute | solution.py:18
  172.1 1.7 scatter_custom_fusion.1
  173.8 8.4 %all-to-all-start.5 = ((bf16[16,16,512]{2,1,0:T(8,128)(2,1)}), bf16[16,16,512]{2,1,0:T(8,128)(2,1)S(1)}, u32[]{:S(2)}, u32[]{:S(2)}) async-start(bf16[16,16,512]{2,1,0:T(8,128)(2,1)} %bitcast.35), calls=%async_computation.5 | async-start | bytes 524288 | tf_op jit(solution)/shard_map/all_to_all | solution.py:158
  183.2 6.2 %all-to-all-done.5 = bf16[16,16,512]{2,1,0:T(8,128)(2,1)S(1)} async-done(((bf16[16,16,512]{2,1,0:T(8,128)(2,1)}), bf16[16,16,512]{2,1,0:T(8,128)(2,1)S(1)}, u32[]{:S(2)}, u32[]{:S(2)}) %all-to-all-start.5) | async-done | bytes 262176 | tf_op jit(solution)/shard_map/all_to_all | solution.py:158
  190.6 2.9 %scatter_custom_fusion.2 = f32[1024,512]{1,0:T(8,128)S(1)} fusion(f32[1024,512]{1,0:T(8,128)S(1)} %convert_element_type.45, s32[256]{0:T(256)S(1)} %bitcast.187, bf16[256,512]{1,0:T(8,128)(2,1)S(1)} %gather_fusion.6), kind=kCustom, calls=%fused_computation.44 | custom fusion | flops 262144 | bytes 2359296 | tf_op jit(solution)/shard_map/scatter-add | solution.py:164
  (221 shorter events, 33.6 us)
Async XLA Ops:
  0.0 19.4 %copy-start = (bf16[1,256]{1,0:T(2,128)(2,1)S(1)}, bf16[1,256]{1,0:T(2,128)(2,1)}, u32[]{:S(2)}) copy-start(bf16[1,256]{1,0:T(2,128)(2,1)} %param.11) | copy-start | bytes 1540
  1.5 21.6 %all-to-all-start.1 = ((bf16[16,16,256]{2,0,1:T(8,128)(2,1)}), bf16[16,16,256]{2,0,1:T(8,128)(2,1)S(1)}, u32[]{:S(2)}, u32[]{:S(2)}) async-start(bf16[16,16,256]{2,0,1:T(8,128)(2,1)} %bitcast.7), calls=%async_computation.1 | async-start | bytes 262144 | tf_op jit(solution)/shard_map/all_to_all | solution.py:87
  23.1 18.6 %all-to-all-start.3 = ((bf16[16,16,512]{2,0,1:T(8,128)(2,1)}), bf16[16,16,512]{2,0,1:T(8,128)(2,1)S(1)}, u32[]{:S(2)}, u32[]{:S(2)}) async-start(bf16[16,16,512]{2,0,1:T(8,128)(2,1)} %copy.68), calls=%async_computation.3 | async-start | bytes 524288 | tf_op jit(solution)/shard_map/all_to_all | solution.py:86
  41.7 13.3 %all-to-all-start = ((bf16[16,1,16]{2,1,0:T(2,128)(2,1)}), bf16[16,1,16]{2,1,0:T(2,128)(2,1)S(1)}, u32[]{:S(2)}, u32[]{:S(2)}) async-start(bf16[16,1,16]{2,1,0:T(2,128)(2,1)} %all_to_all.48), calls=%async_computation | async-start | bytes 16384 | tf_op jit(solution)/shard_map/all_to_all | solution.py:116
  55.0 10.2 %all-to-all-start.2 = ((bf16[16,16,256]{2,1,0:T(8,128)(2,1)}), bf16[16,16,256]{2,1,0:T(8,128)(2,1)S(1)}, u32[]{:S(2)}, u32[]{:S(2)}) async-start(bf16[16,16,256]{2,1,0:T(8,128)(2,1)} %broadcast_select_fusion.1), calls=%async_computation.2 | async-start | bytes 262144 | tf_op jit(solution)/shard_map/all_to_all | solution.py:115
  65.2 11.2 %all-to-all-start.4 = ((bf16[16,16,512]{2,1,0:T(8,128)(2,1)}), bf16[16,16,512]{2,1,0:T(8,128)(2,1)S(1)}, u32[]{:S(2)}, u32[]{:S(2)}) async-start(bf16[16,16,512]{2,1,0:T(8,128)(2,1)} %broadcast_select_fusion), calls=%async_computation.4 | async-start | bytes 524288 | tf_op jit(solution)/shard_map/all_to_all | solution.py:114
  78.0 2.6 %collective-permute-start = (bf16[128,256]{0,1:T(8,128)(2,1)S(1)}, bf16[128,256]{0,1:T(8,128)(2,1)S(1)}, u32[]{:S(2)}, u32[]{:S(2)}) collective-permute-start(bf16[128,256]{0,1:T(8,128)(2,1)S(1)} %get-tuple-element.420), channel_id=1, source_target_pairs={{240,0},{0,16},{16,32},{32,48},{48,64},{64,80},{80,96},{96,112},{1... | collective-permute-start | bytes 196616 | tf_op jit(solution)/shard_map/while/body/eval_jaxpr/ppermute | solution.py:18
  81.3 5.1 %collective-permute-start = (bf16[128,256]{0,1:T(8,128)(2,1)S(1)}, bf16[128,256]{0,1:T(8,128)(2,1)S(1)}, u32[]{:S(2)}, u32[]{:S(2)}) collective-permute-start(bf16[128,256]{0,1:T(8,128)(2,1)S(1)} %get-tuple-element.420), channel_id=1, source_target_pairs={{240,0},{0,16},{16,32},{32,48},{48,64},{64,80},{80,96},{96,112},{1... | collective-permute-start | bytes 196616 | tf_op jit(solution)/shard_map/while/body/eval_jaxpr/ppermute | solution.py:18
  87.0 5.9 %collective-permute-start = (bf16[128,256]{0,1:T(8,128)(2,1)S(1)}, bf16[128,256]{0,1:T(8,128)(2,1)S(1)}, u32[]{:S(2)}, u32[]{:S(2)}) collective-permute-start(bf16[128,256]{0,1:T(8,128)(2,1)S(1)} %get-tuple-element.420), channel_id=1, source_target_pairs={{240,0},{0,16},{16,32},{32,48},{48,64},{64,80},{80,96},{96,112},{1... | collective-permute-start | bytes 196616 | tf_op jit(solution)/shard_map/while/body/eval_jaxpr/ppermute | solution.py:18
  93.6 5.9 %collective-permute-start = (bf16[128,256]{0,1:T(8,128)(2,1)S(1)}, bf16[128,256]{0,1:T(8,128)(2,1)S(1)}, u32[]{:S(2)}, u32[]{:S(2)}) collective-permute-start(bf16[128,256]{0,1:T(8,128)(2,1)S(1)} %get-tuple-element.420), channel_id=1, source_target_pairs={{240,0},{0,16},{16,32},{32,48},{48,64},{64,80},{80,96},{96,112},{1... | collective-permute-start | bytes 196616 | tf_op jit(solution)/shard_map/while/body/eval_jaxpr/ppermute | solution.py:18
  100.1 5.9 %collective-permute-start = (bf16[128,256]{0,1:T(8,128)(2,1)S(1)}, bf16[128,256]{0,1:T(8,128)(2,1)S(1)}, u32[]{:S(2)}, u32[]{:S(2)}) collective-permute-start(bf16[128,256]{0,1:T(8,128)(2,1)S(1)} %get-tuple-element.420), channel_id=1, source_target_pairs={{240,0},{0,16},{16,32},{32,48},{48,64},{64,80},{80,96},{96,112},{1... | collective-permute-start | bytes 196616 | tf_op jit(solution)/shard_map/while/body/eval_jaxpr/ppermute | solution.py:18
  106.6 5.9 %collective-permute-start = (bf16[128,256]{0,1:T(8,128)(2,1)S(1)}, bf16[128,256]{0,1:T(8,128)(2,1)S(1)}, u32[]{:S(2)}, u32[]{:S(2)}) collective-permute-start(bf16[128,256]{0,1:T(8,128)(2,1)S(1)} %get-tuple-element.420), channel_id=1, source_target_pairs={{240,0},{0,16},{16,32},{32,48},{48,64},{64,80},{80,96},{96,112},{1... | collective-permute-start | bytes 196616 | tf_op jit(solution)/shard_map/while/body/eval_jaxpr/ppermute | solution.py:18
  113.1 5.9 %collective-permute-start = (bf16[128,256]{0,1:T(8,128)(2,1)S(1)}, bf16[128,256]{0,1:T(8,128)(2,1)S(1)}, u32[]{:S(2)}, u32[]{:S(2)}) collective-permute-start(bf16[128,256]{0,1:T(8,128)(2,1)S(1)} %get-tuple-element.420), channel_id=1, source_target_pairs={{240,0},{0,16},{16,32},{32,48},{48,64},{64,80},{80,96},{96,112},{1... | collective-permute-start | bytes 196616 | tf_op jit(solution)/shard_map/while/body/eval_jaxpr/ppermute | solution.py:18
  119.6 5.9 %collective-permute-start = (bf16[128,256]{0,1:T(8,128)(2,1)S(1)}, bf16[128,256]{0,1:T(8,128)(2,1)S(1)}, u32[]{:S(2)}, u32[]{:S(2)}) collective-permute-start(bf16[128,256]{0,1:T(8,128)(2,1)S(1)} %get-tuple-element.420), channel_id=1, source_target_pairs={{240,0},{0,16},{16,32},{32,48},{48,64},{64,80},{80,96},{96,112},{1... | collective-permute-start | bytes 196616 | tf_op jit(solution)/shard_map/while/body/eval_jaxpr/ppermute | solution.py:18
  126.1 5.9 %collective-permute-start = (bf16[128,256]{0,1:T(8,128)(2,1)S(1)}, bf16[128,256]{0,1:T(8,128)(2,1)S(1)}, u32[]{:S(2)}, u32[]{:S(2)}) collective-permute-start(bf16[128,256]{0,1:T(8,128)(2,1)S(1)} %get-tuple-element.420), channel_id=1, source_target_pairs={{240,0},{0,16},{16,32},{32,48},{48,64},{64,80},{80,96},{96,112},{1... | collective-permute-start | bytes 196616 | tf_op jit(solution)/shard_map/while/body/eval_jaxpr/ppermute | solution.py:18
  132.7 5.9 %collective-permute-start = (bf16[128,256]{0,1:T(8,128)(2,1)S(1)}, bf16[128,256]{0,1:T(8,128)(2,1)S(1)}, u32[]{:S(2)}, u32[]{:S(2)}) collective-permute-start(bf16[128,256]{0,1:T(8,128)(2,1)S(1)} %get-tuple-element.420), channel_id=1, source_target_pairs={{240,0},{0,16},{16,32},{32,48},{48,64},{64,80},{80,96},{96,112},{1... | collective-permute-start | bytes 196616 | tf_op jit(solution)/shard_map/while/body/eval_jaxpr/ppermute | solution.py:18
  139.2 5.9 %collective-permute-start = (bf16[128,256]{0,1:T(8,128)(2,1)S(1)}, bf16[128,256]{0,1:T(8,128)(2,1)S(1)}, u32[]{:S(2)}, u32[]{:S(2)}) collective-permute-start(bf16[128,256]{0,1:T(8,128)(2,1)S(1)} %get-tuple-element.420), channel_id=1, source_target_pairs={{240,0},{0,16},{16,32},{32,48},{48,64},{64,80},{80,96},{96,112},{1... | collective-permute-start | bytes 196616 | tf_op jit(solution)/shard_map/while/body/eval_jaxpr/ppermute | solution.py:18
  145.7 5.9 %collective-permute-start = (bf16[128,256]{0,1:T(8,128)(2,1)S(1)}, bf16[128,256]{0,1:T(8,128)(2,1)S(1)}, u32[]{:S(2)}, u32[]{:S(2)}) collective-permute-start(bf16[128,256]{0,1:T(8,128)(2,1)S(1)} %get-tuple-element.420), channel_id=1, source_target_pairs={{240,0},{0,16},{16,32},{32,48},{48,64},{64,80},{80,96},{96,112},{1... | collective-permute-start | bytes 196616 | tf_op jit(solution)/shard_map/while/body/eval_jaxpr/ppermute | solution.py:18
  152.2 5.9 %collective-permute-start = (bf16[128,256]{0,1:T(8,128)(2,1)S(1)}, bf16[128,256]{0,1:T(8,128)(2,1)S(1)}, u32[]{:S(2)}, u32[]{:S(2)}) collective-permute-start(bf16[128,256]{0,1:T(8,128)(2,1)S(1)} %get-tuple-element.420), channel_id=1, source_target_pairs={{240,0},{0,16},{16,32},{32,48},{48,64},{64,80},{80,96},{96,112},{1... | collective-permute-start | bytes 196616 | tf_op jit(solution)/shard_map/while/body/eval_jaxpr/ppermute | solution.py:18
  158.7 5.9 %collective-permute-start = (bf16[128,256]{0,1:T(8,128)(2,1)S(1)}, bf16[128,256]{0,1:T(8,128)(2,1)S(1)}, u32[]{:S(2)}, u32[]{:S(2)}) collective-permute-start(bf16[128,256]{0,1:T(8,128)(2,1)S(1)} %get-tuple-element.420), channel_id=1, source_target_pairs={{240,0},{0,16},{16,32},{32,48},{48,64},{64,80},{80,96},{96,112},{1... | collective-permute-start | bytes 196616 | tf_op jit(solution)/shard_map/while/body/eval_jaxpr/ppermute | solution.py:18
  165.2 5.9 %collective-permute-start = (bf16[128,256]{0,1:T(8,128)(2,1)S(1)}, bf16[128,256]{0,1:T(8,128)(2,1)S(1)}, u32[]{:S(2)}, u32[]{:S(2)}) collective-permute-start(bf16[128,256]{0,1:T(8,128)(2,1)S(1)} %get-tuple-element.420), channel_id=1, source_target_pairs={{240,0},{0,16},{16,32},{32,48},{48,64},{64,80},{80,96},{96,112},{1... | collective-permute-start | bytes 196616 | tf_op jit(solution)/shard_map/while/body/eval_jaxpr/ppermute | solution.py:18
  171.8 10.4 %copy-start.1 = (bf16[1024,512]{1,0:T(8,128)(2,1)S(1)}, bf16[1024,512]{1,0:T(8,128)(2,1)}, u32[]{:S(2)}) copy-start(bf16[1024,512]{1,0:T(8,128)(2,1)} %param.7) | copy-start | bytes 3145732
  173.8 15.6 %all-to-all-start.5 = ((bf16[16,16,512]{2,1,0:T(8,128)(2,1)}), bf16[16,16,512]{2,1,0:T(8,128)(2,1)S(1)}, u32[]{:S(2)}, u32[]{:S(2)}) async-start(bf16[16,16,512]{2,1,0:T(8,128)(2,1)} %bitcast.35), calls=%async_computation.5 | async-start | bytes 524288 | tf_op jit(solution)/shard_map/all_to_all | solution.py:158
where the time goes:
time: 196 us; the launch traced here: 195 us
  waiting for transfers between devices  107 us (55%)
  starting transfers between devices  48.9 us (25%)
  local copies, waits for them, and re-layouts  16.4 us (8%)
  other arithmetic  12.7 us (6%)
  matrix products  7.67 us (4%)
    ppermute x15, waiting for transfers between devices, passed_along(): return lax.ppermute(block, axis, route)  76.3 us
    all_to_all x1, starting transfers between devices, shards(): lax.all_to_all(pair_rows, 'tp', split_axis=1, concat_axis=0, tiled=True)  11.6 us
    all_to_all x1, waiting for transfers between devices, shards(): lax.all_to_all(query_rows, 'tp', split_axis=1, concat_axis=0, tiled=True)  9.17 us
    all_to_all x1, starting transfers between devices, shards(): lax.all_to_all(send_back, 'ctx', split_axis=0, concat_axis=0, tiled=True)  8.37 us
    all_to_all x1, starting transfers between devices, shards(): lax.all_to_all(send_router, 'ctx', split_axis=0, concat_axis=0, tiled=True)  7.8 us
    all_to_all x1, starting transfers between devices, shards(): lax.all_to_all(query_rows, 'tp', split_axis=1, concat_axis=0, tiled=True)  7.31 us
    all_to_all x1, waiting for transfers between devices, shards(): lax.all_to_all(send_back, 'ctx', split_axis=0, concat_axis=0, tiled=True)  6.22 us
    ppermute x15, starting transfers between devices, passed_along(): return lax.ppermute(block, axis, route)  5.88 us
  transfers between devices with their start and end apart: 21, of which 21 were waited for; matrix products, arithmetic and copies ran while one was open for 9% of the time, Pallas kernels for 0%

commit v1 on v0

v1 whole, which is shorter than its diff:
```python
import math

import jax
import jax.numpy as jnp
from jax import lax
from jax.experimental import pallas as pl
from jax.experimental.pallas import tpu as pltpu
from jax.sharding import Mesh, PartitionSpec as P

H = 64
KVH = 8
HD = 128
TOK_DEV = 1024
CAP = 256
N_CTX = 16
HEADS = 4
ROWS = HEADS * CAP
HALF = 128
GRAN = 16
TILE = 256
CTX = ("y", "xl", "co")
TP = ("z", "xh")
BF = jnp.bfloat16
F32 = jnp.float32
EXP2_SCALE = math.log2(math.e) / math.sqrt(HD)
CONTRACT_LAST = (((1,), (1,)), ((), ()))


def shift(block, axis, distance):
    size = lax.axis_size(axis)
    return lax.ppermute(block, axis, [(i, (i + distance) % size) for i in range(size)])


def shift_x(block, distance):
    def at(x):
        return (x % 2) * 2 + x // 2

    return lax.ppermute(block, ("xl", "xh"), [(at(x), at((x + distance) % 4)) for x in range(4)])


def compact(pieces, rows, live_ref, offset_ref, fill_key, k_buf, v_buf):
    ones = jnp.ones((rows, HD), BF)
    row_in = lax.broadcasted_iota(jnp.int32, (GRAN, 2 * HD), 0)
    for at, (piece, first) in enumerate(pieces):
        live = live_ref[at]
        start = pl.multiple_of(offset_ref[at], GRAN)

        @pl.when(live > 0)
        def _():
            k_buf[pl.ds(start, rows), :] = piece[first : first + rows, :HD]
            v_buf[pl.ds(start, rows), :HD] = piece[first : first + rows, HD:]
            v_buf[pl.ds(start, rows), HD:] = ones

        @pl.when(live % GRAN > 0)
        def _():
            edge = pl.multiple_of(start + (live // GRAN) * GRAN, GRAN)
            inside = row_in < live % GRAN
            keys = k_buf[pl.ds(edge, GRAN), :].astype(F32)
            values = v_buf[pl.ds(edge, GRAN), :].astype(F32)
            fill = jnp.broadcast_to(fill_key.astype(F32), (GRAN, HD))
            k_buf[pl.ds(edge, GRAN), :] = jnp.where(inside[:, :HD], keys, fill).astype(BF)
            v_buf[pl.ds(edge, GRAN), :] = jnp.where(inside, values, 0.0).astype(BF)

    end = pl.multiple_of(offset_ref[len(pieces)], GRAN)
    k_buf[pl.ds(end, TILE), :] = jnp.broadcast_to(fill_key, (TILE, HD))
    v_buf[pl.ds(end, TILE), :] = jnp.zeros((TILE, 2 * HD), BF)
    return (end + TILE - 1) // TILE


def lane_max(scores):
    return jnp.maximum(scores[:, :HD], scores[:, HD:])


def twice(column):
    return jnp.concatenate([column, column], axis=1)


def score_tiles(tiles, q_all, k_buf, s_buf, top_buf):
    def one_tile(tile, _):
        first = pl.multiple_of(tile * TILE, TILE)
        scores = lax.dot_general(
            q_all[...], k_buf[pl.ds(first, TILE), :], CONTRACT_LAST, preferred_element_type=F32
        )
        s_buf[tile] = scores
        top_buf[...] = jnp.maximum(top_buf[...], lane_max(scores))
        return 0

    lax.fori_loop(0, tiles, one_tile, 0)


def weigh_tiles(tiles, top, v_buf, s_buf, sum_ref):
    def one_tile(tile, _):
        first = pl.multiple_of(tile * TILE, TILE)
        weights = jnp.exp2(s_buf[tile] * EXP2_SCALE - twice(top)).astype(BF)
        sum_ref[...] += jnp.dot(weights, v_buf[pl.ds(first, TILE), :], preferred_element_type=F32)
        return 0

    lax.fori_loop(0, tiles, one_tile, 0)


def heads_below(q_ref, q_all):
    for head in range(HEADS):
        q_all[head * CAP : (head + 1) * CAP, :] = q_ref[:, head * HD : (head + 1) * HD]


def near_kernel(live_ref, offset_ref, q_ref, col_ref, other_ref, kept_ref, top_ref, sum_ref, chosen_ref, q_all, k_buf, v_buf, s_buf, near_buf):
    heads_below(q_ref, q_all)
    fill_key = col_ref[0:1, :HD]
    pieces = [(col_ref, CAP * i) for i in (1, 2, 3)] + [(other_ref, CAP * i) for i in range(4)]
    tiles = compact(pieces, CAP, live_ref, offset_ref, fill_key, k_buf, v_buf)
    scores = lax.dot_general(q_all[...], col_ref[:CAP, :HD], CONTRACT_LAST, preferred_element_type=F32)
    rows = lax.broadcasted_iota(jnp.int32, (ROWS, CAP), 0) % CAP
    cols = lax.broadcasted_iota(jnp.int32, (ROWS, CAP), 1)
    scores = jnp.where(cols <= rows, scores, -1e30)
    near_buf[...] = scores
    top_ref[...] = lane_max(scores)
    score_tiles(tiles, q_all, k_buf, s_buf, top_ref)
    top = jnp.broadcast_to(jnp.max(top_ref[...], axis=1, keepdims=True), (ROWS, HD))
    top_ref[...] = top
    top = top * EXP2_SCALE
    weights = jnp.exp2(near_buf[...] * EXP2_SCALE - twice(top)).astype(BF)
    values = jnp.concatenate([col_ref[:CAP, HD:], jnp.ones((CAP, HD), BF)], axis=1)
    sum_ref[...] = jnp.dot(weights, values, preferred_element_type=F32)
    weigh_tiles(tiles, top, v_buf, s_buf, sum_ref)
    place = lax.broadcasted_iota(jnp.int32, (TOK_DEV, CAP), 0)
    chosen_ref[...] = jnp.where(place == kept_ref[...], 1.0, 0.0).astype(BF)


def far_kernel(live_ref, offset_ref, q_ref, col_ref, a_ref, b_ref, oa_ref, ob_ref, top1_ref, sum1_ref, chosen_ref, router_ref, residual_ref, out_ref, q_all, k_buf, v_buf, s_buf, top_buf, sum_buf, out_buf, sems):
    heads_below(q_ref, q_all)
    fill_key = col_ref[0:1, :HD]
    pieces = [(ref, HALF * i) for ref in (a_ref, b_ref, oa_ref, ob_ref) for i in range(4)]
    tiles = compact(pieces, HALF, live_ref, offset_ref, fill_key, k_buf, v_buf)
    top_buf[...] = top1_ref[...]
    score_tiles(tiles, q_all, k_buf, s_buf, top_buf)
    top = jnp.broadcast_to(jnp.max(top_buf[...], axis=1, keepdims=True), (ROWS, HD))
    factor = jnp.exp2((top1_ref[...] - top) * EXP2_SCALE)
    sum_buf[...] = sum1_ref[...] * twice(factor)
    weigh_tiles(tiles, top * EXP2_SCALE, v_buf, s_buf, sum_buf)
    updates = []
    for head in range(HEADS):
        now = slice(head * CAP, (head + 1) * CAP)
        attention = sum_buf[now, :HD] / sum_buf[now, HD:]
        updates.append((router_ref[...] * attention).astype(BF))
    update = jnp.concatenate(updates, axis=1)
    copies = []
    for part, row in enumerate(range(0, TOK_DEV, CAP)):
        now = slice(row, row + CAP)
        added = jnp.dot(chosen_ref[now, :], update, preferred_element_type=F32)
        out_buf[now, :] = (residual_ref[now, :].astype(F32) + added).astype(BF)
        copy = pltpu.make_async_copy(out_buf.at[now], out_ref.at[now], sems.at[part])
        copy.start()
        copies.append(copy)
    for copy in copies:
        copy.wait()


VMEM = pl.BlockSpec(memory_space=pltpu.VMEM)
SMEM = pl.BlockSpec(memory_space=pltpu.SMEM)


def near_part(live, offset, query_rows, col, other, own_kept):
    reach = 7 * CAP
    return pl.pallas_call(
        near_kernel,
        out_shape=[
            jax.ShapeDtypeStruct((ROWS, HD), F32),
            jax.ShapeDtypeStruct((ROWS, 2 * HD), F32),
            jax.ShapeDtypeStruct((TOK_DEV, CAP), BF),
        ],
        in_specs=[SMEM, SMEM] + [VMEM] * 4,
        out_specs=[VMEM] * 3,
        scratch_shapes=[
            pltpu.VMEM((ROWS, HD), BF),
            pltpu.VMEM((reach + TILE, HD), BF),
            pltpu.VMEM((reach + TILE, 2 * HD), BF),
            pltpu.VMEM((reach // TILE, ROWS, TILE), F32),
            pltpu.VMEM((ROWS, CAP), F32),
        ],
        cost_estimate=pl.CostEstimate(flops=2_000_000_000, bytes_accessed=4_000_000, transcendentals=1_500_000),
        compiler_params=pltpu.CompilerParams(vmem_limit_bytes=20 * 1024 * 1024),
    )(live, offset, query_rows, col, other, own_kept)


def far_part(live, offset, query_rows, col, gathered, near, router, residual):
    reach = 8 * CAP
    return pl.pallas_call(
        far_kernel,
        out_shape=jax.ShapeDtypeStruct((TOK_DEV, HEADS * HD), BF),
        in_specs=[SMEM, SMEM] + [VMEM] * 11,
        out_specs=pl.BlockSpec(memory_space=pl.ANY),
        scratch_shapes=[
            pltpu.VMEM((ROWS, HD), BF),
            pltpu.VMEM((reach + TILE, HD), BF),
            pltpu.VMEM((reach + TILE, 2 * HD), BF),
            pltpu.VMEM((reach // TILE, ROWS, TILE), F32),
            pltpu.VMEM((ROWS, HD), F32),
            pltpu.VMEM((ROWS, 2 * HD), F32),
            pltpu.VMEM((TOK_DEV, HEADS * HD), BF),
            pltpu.SemaphoreType.DMA((4,)),
        ],
        compiler_params=pltpu.CompilerParams(vmem_limit_bytes=24 * 1024 * 1024),
    )(live, offset, query_rows, col, *gathered, *near, router, residual)


def live_rows(counts, block, own, first, rows):
    block_count = jnp.sum(jnp.where(block[:, None] == jnp.arange(N_CTX), counts[None, :], 0), axis=1)
    live = jnp.where(block < own, jnp.clip(block_count - first, 0, rows), 0)
    taken = (live + GRAN - 1) // GRAN * GRAN
    size = block.shape[0]
    before = jnp.arange(size + 1)[:, None] > jnp.arange(size)[None, :]
    return live, jnp.sum(jnp.where(before, taken[None, :], 0), axis=1).astype(jnp.int32)


def shards(residual, queries, keys_values, kept_local, router_weight):
    y, xl, co = (lax.axis_index(a) for a in CTX)
    own = (y * 2 + xl) * 2 + co
    rows_tp = queries.shape[1]
    pairs = keys_values.reshape(rows_tp, KVH, 1, 2 * HD)
    pairs = jnp.broadcast_to(pairs, (rows_tp, KVH, 2, 2 * HD)).reshape(rows_tp, 2 * KVH, 2 * HD)
    pairs = lax.all_to_all(pairs, TP, split_axis=1, concat_axis=0, tiled=True)
    pairs = pairs.reshape(CAP, 2 * HD)
    query_rows = queries.reshape(rows_tp, 2 * KVH, HEADS * HD)
    query_rows = lax.all_to_all(query_rows, TP, split_axis=1, concat_axis=0, tiled=True)
    query_rows = query_rows.reshape(CAP, HEADS * HD)

    behind_2, behind_1, behind_3 = (shift(pairs, "y", d) for d in (2, 1, 3))
    col = jnp.concatenate([pairs, behind_1, behind_3, behind_2], axis=0)
    halves = col.reshape(4, 2, HALF, 2 * HD)
    lower = shift_x(halves[:, 0].reshape(4 * HALF, 2 * HD), 1)
    upper = shift_x(halves[:, 1].reshape(4 * HALF, 2 * HD), 3)
    other = shift(col, "co", 1)
    gathered = [lower, upper, shift(lower, "co", 1), shift(upper, "co", 1)]

    counts = jnp.sum((kept_local < TOK_DEV).astype(jnp.int32), axis=1)
    y_of = [(y - d) % 4 for d in (0, 1, 3, 2)]

    def block_of(row, x, core):
        return (row * 2 + x) * 2 + core

    near_block = jnp.stack([block_of(r, xl, co) for r in y_of[1:]] + [block_of(r, xl, 1 - co) for r in y_of])
    near_live, near_offset = live_rows(counts, near_block, own, 0, CAP)
    far_block = jnp.stack([block_of(r, 1 - xl, c) for c in (co, 1 - co) for _ in (0, 1) for r in y_of])
    far_first = jnp.array(([0] * 4 + [HALF] * 4) * 2, jnp.int32)
    far_live, far_offset = live_rows(counts, far_block, own, far_first, HALF)

    own_kept = lax.dynamic_slice_in_dim(kept_local, own, 1, axis=0)
    router = jnp.broadcast_to(router_weight[0].astype(F32)[:, None], (CAP, HD))
    near = near_part(near_live, near_offset, query_rows, col, other, own_kept)
    return far_part(far_live, far_offset, query_rows, col, gathered, near, router, residual)


def solution(mesh):
    grid = Mesh(mesh.devices.reshape(4, 2, 2, 8, 2), CTX + TP)
    placed = (P(CTX, TP), P(CTX, TP, None), P(CTX, TP, None), P(), P(CTX, None))
    return jax.shard_map(shards, mesh=grid, in_specs=placed, out_specs=P(CTX, TP), check_vma=False)
```

time: 196 us -> 57 us (0.29)
  the two profiles are of different devices: /device:TPU:1 before, /device:TPU:31 now
where the time goes in v1:
time: 57 us; the launch traced here: 56.2 us
  starting transfers between devices  27.5 us (48%)
  waiting for transfers between devices  14.3 us (25%)
  Pallas kernels  9.39 us (16%)
  local copies, waits for them, and re-layouts  4.07 us (7%)
  other arithmetic  0.75 us (1%)
    all_to_all x1, starting transfers between devices, shards(): pairs = lax.all_to_all(pairs, TP, split_axis=1, concat_axis=0, tiled=True)  11 us
    ppermute x6, starting transfers between devices, shift(): lax.ppermute(block, axis, [(i, (i + distance) % size) for i in range(size)])  8.96 us
    all_to_all x1, starting transfers between devices, shards(): lax.all_to_all(query_rows, TP, split_axis=1, concat_axis=0, tiled=True)  6 us
    ppermute x2, waiting for transfers between devices, shift_x(): lax.ppermute(block, ('xl', 'xh'), [(at(x), at((x + distance) % 4)) for x...  5.8 us
    all_to_all x1, waiting for transfers between devices, shards(): pairs = lax.all_to_all(pairs, TP, split_axis=1, concat_axis=0, tiled=True)  5.44 us
    pallas_call x1, Pallas kernels, far_part(): pl.pallas_call(far_kernel, out_shape=jax.ShapeDtypeStruct((TOK_DEV, HEADS...  5.15 us
    pallas_call x1, Pallas kernels, near_part(): pl.pallas_call(near_kernel, out_shape=[jax.ShapeDtypeStruct((ROWS, HD), F...  4.24 us
    ppermute x6, waiting for transfers between devices, shift(): lax.ppermute(block, axis, [(i, (i + distance) % size) for i in range(size)])  3.08 us
  transfers between devices with their start and end apart: 10, of which 5 were waited for; matrix products, arithmetic and copies ran while one was open for 3% of the time, Pallas kernels for 8%

profile of v1, /device:TPU:31, one launch (start us, length us, event | category | flops | bytes accessed | tf_op | source)
XLA Modules:
  0.0 56.2 jit_solution(4363286685328126584)
XLA Ops:
  0.0 0.9 %copy.18 = bf16[2,8,8,256]{3,2,1,0:T(8,128)(2,1)S(1)} copy(bf16[2,8,8,256]{3,1,2,0:T(8,128)(2,1)} %bitcast.52) | data formatting | bytes 131072
  0.9 0.7 %broadcast_in_dim.82 = bf16[16,8,2,256]{3,0,2,1:T(8,128)(2,1)} broadcast(bf16[16,8,256]{2,0,1:T(8,128)(2,1)S(1)} %copy.12), dimensions={0,1,3} | broadcast | bytes 196608 | tf_op jit(solution)/shard_map/broadcast_in_dim | solution.py:220
  1.5 11.0 %all-to-all-start.1 = ((bf16[16,16,256]{2,0,1:T(8,128)(2,1)}), bf16[16,16,256]{2,0,1:T(8,128)(2,1)S(1)}, u32[]{:S(2)}, u32[]{:S(2)}) async-start(bf16[16,16,256]{2,0,1:T(8,128)(2,1)} %bitcast.11), calls=%async_computation.1 | async-start | bytes 262144 | tf_op jit(solution)/shard_map/all_to_all | solution.py:221
  12.6 0.1 copy.17
  12.6 0.9 %copy.11 = bf16[16,16,512]{2,0,1:T(8,128)(2,1)} copy(bf16[16,16,512]{2,1,0:T(8,128)(2,1)S(1)} %bitcast.43) | data formatting | bytes 524288 | tf_op jit(solution)/shard_map/reshape | solution.py:223
  13.5 0.1 stack.67
  13.6 0.6 %copy-done.2 = s32[16,256]{1,0:T(8,128)S(1)} copy-done((s32[16,256]{1,0:T(8,128)S(1)}, s32[16,256]{1,0:T(8,128)}, u32[]{:S(2)}) %copy-start.2) | copy-done | bytes 16408
  14.2 0.1 convert_reduce_fusion
  14.3 0.2 select_reduce_fusion.1
  14.5 5.4 %all-to-all-done.1 = bf16[16,16,256]{2,0,1:T(8,128)(2,1)S(1)} async-done(((bf16[16,16,256]{2,0,1:T(8,128)(2,1)}), bf16[16,16,256]{2,0,1:T(8,128)(2,1)S(1)}, u32[]{:S(2)}, u32[]{:S(2)}) %all-to-all-start.1) | async-done | bytes 131104 | tf_op jit(solution)/shard_map/all_to_all | solution.py:221
  20.0 6.0 %all-to-all-start = ((bf16[16,16,512]{2,0,1:T(8,128)(2,1)}), bf16[16,16,512]{2,0,1:T(8,128)(2,1)S(1)}, u32[]{:S(2)}, u32[]{:S(2)}) async-start(bf16[16,16,512]{2,0,1:T(8,128)(2,1)} %copy.11), calls=%async_computation | async-start | bytes 524288 | tf_op jit(solution)/shard_map/all_to_all | solution.py:224
  26.0 1.0 %collective-permute-start.2 = (bf16[256,256]{1,0:T(8,128)(2,1)S(1)}, bf16[256,256]{1,0:T(8,128)(2,1)S(1)}, u32[]{:S(2)}, u32[]{:S(2)}) collective-permute-start(bf16[256,256]{1,0:T(8,128)(2,1)S(1)} %bitcast.44), channel_id=1, source_target_pairs={{0,128},{64,192},{128,0},{192,64},{1,129},{65,193},{129,1},{193,65... | collective-permute-start | bytes 393224 | tf_op jit(solution)/shard_map/ppermute | solution.py:31
  27.0 2.7 %collective-permute-start = (bf16[256,256]{1,0:T(8,128)(2,1)S(1)}, bf16[256,256]{1,0:T(8,128)(2,1)S(1)}, u32[]{:S(2)}, u32[]{:S(2)}) collective-permute-start(bf16[256,256]{1,0:T(8,128)(2,1)S(1)} %bitcast.46), channel_id=1, source_target_pairs={{0,64},{64,128},{128,192},{192,0},{1,65},{65,129},{129,193},{193,1... | collective-permute-start | bytes 393224 | tf_op jit(solution)/shard_map/ppermute | solution.py:31
  29.7 0.1 stack.75
  29.8 0.2 select_reduce_fusion.3
  30.0 1.4 %collective-permute-done.2 = bf16[256,256]{1,0:T(8,128)(2,1)S(1)} collective-permute-done((bf16[256,256]{1,0:T(8,128)(2,1)S(1)}, bf16[256,256]{1,0:T(8,128)(2,1)S(1)}, u32[]{:S(2)}, u32[]{:S(2)}) %collective-permute-start.2) | collective-permute-done | bytes 131104 | tf_op jit(solution)/shard_map/ppermute | solution.py:31
  31.4 1.6 %collective-permute-done.1 = bf16[256,256]{1,0:T(8,128)(2,1)S(1)} collective-permute-done((bf16[256,256]{1,0:T(8,128)(2,1)S(1)}, bf16[256,256]{1,0:T(8,128)(2,1)S(1)}, u32[]{:S(2)}, u32[]{:S(2)}) %collective-permute-start.1) | collective-permute-done | bytes 131104 | tf_op jit(solution)/shard_map/ppermute | solution.py:31
  33.1 3.3 %collective-permute-start.7 = (bf16[1024,256]{1,0:T(8,128)(2,1)S(1)}, bf16[1024,256]{1,0:T(8,128)(2,1)S(1)}, u32[]{:S(2)}, u32[]{:S(2)}) collective-permute-start(bf16[1024,256]{1,0:T(8,128)(2,1)S(1)} %pad_maximum_fusion.col_ref), channel_id=1, source_target_pairs={{0,16},{16,0},{1,17},{17,1},{2,18},{18,2},{3,19},{19,3},{4,20},{20... | collective-permute-start | bytes 1572872 | tf_op jit(solution)/shard_map/ppermute | solution.py:31
  36.5 0.2 collective-permute-start.3
  36.7 1.3 %collective-permute-start.4 = (bf16[512,256]{1,0:T(8,128)(2,1)S(1)}, bf16[512,256]{1,0:T(8,128)(2,1)S(1)}, u32[]{:S(2)}, u32[]{:S(2)}) collective-permute-start(bf16[512,256]{1,0:T(8,128)(2,1)S(1)} %bitcast.50), channel_id=1, source_target_pairs={{0,33},{32,0},{1,32},{33,1},{2,35},{34,2},{3,34},{35,3},{4,37},{36... | collective-permute-start | bytes 786440 | tf_op jit(solution)/shard_map/ppermute | solution.py:38
  38.0 0.0 copy-start.3
  38.0 0.7 %copy-done.3 = bf16[1,256]{1,0:T(2,128)(2,1)S(1)} copy-done((bf16[1,256]{1,0:T(2,128)(2,1)S(1)}, bf16[1,256]{1,0:T(2,128)(2,1)}, u32[]{:S(2)}) %copy-start.3) | copy-done | bytes 536
  38.7 0.1 select_reduce_fusion.2.offset_ref
  38.8 0.1 select_reduce_fusion.offset_ref
  38.9 5.6 %collective-permute-done.3.a_ref = bf16[512,256]{1,0:T(8,128)(2,1)S(1)} collective-permute-done((bf16[512,256]{1,0:T(8,128)(2,1)S(1)}, bf16[512,256]{1,0:T(8,128)(2,1)S(1)}, u32[]{:S(2)}, u32[]{:S(2)}) %collective-permute-start.3) | collective-permute-done | bytes 262176 | tf_op jit(solution)/shard_map/ppermute | solution.py:38
  44.5 0.8 %collective-permute-start.5 = (bf16[512,256]{1,0:T(8,128)(2,1)S(1)}, bf16[512,256]{1,0:T(8,128)(2,1)S(1)}, u32[]{:S(2)}, u32[]{:S(2)}) collective-permute-start(bf16[512,256]{1,0:T(8,128)(2,1)S(1)} %collective-permute-done.3.a_ref), channel_id=1, source_target_pairs={{0,16},{16,0},{1,17},{17,1},{2,18},{18,2},{3,19},{19,3},{4,20},{20... | collective-permute-start | bytes 786440 | tf_op jit(solution)/shard_map/ppermute | solution.py:31
  45.3 0.3 collective-permute-done.4.b_ref
  45.5 1.1 %collective-permute-start.6 = (bf16[512,256]{1,0:T(8,128)(2,1)S(1)}, bf16[512,256]{1,0:T(8,128)(2,1)S(1)}, u32[]{:S(2)}, u32[]{:S(2)}) collective-permute-start(bf16[512,256]{1,0:T(8,128)(2,1)S(1)} %collective-permute-done.4.b_ref), channel_id=1, source_target_pairs={{0,16},{16,0},{1,17},{17,1},{2,18},{18,2},{3,19},{19,3},{4,20},{20... | collective-permute-start | bytes 786440 | tf_op jit(solution)/shard_map/ppermute | solution.py:31
  46.7 0.0 copy-start
  46.7 4.2 %shard_map.64 = (f32[1024,128]{1,0:T(8,128)S(1)}, f32[1024,256]{1,0:T(8,128)S(1)}, bf16[1024,256]{1,0:T(8,128)(2,1)S(1)}) custom-call(s32[7]{0:T(128)S(1)} %get-tuple-element.12.live_ref, s32[8]{0:T(128)S(1)} %select_reduce_fusion.2.offset_ref, bf16[256,512]{1,0:T(8,128)(2,1)S(1)} %bitcast.41, bf16[1024,256]{1,0:T(8,128)(2,1)S(1)} %pad_maximum_fusion.col_ref, ...), custom_call_target="tpu_custom_call" | custom-call | flops 2000000000 | bytes 4000000 | tf_op jit(solution)/shard_map/pallas_call | solution.py:164
  50.9 0.1 broadcast_in_dim.87.router_ref
  51.1 5.2 %shard_map.65 = bf16[1024,512]{1,0:T(8,128)(2,1)} custom-call(s32[16]{0:T(128)S(1)} %get-tuple-element.14.live_ref, s32[17]{0:T(128)S(1)} %select_reduce_fusion.offset_ref, bf16[256,512]{1,0:T(8,128)(2,1)S(1)} %bitcast.42, bf16[1024,256]{1,0:T(8,128)(2,1)S(1)} %pad_maximum_fusion.col_ref, bf16[512,256]{1,0:T(8,128)(2,1)S(1)} %collective-permute-done.3.a_ref, ...), custom_call_target="tpu_custom_call" | custom-call | tf_op jit(solution)/shard_map/pallas_call | solution.py:187
  (19 shorter events, 0.2 us)
Async XLA Ops:
  1.5 11.0 %copy-start.1 = (bf16[1,16,8192]{2,1,0:T(8,128)(2,1)S(1)}, bf16[1,16,8192]{2,1,0:T(8,128)(2,1)}, u32[]{:S(2)}) copy-start(bf16[1,16,8192]{2,1,0:T(8,128)(2,1)} %param.7) | copy-start | bytes 786436
  1.5 18.4 %all-to-all-start.1 = ((bf16[16,16,256]{2,0,1:T(8,128)(2,1)}), bf16[16,16,256]{2,0,1:T(8,128)(2,1)S(1)}, u32[]{:S(2)}, u32[]{:S(2)}) async-start(bf16[16,16,256]{2,0,1:T(8,128)(2,1)} %bitcast.11), calls=%async_computation.1 | async-start | bytes 262144 | tf_op jit(solution)/shard_map/all_to_all | solution.py:221
  13.5 0.7 %copy-start.2 = (s32[16,256]{1,0:T(8,128)S(1)}, s32[16,256]{1,0:T(8,128)}, u32[]{:S(2)}) copy-start(s32[16,256]{1,0:T(8,128)} %param.9) | copy-start | bytes 49156
  20.0 26.7 %all-to-all-start = ((bf16[16,16,512]{2,0,1:T(8,128)(2,1)}), bf16[16,16,512]{2,0,1:T(8,128)(2,1)S(1)}, u32[]{:S(2)}, u32[]{:S(2)}) async-start(bf16[16,16,512]{2,0,1:T(8,128)(2,1)} %copy.11), calls=%async_computation | async-start | bytes 524288 | tf_op jit(solution)/shard_map/all_to_all | solution.py:224
  26.0 3.7 %copy-start.4 = (s32[16]{0:T(128)S(1)}, s32[16]{0:T(128)}, u32[]{:S(2)}) copy-start(s32[16]{0:T(128)} %constant.95) | copy-start | bytes 196
  26.0 5.5 %collective-permute-start.2 = (bf16[256,256]{1,0:T(8,128)(2,1)S(1)}, bf16[256,256]{1,0:T(8,128)(2,1)S(1)}, u32[]{:S(2)}, u32[]{:S(2)}) collective-permute-start(bf16[256,256]{1,0:T(8,128)(2,1)S(1)} %bitcast.44), channel_id=1, source_target_pairs={{0,128},{64,192},{128,0},{192,64},{1,129},{65,193},{129,1},{193,65... | collective-permute-start | bytes 393224 | tf_op jit(solution)/shard_map/ppermute | solution.py:31
  27.0 6.1 %collective-permute-start.1 = (bf16[256,256]{1,0:T(8,128)(2,1)S(1)}, bf16[256,256]{1,0:T(8,128)(2,1)S(1)}, u32[]{:S(2)}, u32[]{:S(2)}) collective-permute-start(bf16[256,256]{1,0:T(8,128)(2,1)S(1)} %bitcast.45), channel_id=1, source_target_pairs={{0,192},{64,0},{128,64},{192,128},{1,193},{65,1},{129,65},{193,129... | collective-permute-start | bytes 393224 | tf_op jit(solution)/shard_map/ppermute | solution.py:31
  27.0 6.1 %collective-permute-start = (bf16[256,256]{1,0:T(8,128)(2,1)S(1)}, bf16[256,256]{1,0:T(8,128)(2,1)S(1)}, u32[]{:S(2)}, u32[]{:S(2)}) collective-permute-start(bf16[256,256]{1,0:T(8,128)(2,1)S(1)} %bitcast.46), channel_id=1, source_target_pairs={{0,64},{64,128},{128,192},{192,0},{1,65},{65,129},{129,193},{193,1... | collective-permute-start | bytes 393224 | tf_op jit(solution)/shard_map/ppermute | solution.py:31
  33.1 13.5 %collective-permute-start.7 = (bf16[1024,256]{1,0:T(8,128)(2,1)S(1)}, bf16[1024,256]{1,0:T(8,128)(2,1)S(1)}, u32[]{:S(2)}, u32[]{:S(2)}) collective-permute-start(bf16[1024,256]{1,0:T(8,128)(2,1)S(1)} %pad_maximum_fusion.col_ref), channel_id=1, source_target_pairs={{0,16},{16,0},{1,17},{17,1},{2,18},{18,2},{3,19},{19,3},{4,20},{20... | collective-permute-start | bytes 1572872 | tf_op jit(solution)/shard_map/ppermute | solution.py:31
  36.5 8.0 %collective-permute-start.3 = (bf16[512,256]{1,0:T(8,128)(2,1)S(1)}, bf16[512,256]{1,0:T(8,128)(2,1)S(1)}, u32[]{:S(2)}, u32[]{:S(2)}) collective-permute-start(bf16[512,256]{1,0:T(8,128)(2,1)S(1)} %bitcast.51), channel_id=1, source_target_pairs={{0,32},{32,1},{1,33},{33,0},{2,34},{34,3},{3,35},{35,2},{4,36},{36... | collective-permute-start | bytes 786440 | tf_op jit(solution)/shard_map/ppermute | solution.py:38
  36.7 8.8 %collective-permute-start.4 = (bf16[512,256]{1,0:T(8,128)(2,1)S(1)}, bf16[512,256]{1,0:T(8,128)(2,1)S(1)}, u32[]{:S(2)}, u32[]{:S(2)}) collective-permute-start(bf16[512,256]{1,0:T(8,128)(2,1)S(1)} %bitcast.50), channel_id=1, source_target_pairs={{0,33},{32,0},{1,32},{33,1},{2,35},{34,2},{3,34},{35,3},{4,37},{36... | collective-permute-start | bytes 786440 | tf_op jit(solution)/shard_map/ppermute | solution.py:38
  38.0 0.7 %copy-start.3 = (bf16[1,256]{1,0:T(2,128)(2,1)S(1)}, bf16[1,256]{1,0:T(2,128)(2,1)}, u32[]{:S(2)}) copy-start(bf16[1,256]{1,0:T(2,128)(2,1)} %param.10) | copy-start | bytes 1540
  44.5 6.5 %collective-permute-start.5 = (bf16[512,256]{1,0:T(8,128)(2,1)S(1)}, bf16[512,256]{1,0:T(8,128)(2,1)S(1)}, u32[]{:S(2)}, u32[]{:S(2)}) collective-permute-start(bf16[512,256]{1,0:T(8,128)(2,1)S(1)} %collective-permute-done.3.a_ref), channel_id=1, source_target_pairs={{0,16},{16,0},{1,17},{17,1},{2,18},{18,2},{3,19},{19,3},{4,20},{20... | collective-permute-start | bytes 786440 | tf_op jit(solution)/shard_map/ppermute | solution.py:31
  45.5 5.4 %collective-permute-start.6 = (bf16[512,256]{1,0:T(8,128)(2,1)S(1)}, bf16[512,256]{1,0:T(8,128)(2,1)S(1)}, u32[]{:S(2)}, u32[]{:S(2)}) collective-permute-start(bf16[512,256]{1,0:T(8,128)(2,1)S(1)} %collective-permute-done.4.b_ref), channel_id=1, source_target_pairs={{0,16},{16,0},{1,17},{17,1},{2,18},{18,2},{3,19},{19,3},{4,20},{20... | collective-permute-start | bytes 786440 | tf_op jit(solution)/shard_map/ppermute | solution.py:31
  46.7 4.4 %copy-start = (bf16[1024,512]{1,0:T(8,128)(2,1)S(1)}, bf16[1024,512]{1,0:T(8,128)(2,1)}, u32[]{:S(2)}) copy-start(bf16[1024,512]{1,0:T(8,128)(2,1)} %residual_ref.1) | copy-start | bytes 3145732

commit v2 on v1

v2 whole, which is shorter than its diff:
```python
import math

import jax
import jax.numpy as jnp
from jax import lax
from jax.experimental import pallas as pl
from jax.experimental.pallas import tpu as pltpu
from jax.sharding import Mesh, PartitionSpec as P

H = 64
KVH = 8
HD = 128
TOK_DEV = 1024
CAP = 256
N_CTX = 16
HEADS = 4
ROWS = HEADS * CAP
HALF = 128
GRAN = 16
TILE = 256
PIECES = 8
PIECES_ALL = 4 * PIECES
FIRST = (0, PIECES, 3 * PIECES, 4 * PIECES)
CTX = ("y", "xl", "co")
TP = ("z", "xh")
BF = jnp.bfloat16
F32 = jnp.float32
HIDDEN = -1e30
EXP2_SCALE = math.log2(math.e) / math.sqrt(HD)
CONTRACT_LAST = (((1,), (1,)), ((), ()))
VMEM = pl.BlockSpec(memory_space=pltpu.VMEM)
SMEM = pl.BlockSpec(memory_space=pltpu.SMEM)
ANY = pl.BlockSpec(memory_space=pltpu.HBM)
STATE = [jax.ShapeDtypeStruct((ROWS, HD), F32), jax.ShapeDtypeStruct((ROWS, 2 * HD), F32)]


def buffers(pieces):
    rows = pieces * HALF + TILE
    return [pltpu.VMEM((rows, HD), BF), pltpu.VMEM((rows, 2 * HD), BF)]


def shift(block, axis, distance):
    size = lax.axis_size(axis)
    return lax.ppermute(block, axis, [(i, (i + distance) % size) for i in range(size)])


def shift_x(block, distance):
    def at(x):
        return (x % 2) * 2 + x // 2

    return lax.ppermute(block, ("xl", "xh"), [(at(x), at((x + distance) % 4)) for x in range(4)])


def compact(pieces, group, table_ref, fill_ref, k_buf, v_buf):
    row_in = lax.broadcasted_iota(jnp.int32, (HALF, HD), 0)
    fill = jnp.broadcast_to(fill_ref[0:1, :HD], (HALF, HD))
    for at, (piece, first) in enumerate(pieces):
        start = pl.multiple_of(table_ref[PIECES_ALL + FIRST[group] + at], GRAN)
        inside = row_in < table_ref[FIRST[group] + at]
        rows, now = pl.ds(start, HALF), slice(first, first + HALF)
        k_buf[rows, :] = jnp.where(inside, piece[now, :HD], fill)
        v_buf[rows, :HD] = jnp.where(inside, piece[now, HD:], jnp.zeros((HALF, HD), BF))
        v_buf[rows, HD:] = jnp.where(inside, 1.0, 0.0).astype(BF)
    end = pl.multiple_of(table_ref[2 * PIECES_ALL + group], GRAN)
    k_buf[pl.ds(end, TILE), :] = jnp.broadcast_to(fill_ref[0:1, :HD], (TILE, HD))
    v_buf[pl.ds(end, TILE), :] = jnp.zeros((TILE, 2 * HD), BF)
    return (end + TILE - 1) // TILE


def twice(column):
    return jnp.concatenate([column, column], axis=1)


def soften(scores, before):
    top = before
    for lane in range(0, scores.shape[1], HD):
        now = scores[:, lane : lane + HD]
        top = now if top is None else jnp.maximum(top, now)
    top = jnp.broadcast_to(jnp.max(top, axis=1, keepdims=True), (CAP, HD))
    shifted = top * EXP2_SCALE
    shifted = jnp.concatenate([shifted] * (scores.shape[1] // HD), axis=1)
    return top, jnp.exp2(scores * EXP2_SCALE - shifted).astype(BF)


def absorb(tiles, q_ref, k_buf, v_buf, old, new):
    (top_old, sum_old), (top_new, sum_new) = old, new
    for count in range((k_buf.shape[0] - TILE) // TILE + 1):

        @pl.when(tiles == count)
        def _():
            if count == 0:
                top_new[...] = top_old[...]
                sum_new[...] = sum_old[...]
                return
            keys = count * TILE
            for head in range(HEADS):
                now = slice(head * CAP, (head + 1) * CAP)
                query = q_ref[:, head * HD : (head + 1) * HD]
                scores = lax.dot_general(
                    query, k_buf[:keys, :], CONTRACT_LAST, preferred_element_type=F32
                )
                before = top_old[now, :]
                top, weights = soften(scores, before)
                factor = jnp.exp2((before - top) * EXP2_SCALE)
                added = jnp.dot(weights, v_buf[:keys, :], preferred_element_type=F32)
                sum_new[now, :] = sum_old[now, :] * twice(factor) + added
                top_new[now, :] = top


def pieces_of(*refs):
    return [(ref, HALF * i) for ref in refs for i in range(PIECES // 2)]


def own_kernel(table_ref, q_ref, lower_ref, upper_ref, top_ref, sum_ref, k_buf, v_buf):
    rows = lax.broadcasted_iota(jnp.int32, (CAP, CAP), 0)
    cols = lax.broadcasted_iota(jnp.int32, (CAP, CAP), 1)
    tiles = compact(pieces_of(lower_ref, upper_ref), 0, table_ref, lower_ref, k_buf, v_buf)
    keys = lower_ref[:CAP, :HD]
    values = jnp.concatenate([lower_ref[:CAP, HD:], jnp.ones((CAP, HD), BF)], axis=1)
    for head in range(HEADS):
        now = slice(head * CAP, (head + 1) * CAP)
        query = q_ref[:, head * HD : (head + 1) * HD]
        scores = lax.dot_general(query, keys, CONTRACT_LAST, preferred_element_type=F32)
        top, weights = soften(jnp.where(cols <= rows, scores, HIDDEN), None)
        top_ref[now, :] = top
        sum_ref[now, :] = jnp.dot(weights, values, preferred_element_type=F32)
    state = (top_ref, sum_ref)
    absorb(tiles, q_ref, k_buf, v_buf, state, state)


def more_kernel(table_ref, q_ref, fill_ref, *rest):
    blocks, state, (top_ref, sum_ref, k_buf, v_buf) = rest[:-6], rest[-6:-4], rest[-4:]
    tiles = compact(pieces_of(*blocks), 1, table_ref, fill_ref, k_buf, v_buf)
    absorb(tiles, q_ref, k_buf, v_buf, state, (top_ref, sum_ref))


def last_kernel(table_ref, q_ref, fill_ref, lower_ref, upper_ref, top0, sum0, kept_ref, router_ref, residual_ref, out_ref, k_buf, v_buf, top_ref, sum_ref, residual_buf, out_buf, sems):
    fetch = pltpu.make_async_copy(residual_ref, residual_buf, sems.at[4])
    fetch.start()
    pieces = pieces_of(lower_ref, upper_ref)
    tiles = compact(pieces, 2, table_ref, fill_ref, k_buf, v_buf)
    absorb(tiles, q_ref, k_buf, v_buf, (top0, sum0), (top_ref, sum_ref))
    updates = []
    for head in range(HEADS):
        now = slice(head * CAP, (head + 1) * CAP)
        attention = sum_ref[now, :HD] / sum_ref[now, HD:]
        updates.append((router_ref[...] * attention).astype(BF))
    update = jnp.concatenate(updates, axis=1)
    kept = kept_ref[pl.ds(table_ref[2 * PIECES_ALL + 3], 1), :]
    fetch.wait()
    copies = []
    for part, row in enumerate(range(0, TOK_DEV, CAP)):
        now = slice(row, row + CAP)
        place = lax.broadcasted_iota(jnp.int32, (CAP, CAP), 0) + row
        chosen = jnp.where(place == kept, 1.0, 0.0).astype(BF)
        added = jnp.dot(chosen, update, preferred_element_type=F32)
        out_buf[now, :] = (residual_buf[now, :].astype(F32) + added).astype(BF)
        copy = pltpu.make_async_copy(out_buf.at[now], out_ref.at[now], sems.at[part])
        copy.start()
        copies.append(copy)
    for copy in copies:
        copy.wait()


def params(mebibytes):
    return pltpu.CompilerParams(vmem_limit_bytes=mebibytes * 1024 * 1024)


SMALL = pl.CostEstimate(flops=1_000_000, bytes_accessed=10_000, transcendentals=1_000)


def sorted_kernel(queries_ref, pairs_ref, out_ref, buf, in_sems, out_sems):
    width = HEADS * HD
    arrive, leave = [], []
    for to in range(2 * KVH):
        here = queries_ref.at[0, :, pl.ds(to * width, width)]
        arrive.append(pltpu.make_async_copy(here, buf.at[to, :, pl.ds(0, width)], in_sems.at[2 * to]))
        here = pairs_ref.at[0, :, pl.ds(to // 2 * 2 * HD, 2 * HD)]
        arrive.append(pltpu.make_async_copy(here, buf.at[to, :, pl.ds(width, 2 * HD)], in_sems.at[2 * to + 1]))
        leave.append(pltpu.make_async_copy(buf.at[to], out_ref.at[to], out_sems.at[to]))
    for copy in arrive:
        copy.start()
    for to in range(2 * KVH):
        arrive[2 * to].wait()
        arrive[2 * to + 1].wait()
        leave[to].start()
    for copy in leave:
        copy.wait()


def sorted_part(queries, pairs):
    shape = (2 * KVH, queries.shape[1], (HEADS + 2) * HD)
    return pl.pallas_call(
        sorted_kernel,
        out_shape=jax.ShapeDtypeStruct(shape, BF),
        in_specs=[ANY, ANY],
        out_specs=ANY,
        scratch_shapes=[
            pltpu.VMEM(shape, BF),
            pltpu.SemaphoreType.DMA((4 * KVH,)),
            pltpu.SemaphoreType.DMA((2 * KVH,)),
        ],
        compiler_params=params(60),
    )(queries, pairs)


def own_part(table, query_rows, lower, upper):
    return pl.pallas_call(
        own_kernel,
        out_shape=STATE,
        in_specs=[SMEM] + [VMEM] * 3,
        out_specs=[VMEM] * 2,
        scratch_shapes=buffers(PIECES),
        cost_estimate=SMALL,
        compiler_params=params(16),
    )(table, query_rows, lower, upper)


def more_part(table, query_rows, fill, blocks, state):
    return pl.pallas_call(
        more_kernel,
        out_shape=STATE,
        in_specs=[SMEM] + [VMEM] * (4 + len(blocks)),
        out_specs=[VMEM] * 2,
        scratch_shapes=buffers(2 * PIECES),
        cost_estimate=SMALL,
        compiler_params=params(16),
    )(table, query_rows, fill, *blocks, *state)


def last_part(table, query_rows, fill, blocks, state, kept_local, router, residual):
    return pl.pallas_call(
        last_kernel,
        out_shape=jax.ShapeDtypeStruct((TOK_DEV, HEADS * HD), BF),
        in_specs=[SMEM] + [VMEM] * 8 + [ANY],
        out_specs=ANY,
        scratch_shapes=buffers(PIECES)
        + [pltpu.VMEM(s.shape, s.dtype) for s in STATE]
        + [pltpu.VMEM((TOK_DEV, HEADS * HD), BF)] * 2
        + [pltpu.SemaphoreType.DMA((5,))],
        compiler_params=params(16),
    )(table, query_rows, fill, *blocks, *state, kept_local, router, residual)


def tables(kept_local, y, xl, co):
    own = (y * 2 + xl) * 2 + co
    counts = jnp.sum((kept_local < TOK_DEV).astype(jnp.int32), axis=1)
    at = jnp.arange(4 * PIECES, dtype=jnp.int32)
    group, piece = at // PIECES, at % PIECES
    behind, half = piece // 2, piece % 2
    behind = behind ^ (behind // 2)
    block = (((y - behind + 4) % 4) * 2 + (xl ^ (group // 2))) * 2 + (co ^ (group % 2))
    block_count = jnp.sum(jnp.where(block[:, None] == jnp.arange(N_CTX), counts[None, :], 0), axis=1)
    live = jnp.where(block < own, jnp.clip(block_count - half * HALF, 0, HALF), 0)
    taken = (live + GRAN - 1) // GRAN * GRAN
    part = (group + 1) // 2
    to = jnp.arange(PIECES_ALL + 3, dtype=jnp.int32)[:, None]
    to_part = jnp.where(to < PIECES_ALL, (to // PIECES + 1) // 2, to - PIECES_ALL)
    counted = (to_part == part[None, :]) & (at[None, :] < to)
    offset = jnp.sum(jnp.where(counted, taken[None, :], 0), axis=1)
    return jnp.concatenate([live, offset, jnp.broadcast_to(own, (1,))]).astype(jnp.int32)


def shards(residual, queries, keys_values, kept_local, router_weight):
    y, xl, co = (lax.axis_index(a) for a in CTX)
    sent = sorted_part(queries, keys_values)
    sent = lax.all_to_all(sent, TP, split_axis=0, concat_axis=0, tiled=True)
    sent = sent.reshape(CAP, (HEADS + 2) * HD)
    query_rows, pairs = sent[:, : HEADS * HD], sent[:, HEADS * HD :]
    table = tables(kept_local, y, xl, co)
    router = jnp.broadcast_to(router_weight[0].astype(F32)[:, None], (CAP, HD))
    pairs, table, router = lax.optimization_barrier((pairs, table, router))

    behind_1, behind_3, behind_2 = (shift(pairs, "y", d) for d in (1, 3, 2))
    lower = jnp.concatenate([pairs, behind_1], axis=0)
    upper = jnp.concatenate([behind_3, behind_2], axis=0)
    lower_x, upper_x = shift_x(lower, 1), shift_x(upper, 3)
    state = own_part(table, query_rows, lower, upper)
    low, up, *state = lax.optimization_barrier((lower, upper, *state))
    others = [shift(low, "co", 1), shift(up, "co", 1)]
    lower_x, upper_x, *state = lax.optimization_barrier((lower_x, upper_x, *state))
    swapped = [shift(lower_x, "co", 1), shift(upper_x, "co", 1)]
    state = more_part(table, query_rows, pairs, [*others, lower_x, upper_x], state)
    return last_part(table, query_rows, pairs, swapped, state, kept_local, router, residual)


def solution(mesh):
    grid = Mesh(mesh.devices.reshape(4, 2, 2, 8, 2), CTX + TP)
    placed = (P(CTX, TP), P(CTX, TP, None), P(CTX, TP, None), P(), P(CTX, None))
    return jax.shard_map(shards, mesh=grid, in_specs=placed, out_specs=P(CTX, TP), check_vma=False)
```

time: 57 us -> 54.1 us (0.949)
  the two profiles are of different devices: /device:TPU:31 before, /device:TPU:1 now
where the time goes in v2:
time: 54.1 us; the launch traced here: 53.8 us
  starting transfers between devices  25 us (46%)
  waiting for transfers between devices  19.6 us (36%)
  Pallas kernels  7.54 us (14%)
  local copies, waits for them, and re-layouts  0.83 us (2%)
    all_to_all x1, waiting for transfers between devices, shards(): sent = lax.all_to_all(sent, TP, split_axis=0, concat_axis=0, tiled=True)  13.6 us
    ppermute x7, starting transfers between devices, shift(): lax.ppermute(block, axis, [(i, (i + distance) % size) for i in range(size)])  12.9 us
    all_to_all x1, starting transfers between devices, shards(): sent = lax.all_to_all(sent, TP, split_axis=0, concat_axis=0, tiled=True)  11.6 us
    ppermute x7, waiting for transfers between devices, shift(): lax.ppermute(block, axis, [(i, (i + distance) % size) for i in range(size)])  5.49 us
    pallas_call x1, Pallas kernels, last_part(): pl.pallas_call(last_kernel, out_shape=jax.ShapeDtypeStruct((TOK_DEV, HEAD...  2.3 us
    pallas_call x1, Pallas kernels, sorted_part(): pl.pallas_call(sorted_kernel, out_shape=jax.ShapeDtypeStruct(shape, BF),...  2.01 us
    pallas_call x1, Pallas kernels, more_part(): pl.pallas_call(more_kernel, out_shape=STATE, in_specs=[SMEM] + [VMEM] * (...  1.92 us
    pallas_call x1, Pallas kernels, own_part(): pl.pallas_call(own_kernel, out_shape=STATE, in_specs=[SMEM] + [VMEM] * 3,...  1.31 us
  transfers between devices with their start and end apart: 10, of which 5 were waited for; matrix products, arithmetic and copies ran while one was open for 1% of the time, Pallas kernels for 6%

profile of v2, /device:TPU:1, one launch (start us, length us, event | category | flops | bytes accessed | tf_op | source)
XLA Modules:
  0.0 53.8 jit_solution(7954776198540949009)
XLA Ops:
  0.0 2.0 %shard_map.55 = bf16[16,16,768]{2,1,0:T(8,128)(2,1)} custom-call(bf16[1,16,8192]{2,1,0:T(8,128)(2,1)} %queries_ref.1, bf16[1,16,2048]{2,1,0:T(8,128)(2,1)} %pairs_ref.1), custom_call_target="tpu_custom_call" | custom-call | tf_op jit(solution)/shard_map/pallas_call | solution.py:193
  2.0 11.6 %all-to-all-start = ((bf16[16,16,768]{2,1,0:T(8,128)(2,1)}), bf16[16,16,768]{2,1,0:T(8,128)(2,1)S(1)}, u32[]{:S(2)}, u32[]{:S(2)}) async-start(bf16[16,16,768]{2,1,0:T(8,128)(2,1)} %shard_map.55), calls=%async_computation | async-start | bytes 786432 | tf_op jit(solution)/shard_map/all_to_all | solution.py:267
  13.6 0.0 copy-start.1
  13.7 0.0 copy-start.2
  13.7 0.7 %copy-done.2 = bf16[1,256]{1,0:T(2,128)(2,1)S(1)} copy-done((bf16[1,256]{1,0:T(2,128)(2,1)S(1)}, bf16[1,256]{1,0:T(2,128)(2,1)}, u32[]{:S(2)}) %copy-start.2) | copy-done | bytes 536
  14.4 0.1 convert_reduce_fusion
  14.5 0.1 select_reduce_fusion.1
  14.6 0.1 select_reduce_fusion
  14.7 0.1 pad_add_fusion.table_ref
  14.8 13.6 %all-to-all-done = bf16[16,16,768]{2,1,0:T(8,128)(2,1)S(1)} async-done(((bf16[16,16,768]{2,1,0:T(8,128)(2,1)}), bf16[16,16,768]{2,1,0:T(8,128)(2,1)S(1)}, u32[]{:S(2)}, u32[]{:S(2)}) %all-to-all-start) | async-done | bytes 393248 | tf_op jit(solution)/shard_map/all_to_all | solution.py:267
  28.4 0.1 broadcast_in_dim.47.router_ref
  28.5 2.8 %collective-permute-start.2 = (bf16[256,256]{1,0:T(8,128)(2,1)S(1)}, bf16[256,256]{1,0:T(8,128)(2,1)S(1)}, u32[]{:S(2)}, u32[]{:S(2)}) collective-permute-start(bf16[256,256]{1,0:T(8,128)(2,1)S(1)} %slice.8.fill_ref), channel_id=1, source_target_pairs={{0,192},{64,0},{128,64},{192,128},{1,193},{65,1},{129,65},{193,129... | collective-permute-start | bytes 393224 | tf_op jit(solution)/shard_map/ppermute | solution.py:44
  31.3 0.3 collective-permute-start.3
  31.7 0.8 %collective-permute-start = (bf16[256,256]{1,0:T(8,128)(2,1)S(1)}, bf16[256,256]{1,0:T(8,128)(2,1)S(1)}, u32[]{:S(2)}, u32[]{:S(2)}) collective-permute-start(bf16[256,256]{1,0:T(8,128)(2,1)S(1)} %slice.8.fill_ref), channel_id=1, source_target_pairs={{0,64},{64,128},{128,192},{192,0},{1,65},{65,129},{129,193},{193,1... | collective-permute-start | bytes 393224 | tf_op jit(solution)/shard_map/ppermute | solution.py:44
  32.5 1.6 %collective-permute-done.2 = bf16[256,256]{1,0:T(8,128)(2,1)S(1)} collective-permute-done((bf16[256,256]{1,0:T(8,128)(2,1)S(1)}, bf16[256,256]{1,0:T(8,128)(2,1)S(1)}, u32[]{:S(2)}, u32[]{:S(2)}) %collective-permute-start.2) | collective-permute-done | bytes 131104 | tf_op jit(solution)/shard_map/ppermute | solution.py:44
  34.0 2.7 %collective-permute-done.3 = bf16[256,256]{1,0:T(8,128)(2,1)S(1)} collective-permute-done((bf16[256,256]{1,0:T(8,128)(2,1)S(1)}, bf16[256,256]{1,0:T(8,128)(2,1)S(1)}, u32[]{:S(2)}, u32[]{:S(2)}) %collective-permute-start.3) | collective-permute-done | bytes 131104 | tf_op jit(solution)/shard_map/ppermute | solution.py:44
  36.8 0.1 collective-permute-start.4
  36.9 1.2 %collective-permute-done = bf16[256,256]{1,0:T(8,128)(2,1)S(1)} collective-permute-done((bf16[256,256]{1,0:T(8,128)(2,1)S(1)}, bf16[256,256]{1,0:T(8,128)(2,1)S(1)}, u32[]{:S(2)}, u32[]{:S(2)}) %collective-permute-start) | collective-permute-done | bytes 131104 | tf_op jit(solution)/shard_map/ppermute | solution.py:44
  38.1 0.4 collective-permute-start.1
  38.5 1.3 %shard_map.56 = (f32[1024,128]{1,0:T(8,128)S(1)}, f32[1024,256]{1,0:T(8,128)S(1)}) custom-call(s32[68]{0:T(128)S(1)} %pad_add_fusion.table_ref, bf16[256,512]{1,0:T(8,128)(2,1)S(1)} %slice.9.q_ref, bf16[512,256]{1,0:T(8,128)(2,1)S(1)} %constant_dynamic-update-slice_fusion.lower_ref, bf16[512,256]{1,0:T(8,128)(2,1)S(1)} %constant_dynamic-update-slice_fusion.2.upper_ref), custom_call_target="tpu_custom_call" | custom-call | flops 1000000 | bytes 10000 | tf_op jit(solution)/shard_map/pallas_call | solution.py:208
  39.8 0.0 copy-start
  39.8 4.2 %collective-permute-start.7 = (bf16[512,256]{1,0:T(8,128)(2,1)S(1)}, bf16[512,256]{1,0:T(8,128)(2,1)S(1)}, u32[]{:S(2)}, u32[]{:S(2)}) collective-permute-start(bf16[512,256]{1,0:T(8,128)(2,1)S(1)} %constant_dynamic-update-slice_fusion.lower_ref), channel_id=1, source_target_pairs={{0,16},{16,0},{1,17},{17,1},{2,18},{18,2},{3,19},{19,3},{4,20},{20... | collective-permute-start | bytes 786440 | tf_op jit(solution)/shard_map/ppermute | solution.py:44
  44.0 0.1 collective-permute-start.8
  44.1 0.0 collective-permute-done.4.rest_3_
  44.1 0.5 collective-permute-done.1.rest_2_
  44.6 4.7 %collective-permute-start.5 = (bf16[512,256]{1,0:T(8,128)(2,1)S(1)}, bf16[512,256]{1,0:T(8,128)(2,1)S(1)}, u32[]{:S(2)}, u32[]{:S(2)}) collective-permute-start(bf16[512,256]{1,0:T(8,128)(2,1)S(1)} %collective-permute-done.1.rest_2_), channel_id=1, source_target_pairs={{0,16},{16,0},{1,17},{17,1},{2,18},{18,2},{3,19},{19,3},{4,20},{20... | collective-permute-start | bytes 786440 | tf_op jit(solution)/shard_map/ppermute | solution.py:44
  49.3 0.0 collective-permute-start.6
  49.3 0.0 collective-permute-done.7.rest_0_
  49.3 0.0 collective-permute-done.8.rest_1_
  49.3 1.9 %shard_map.57 = (f32[1024,128]{1,0:T(8,128)S(1)}, f32[1024,256]{1,0:T(8,128)S(1)}) custom-call(s32[68]{0:T(128)S(1)} %pad_add_fusion.table_ref, bf16[256,512]{1,0:T(8,128)(2,1)S(1)} %slice.9.q_ref, bf16[256,256]{1,0:T(8,128)(2,1)S(1)} %slice.8.fill_ref, bf16[512,256]{1,0:T(8,128)(2,1)S(1)} %collective-permute-done.7.rest_0_, ...), custom_call_target="tpu_custom_call" | custom-call | flops 1000000 | bytes 10000 | tf_op jit(solution)/shard_map/pallas_call | solution.py:220
  51.2 0.0 collective-permute-done.5.lower_ref
  51.3 2.3 %shard_map.58 = bf16[1024,512]{1,0:T(8,128)(2,1)} custom-call(s32[68]{0:T(128)S(1)} %pad_add_fusion.table_ref, bf16[256,512]{1,0:T(8,128)(2,1)S(1)} %slice.9.q_ref, bf16[256,256]{1,0:T(8,128)(2,1)S(1)} %slice.8.fill_ref, bf16[512,256]{1,0:T(8,128)(2,1)S(1)} %collective-permute-done.5.lower_ref, bf16[512,256]{1,0:T(8,128)(2,1)S(1)} %collective-permute-done.6.upper_ref, ...), custom_call_target="tpu_custom_call" | custom-call | tf_op jit(solution)/shard_map/pallas_call | solution.py:232
  (13 shorter events, 0.2 us)
Async XLA Ops:
  2.0 26.4 %all-to-all-start = ((bf16[16,16,768]{2,1,0:T(8,128)(2,1)}), bf16[16,16,768]{2,1,0:T(8,128)(2,1)S(1)}, u32[]{:S(2)}, u32[]{:S(2)}) async-start(bf16[16,16,768]{2,1,0:T(8,128)(2,1)} %shard_map.55), calls=%async_computation | async-start | bytes 786432 | tf_op jit(solution)/shard_map/all_to_all | solution.py:267
  13.6 0.7 %copy-start.1 = (s32[16,256]{1,0:T(8,128)S(1)}, s32[16,256]{1,0:T(8,128)}, u32[]{:S(2)}) copy-start(s32[16,256]{1,0:T(8,128)} %kept_ref.1) | copy-start | bytes 49156
  13.7 0.7 %copy-start.2 = (bf16[1,256]{1,0:T(2,128)(2,1)S(1)}, bf16[1,256]{1,0:T(2,128)(2,1)}, u32[]{:S(2)}) copy-start(bf16[1,256]{1,0:T(2,128)(2,1)} %param.9) | copy-start | bytes 1540
  28.5 5.5 %collective-permute-start.2 = (bf16[256,256]{1,0:T(8,128)(2,1)S(1)}, bf16[256,256]{1,0:T(8,128)(2,1)S(1)}, u32[]{:S(2)}, u32[]{:S(2)}) collective-permute-start(bf16[256,256]{1,0:T(8,128)(2,1)S(1)} %slice.8.fill_ref), channel_id=1, source_target_pairs={{0,192},{64,0},{128,64},{192,128},{1,193},{65,1},{129,65},{193,129... | collective-permute-start | bytes 393224 | tf_op jit(solution)/shard_map/ppermute | solution.py:44
  31.3 5.4 %collective-permute-start.3 = (bf16[256,256]{1,0:T(8,128)(2,1)S(1)}, bf16[256,256]{1,0:T(8,128)(2,1)S(1)}, u32[]{:S(2)}, u32[]{:S(2)}) collective-permute-start(bf16[256,256]{1,0:T(8,128)(2,1)S(1)} %slice.8.fill_ref), channel_id=1, source_target_pairs={{0,128},{64,192},{128,0},{192,64},{1,129},{65,193},{129,1},{193,65... | collective-permute-start | bytes 393224 | tf_op jit(solution)/shard_map/ppermute | solution.py:44
  31.7 6.4 %collective-permute-start = (bf16[256,256]{1,0:T(8,128)(2,1)S(1)}, bf16[256,256]{1,0:T(8,128)(2,1)S(1)}, u32[]{:S(2)}, u32[]{:S(2)}) collective-permute-start(bf16[256,256]{1,0:T(8,128)(2,1)S(1)} %slice.8.fill_ref), channel_id=1, source_target_pairs={{0,64},{64,128},{128,192},{192,0},{1,65},{65,129},{129,193},{193,1... | collective-permute-start | bytes 393224 | tf_op jit(solution)/shard_map/ppermute | solution.py:44
  36.8 7.3 %collective-permute-start.4 = (bf16[512,256]{1,0:T(8,128)(2,1)S(1)}, bf16[512,256]{1,0:T(8,128)(2,1)S(1)}, u32[]{:S(2)}, u32[]{:S(2)}) collective-permute-start(bf16[512,256]{1,0:T(8,128)(2,1)S(1)} %constant_dynamic-update-slice_fusion.2.upper_ref), channel_id=1, source_target_pairs={{0,33},{32,0},{1,32},{33,1},{2,35},{34,2},{3,34},{35,3},{4,37},{36... | collective-permute-start | bytes 786440 | tf_op jit(solution)/shard_map/ppermute | solution.py:51
  38.1 6.5 %collective-permute-start.1 = (bf16[512,256]{1,0:T(8,128)(2,1)S(1)}, bf16[512,256]{1,0:T(8,128)(2,1)S(1)}, u32[]{:S(2)}, u32[]{:S(2)}) collective-permute-start(bf16[512,256]{1,0:T(8,128)(2,1)S(1)} %constant_dynamic-update-slice_fusion.lower_ref), channel_id=1, source_target_pairs={{0,32},{32,1},{1,33},{33,0},{2,34},{34,3},{3,35},{35,2},{4,36},{36... | collective-permute-start | bytes 786440 | tf_op jit(solution)/shard_map/ppermute | solution.py:51
  39.8 11.5 %copy-start = (bf16[1024,512]{1,0:T(8,128)(2,1)S(1)}, bf16[1024,512]{1,0:T(8,128)(2,1)}, u32[]{:S(2)}) copy-start(bf16[1024,512]{1,0:T(8,128)(2,1)} %residual_ref.1) | copy-start | bytes 3145732
  39.8 9.5 %collective-permute-start.7 = (bf16[512,256]{1,0:T(8,128)(2,1)S(1)}, bf16[512,256]{1,0:T(8,128)(2,1)S(1)}, u32[]{:S(2)}, u32[]{:S(2)}) collective-permute-start(bf16[512,256]{1,0:T(8,128)(2,1)S(1)} %constant_dynamic-update-slice_fusion.lower_ref), channel_id=1, source_target_pairs={{0,16},{16,0},{1,17},{17,1},{2,18},{18,2},{3,19},{19,3},{4,20},{20... | collective-permute-start | bytes 786440 | tf_op jit(solution)/shard_map/ppermute | solution.py:44
  44.0 5.3 %collective-permute-start.8 = (bf16[512,256]{1,0:T(8,128)(2,1)S(1)}, bf16[512,256]{1,0:T(8,128)(2,1)S(1)}, u32[]{:S(2)}, u32[]{:S(2)}) collective-permute-start(bf16[512,256]{1,0:T(8,128)(2,1)S(1)} %constant_dynamic-update-slice_fusion.2.upper_ref), channel_id=1, source_target_pairs={{0,16},{16,0},{1,17},{17,1},{2,18},{18,2},{3,19},{19,3},{4,20},{20... | collective-permute-start | bytes 786440 | tf_op jit(solution)/shard_map/ppermute | solution.py:44
  44.6 6.7 %collective-permute-start.5 = (bf16[512,256]{1,0:T(8,128)(2,1)S(1)}, bf16[512,256]{1,0:T(8,128)(2,1)S(1)}, u32[]{:S(2)}, u32[]{:S(2)}) collective-permute-start(bf16[512,256]{1,0:T(8,128)(2,1)S(1)} %collective-permute-done.1.rest_2_), channel_id=1, source_target_pairs={{0,16},{16,0},{1,17},{17,1},{2,18},{18,2},{3,19},{19,3},{4,20},{20... | collective-permute-start | bytes 786440 | tf_op jit(solution)/shard_map/ppermute | solution.py:44
  49.3 2.0 %collective-permute-start.6 = (bf16[512,256]{1,0:T(8,128)(2,1)S(1)}, bf16[512,256]{1,0:T(8,128)(2,1)S(1)}, u32[]{:S(2)}, u32[]{:S(2)}) collective-permute-start(bf16[512,256]{1,0:T(8,128)(2,1)S(1)} %collective-permute-done.4.rest_3_), channel_id=1, source_target_pairs={{0,16},{16,0},{1,17},{17,1},{2,18},{18,2},{3,19},{19,3},{4,20},{20... | collective-permute-start | bytes 786440 | tf_op jit(solution)/shard_map/ppermute | solution.py:44

commit v3 on v2

--- a/solution.py
+++ b/solution.py
@@ -108,7 +108,7 @@
 
 
 def pieces_of(*refs):
-    return [(ref, HALF * i) for ref in refs for i in range(PIECES // 2)]
+    return [(ref, row) for ref in refs for row in range(0, ref.shape[0], HALF)]
 
 
 def own_kernel(table_ref, q_ref, lower_ref, upper_ref, top_ref, sum_ref, k_buf, v_buf):
@@ -134,10 +134,10 @@
     absorb(tiles, q_ref, k_buf, v_buf, state, (top_ref, sum_ref))
 
 
-def last_kernel(table_ref, q_ref, fill_ref, lower_ref, upper_ref, top0, sum0, kept_ref, router_ref, residual_ref, out_ref, k_buf, v_buf, top_ref, sum_ref, residual_buf, out_buf, sems):
+def last_kernel(table_ref, q_ref, fill_ref, own_ref, lower_ref, upper_ref, top0, sum0, kept_ref, router_ref, residual_ref, out_ref, k_buf, v_buf, top_ref, sum_ref, residual_buf, out_buf, sems):
     fetch = pltpu.make_async_copy(residual_ref, residual_buf, sems.at[4])
     fetch.start()
-    pieces = pieces_of(lower_ref, upper_ref)
+    pieces = pieces_of(own_ref, lower_ref, upper_ref)
     tiles = compact(pieces, 2, table_ref, fill_ref, k_buf, v_buf)
     absorb(tiles, q_ref, k_buf, v_buf, (top0, sum0), (top_ref, sum_ref))
     updates = []
@@ -169,21 +169,25 @@
 SMALL = pl.CostEstimate(flops=1_000_000, bytes_accessed=10_000, transcendentals=1_000)
 
 
-def sorted_kernel(queries_ref, pairs_ref, out_ref, buf, in_sems, out_sems):
-    width = HEADS * HD
-    arrive, leave = [], []
-    for to in range(2 * KVH):
-        here = queries_ref.at[0, :, pl.ds(to * width, width)]
-        arrive.append(pltpu.make_async_copy(here, buf.at[to, :, pl.ds(0, width)], in_sems.at[2 * to]))
-        here = pairs_ref.at[0, :, pl.ds(to // 2 * 2 * HD, 2 * HD)]
-        arrive.append(pltpu.make_async_copy(here, buf.at[to, :, pl.ds(width, 2 * HD)], in_sems.at[2 * to + 1]))
-        leave.append(pltpu.make_async_copy(buf.at[to], out_ref.at[to], out_sems.at[to]))
+def sorted_kernel(queries_ref, pairs_ref, out_ref, q_buf, kv_buf, out_buf, in_sems, out_sems):
+    width, quarter = HEADS * HD, KVH // 2
+    arrive = [pltpu.make_async_copy(pairs_ref.at[0], kv_buf, in_sems.at[4])]
+    for part in range(4):
+        now = pl.ds(part * quarter * width, quarter * width)
+        arrive.append(pltpu.make_async_copy(queries_ref.at[0, :, now], q_buf.at[:, now], in_sems.at[part]))
     for copy in arrive:
         copy.start()
-    for to in range(2 * KVH):
-        arrive[2 * to].wait()
-        arrive[2 * to + 1].wait()
-        leave[to].start()
+    arrive[0].wait()
+    leave = []
+    for part in range(4):
+        arrive[part + 1].wait()
+        for to in range(part * quarter, (part + 1) * quarter):
+            group = to // 2
+            out_buf[to, :, :width] = q_buf[:, to * width : (to + 1) * width]
+            out_buf[to, :, width:] = kv_buf[:, group * 2 * HD : (group + 1) * 2 * HD]
+        now = pl.ds(part * quarter, quarter)
+        leave.append(pltpu.make_async_copy(out_buf.at[now], out_ref.at[now], out_sems.at[part]))
+        leave[-1].start()
     for copy in leave:
         copy.wait()
 
@@ -196,9 +200,11 @@
         in_specs=[ANY, ANY],
         out_specs=ANY,
         scratch_shapes=[
+            pltpu.VMEM(queries.shape[1:], BF),
+            pltpu.VMEM(pairs.shape[1:], BF),
             pltpu.VMEM(shape, BF),
-            pltpu.SemaphoreType.DMA((4 * KVH,)),
-            pltpu.SemaphoreType.DMA((2 * KVH,)),
+            pltpu.SemaphoreType.DMA((5,)),
+            pltpu.SemaphoreType.DMA((4,)),
         ],
         compiler_params=params(60),
     )(queries, pairs)
@@ -232,7 +238,7 @@
     return pl.pallas_call(
         last_kernel,
         out_shape=jax.ShapeDtypeStruct((TOK_DEV, HEADS * HD), BF),
-        in_specs=[SMEM] + [VMEM] * 8 + [ANY],
+        in_specs=[SMEM] + [VMEM] * 9 + [ANY],
         out_specs=ANY,
         scratch_shapes=buffers(PIECES)
         + [pltpu.VMEM(s.shape, s.dtype) for s in STATE]
@@ -247,8 +253,10 @@
     counts = jnp.sum((kept_local < TOK_DEV).astype(jnp.int32), axis=1)
     at = jnp.arange(4 * PIECES, dtype=jnp.int32)
     group, piece = at // PIECES, at % PIECES
-    behind, half = piece // 2, piece % 2
-    behind = behind ^ (behind // 2)
+    straight = (piece // 2) ^ (piece // 4)
+    split = jnp.where(piece < 4, piece // 2, jnp.where((piece == 4) | (piece == 7), 2, 3))
+    behind = jnp.where(group < 2, straight, split)
+    half = jnp.where((group < 2) | (piece < 4), piece % 2, jnp.where(piece == 5, 0, piece // 6))
     block = (((y - behind + 4) % 4) * 2 + (xl ^ (group // 2))) * 2 + (co ^ (group % 2))
     block_count = jnp.sum(jnp.where(block[:, None] == jnp.arange(N_CTX), counts[None, :], 0), axis=1)
     live = jnp.where(block < own, jnp.clip(block_count - half * HALF, 0, HALF), 0)
@@ -272,15 +280,18 @@
     pairs, table, router = lax.optimization_barrier((pairs, table, router))
 
     behind_1, behind_3, behind_2 = (shift(pairs, "y", d) for d in (1, 3, 2))
+    own_x = shift_x(pairs, 1)
     lower = jnp.concatenate([pairs, behind_1], axis=0)
     upper = jnp.concatenate([behind_3, behind_2], axis=0)
-    lower_x, upper_x = shift_x(lower, 1), shift_x(upper, 3)
+    lower_x = shift_x(jnp.concatenate([behind_1, behind_2[:HALF]], axis=0), 1)
+    upper_x = shift_x(jnp.concatenate([behind_3, behind_2[HALF:]], axis=0), 3)
     state = own_part(table, query_rows, lower, upper)
     low, up, *state = lax.optimization_barrier((lower, upper, *state))
     others = [shift(low, "co", 1), shift(up, "co", 1)]
-    lower_x, upper_x, *state = lax.optimization_barrier((lower_x, upper_x, *state))
-    swapped = [shift(lower_x, "co", 1), shift(upper_x, "co", 1)]
-    state = more_part(table, query_rows, pairs, [*others, lower_x, upper_x], state)
+    own_x, lower_x, upper_x, *state = lax.optimization_barrier((own_x, lower_x, upper_x, *state))
+    arrived = [own_x, lower_x, upper_x]
+    swapped = [shift(x, "co", 1) for x in arrived]
+    state = more_part(table, query_rows, pairs, [*others, *arrived], state)
     return last_part(table, query_rows, pairs, swapped, state, kept_local, router, residual)
 
 

time: 54.1 us -> 53.1 us (0.982)
    ppermute x7 -> x8, waiting for transfers between devices: 5.49 us -> 4.77 us  [shift(): lax.ppermute(block, axis, [(i, (i + distance) % size) for i in range(size)])]
    ppermute x7 -> x8, starting transfers between devices: 12.9 us -> 12.4 us  [shift(): lax.ppermute(block, axis, [(i, (i + distance) % size) for i in range(size)])]
  transfers between devices with their start and end apart: 10 -> 12, of which waited for: 5 -> 5; matrix products, arithmetic and copies ran while one was open for 1% -> 1% of each run, Pallas kernels for 6% -> 6%
where the time goes in v3:
time: 53.1 us; the launch traced here: 52.8 us
  starting transfers between devices  24.8 us (47%)
  waiting for transfers between devices  19.1 us (36%)
  Pallas kernels  7.22 us (14%)
  local copies, waits for them, and re-layouts  0.85 us (2%)
    all_to_all x1, waiting for transfers between devices, shards(): sent = lax.all_to_all(sent, TP, split_axis=0, concat_axis=0, tiled=True)  13.6 us
    ppermute x8, starting transfers between devices, shift(): lax.ppermute(block, axis, [(i, (i + distance) % size) for i in range(size)])  12.4 us
    all_to_all x1, starting transfers between devices, shards(): sent = lax.all_to_all(sent, TP, split_axis=0, concat_axis=0, tiled=True)  11.6 us
    ppermute x8, waiting for transfers between devices, shift(): lax.ppermute(block, axis, [(i, (i + distance) % size) for i in range(size)])  4.77 us
    pallas_call x1, Pallas kernels, last_part(): pl.pallas_call(last_kernel, out_shape=jax.ShapeDtypeStruct((TOK_DEV, HEAD...  2.3 us
    pallas_call x1, Pallas kernels, more_part(): pl.pallas_call(more_kernel, out_shape=STATE, in_specs=[SMEM] + [VMEM] * (...  1.92 us
    pallas_call x1, Pallas kernels, sorted_part(): pl.pallas_call(sorted_kernel, out_shape=jax.ShapeDtypeStruct(shape, BF),...  1.69 us
    pallas_call x1, Pallas kernels, own_part(): pl.pallas_call(own_kernel, out_shape=STATE, in_specs=[SMEM] + [VMEM] * 3,...  1.31 us
  transfers between devices with their start and end apart: 12, of which 5 were waited for; matrix products, arithmetic and copies ran while one was open for 1% of the time, Pallas kernels for 6%

profile of v3, /device:TPU:1, one launch (start us, length us, event | category | flops | bytes accessed | tf_op | source)
XLA Modules:
  0.0 52.8 jit_solution(12856142742250568818)
XLA Ops:
  0.0 1.7 %shard_map.55 = bf16[16,16,768]{2,1,0:T(8,128)(2,1)} custom-call(bf16[1,16,8192]{2,1,0:T(8,128)(2,1)} %queries_ref.1, bf16[1,16,2048]{2,1,0:T(8,128)(2,1)} %pairs_ref.1), custom_call_target="tpu_custom_call" | custom-call | tf_op jit(solution)/shard_map/pallas_call | solution.py:197
  1.7 11.6 %all-to-all-start = ((bf16[16,16,768]{2,1,0:T(8,128)(2,1)}), bf16[16,16,768]{2,1,0:T(8,128)(2,1)S(1)}, u32[]{:S(2)}, u32[]{:S(2)}) async-start(bf16[16,16,768]{2,1,0:T(8,128)(2,1)} %shard_map.55), calls=%async_computation | async-start | bytes 786432 | tf_op jit(solution)/shard_map/all_to_all | solution.py:275
  13.3 0.0 copy-start.1
  13.3 0.0 copy-start.2
  13.4 0.7 %copy-done.2 = bf16[1,256]{1,0:T(2,128)(2,1)S(1)} copy-done((bf16[1,256]{1,0:T(2,128)(2,1)S(1)}, bf16[1,256]{1,0:T(2,128)(2,1)}, u32[]{:S(2)}) %copy-start.2) | copy-done | bytes 536
  14.0 0.1 convert_reduce_fusion
  14.2 0.1 select_reduce_fusion.1
  14.3 0.1 select_reduce_fusion
  14.4 0.1 pad_add_fusion.table_ref
  14.5 13.6 %all-to-all-done = bf16[16,16,768]{2,1,0:T(8,128)(2,1)S(1)} async-done(((bf16[16,16,768]{2,1,0:T(8,128)(2,1)}), bf16[16,16,768]{2,1,0:T(8,128)(2,1)S(1)}, u32[]{:S(2)}, u32[]{:S(2)}) %all-to-all-start) | async-done | bytes 393248 | tf_op jit(solution)/shard_map/all_to_all | solution.py:275
  28.1 0.1 broadcast_in_dim.53.router_ref
  28.2 3.0 %collective-permute-start.2 = (bf16[256,256]{1,0:T(8,128)(2,1)S(1)}, bf16[256,256]{1,0:T(8,128)(2,1)S(1)}, u32[]{:S(2)}, u32[]{:S(2)}) collective-permute-start(bf16[256,256]{1,0:T(8,128)(2,1)S(1)} %slice.16.fill_ref), channel_id=1, source_target_pairs={{0,128},{64,192},{128,0},{192,64},{1,129},{65,193},{129,1},{193,65... | collective-permute-start | bytes 393224 | tf_op jit(solution)/shard_map/ppermute | solution.py:44
  31.2 0.8 %collective-permute-start.4 = (bf16[256,256]{1,0:T(8,128)(2,1)S(1)}, bf16[256,256]{1,0:T(8,128)(2,1)S(1)}, u32[]{:S(2)}, u32[]{:S(2)}) collective-permute-start(bf16[256,256]{1,0:T(8,128)(2,1)S(1)} %slice.16.fill_ref), channel_id=1, source_target_pairs={{0,192},{64,0},{128,64},{192,128},{1,193},{65,1},{129,65},{193,129... | collective-permute-start | bytes 393224 | tf_op jit(solution)/shard_map/ppermute | solution.py:44
  32.0 0.7 %collective-permute-start.1 = (bf16[256,256]{1,0:T(8,128)(2,1)S(1)}, bf16[256,256]{1,0:T(8,128)(2,1)S(1)}, u32[]{:S(2)}, u32[]{:S(2)}) collective-permute-start(bf16[256,256]{1,0:T(8,128)(2,1)S(1)} %slice.16.fill_ref), channel_id=1, source_target_pairs={{0,64},{64,128},{128,192},{192,0},{1,65},{65,129},{129,193},{193,1... | collective-permute-start | bytes 393224 | tf_op jit(solution)/shard_map/ppermute | solution.py:44
  32.7 0.4 collective-permute-start
  33.1 0.5 collective-permute-done.2
  33.6 2.2 %collective-permute-done.4 = bf16[256,256]{1,0:T(8,128)(2,1)S(1)} collective-permute-done((bf16[256,256]{1,0:T(8,128)(2,1)S(1)}, bf16[256,256]{1,0:T(8,128)(2,1)S(1)}, u32[]{:S(2)}, u32[]{:S(2)}) %collective-permute-start.4) | collective-permute-done | bytes 131104 | tf_op jit(solution)/shard_map/ppermute | solution.py:44
  35.8 0.1 collective-permute-start.5
  35.9 2.1 %collective-permute-done.1 = bf16[256,256]{1,0:T(8,128)(2,1)S(1)} collective-permute-done((bf16[256,256]{1,0:T(8,128)(2,1)S(1)}, bf16[256,256]{1,0:T(8,128)(2,1)S(1)}, u32[]{:S(2)}, u32[]{:S(2)}) %collective-permute-start.1) | collective-permute-done | bytes 131104 | tf_op jit(solution)/shard_map/ppermute | solution.py:44
  38.0 0.4 collective-permute-start.3
  38.4 1.3 %shard_map.56 = (f32[1024,128]{1,0:T(8,128)S(1)}, f32[1024,256]{1,0:T(8,128)S(1)}) custom-call(s32[68]{0:T(128)S(1)} %pad_add_fusion.table_ref, bf16[256,512]{1,0:T(8,128)(2,1)S(1)} %slice.17.q_ref, bf16[512,256]{1,0:T(8,128)(2,1)S(1)} %constant_dynamic-update-slice_fusion.lower_ref, bf16[512,256]{1,0:T(8,128)(2,1)S(1)} %constant_dynamic-update-slice_fusion.2.upper_ref), custom_call_target="tpu_custom_call" | custom-call | flops 1000000 | bytes 10000 | tf_op jit(solution)/shard_map/pallas_call | solution.py:214
  39.8 0.0 copy-start
  39.8 3.2 %collective-permute-start.10 = (bf16[512,256]{1,0:T(8,128)(2,1)S(1)}, bf16[512,256]{1,0:T(8,128)(2,1)S(1)}, u32[]{:S(2)}, u32[]{:S(2)}) collective-permute-start(bf16[512,256]{1,0:T(8,128)(2,1)S(1)} %constant_dynamic-update-slice_fusion.2.upper_ref), channel_id=1, source_target_pairs={{0,16},{16,0},{1,17},{17,1},{2,18},{18,2},{3,19},{19,3},{4,20},{20... | collective-permute-start | bytes 786440 | tf_op jit(solution)/shard_map/ppermute | solution.py:44
  43.0 0.1 collective-permute-start.9
  43.1 0.0 collective-permute-done.rest_2_
  43.1 0.0 collective-permute-done.5.rest_4_
  43.1 0.7 %collective-permute-done.3.rest_3_ = bf16[384,256]{1,0:T(8,128)(2,1)S(1)} collective-permute-done((bf16[384,256]{1,0:T(8,128)(2,1)S(1)}, bf16[384,256]{1,0:T(8,128)(2,1)S(1)}, u32[]{:S(2)}, u32[]{:S(2)}) %collective-permute-start.3) | collective-permute-done | bytes 196640 | tf_op jit(solution)/shard_map/ppermute | solution.py:51
  43.8 4.0 %collective-permute-start.7 = (bf16[384,256]{1,0:T(8,128)(2,1)S(1)}, bf16[384,256]{1,0:T(8,128)(2,1)S(1)}, u32[]{:S(2)}, u32[]{:S(2)}) collective-permute-start(bf16[384,256]{1,0:T(8,128)(2,1)S(1)} %collective-permute-done.3.rest_3_), channel_id=1, source_target_pairs={{0,16},{16,0},{1,17},{17,1},{2,18},{18,2},{3,19},{19,3},{4,20},{20... | collective-permute-start | bytes 589832 | tf_op jit(solution)/shard_map/ppermute | solution.py:44
  47.8 0.0 collective-permute-start.8
  47.8 0.5 collective-permute-start.6
  48.4 1.9 %shard_map.57 = (f32[1024,128]{1,0:T(8,128)S(1)}, f32[1024,256]{1,0:T(8,128)S(1)}) custom-call(s32[68]{0:T(128)S(1)} %pad_add_fusion.table_ref, bf16[256,512]{1,0:T(8,128)(2,1)S(1)} %slice.17.q_ref, bf16[256,256]{1,0:T(8,128)(2,1)S(1)} %slice.16.fill_ref, bf16[512,256]{1,0:T(8,128)(2,1)S(1)} %collective-permute-done.9.rest_0_, ...), custom_call_target="tpu_custom_call" | custom-call | flops 1000000 | bytes 10000 | tf_op jit(solution)/shard_map/pallas_call | solution.py:226
  50.3 2.3 %shard_map.58 = bf16[1024,512]{1,0:T(8,128)(2,1)} custom-call(s32[68]{0:T(128)S(1)} %pad_add_fusion.table_ref, bf16[256,512]{1,0:T(8,128)(2,1)S(1)} %slice.17.q_ref, bf16[256,256]{1,0:T(8,128)(2,1)S(1)} %slice.16.fill_ref, bf16[256,256]{1,0:T(8,128)(2,1)S(1)} %collective-permute-done.6.own_ref, bf16[384,256]{1,0:T(8,128)(2,1)S(1)} %collective-permute-done.7.lower_ref, ...), custom_call_target="tpu_custom_call" | custom-call | tf_op jit(solution)/shard_map/pallas_call | solution.py:238
  (20 shorter events, 0.2 us)
Async XLA Ops:
  1.7 26.4 %all-to-all-start = ((bf16[16,16,768]{2,1,0:T(8,128)(2,1)}), bf16[16,16,768]{2,1,0:T(8,128)(2,1)S(1)}, u32[]{:S(2)}, u32[]{:S(2)}) async-start(bf16[16,16,768]{2,1,0:T(8,128)(2,1)} %shard_map.55), calls=%async_computation | async-start | bytes 786432 | tf_op jit(solution)/shard_map/all_to_all | solution.py:275
  13.3 0.7 %copy-start.1 = (s32[16,256]{1,0:T(8,128)S(1)}, s32[16,256]{1,0:T(8,128)}, u32[]{:S(2)}) copy-start(s32[16,256]{1,0:T(8,128)} %kept_ref.1) | copy-start | bytes 49156
  13.3 0.7 %copy-start.2 = (bf16[1,256]{1,0:T(2,128)(2,1)S(1)}, bf16[1,256]{1,0:T(2,128)(2,1)}, u32[]{:S(2)}) copy-start(bf16[1,256]{1,0:T(2,128)(2,1)} %param.9) | copy-start | bytes 1540
  28.2 5.4 %collective-permute-start.2 = (bf16[256,256]{1,0:T(8,128)(2,1)S(1)}, bf16[256,256]{1,0:T(8,128)(2,1)S(1)}, u32[]{:S(2)}, u32[]{:S(2)}) collective-permute-start(bf16[256,256]{1,0:T(8,128)(2,1)S(1)} %slice.16.fill_ref), channel_id=1, source_target_pairs={{0,128},{64,192},{128,0},{192,64},{1,129},{65,193},{129,1},{193,65... | collective-permute-start | bytes 393224 | tf_op jit(solution)/shard_map/ppermute | solution.py:44
  31.2 4.6 %collective-permute-start.4 = (bf16[256,256]{1,0:T(8,128)(2,1)S(1)}, bf16[256,256]{1,0:T(8,128)(2,1)S(1)}, u32[]{:S(2)}, u32[]{:S(2)}) collective-permute-start(bf16[256,256]{1,0:T(8,128)(2,1)S(1)} %slice.16.fill_ref), channel_id=1, source_target_pairs={{0,192},{64,0},{128,64},{192,128},{1,193},{65,1},{129,65},{193,129... | collective-permute-start | bytes 393224 | tf_op jit(solution)/shard_map/ppermute | solution.py:44
  32.0 6.0 %collective-permute-start.1 = (bf16[256,256]{1,0:T(8,128)(2,1)S(1)}, bf16[256,256]{1,0:T(8,128)(2,1)S(1)}, u32[]{:S(2)}, u32[]{:S(2)}) collective-permute-start(bf16[256,256]{1,0:T(8,128)(2,1)S(1)} %slice.16.fill_ref), channel_id=1, source_target_pairs={{0,64},{64,128},{128,192},{192,0},{1,65},{65,129},{129,193},{193,1... | collective-permute-start | bytes 393224 | tf_op jit(solution)/shard_map/ppermute | solution.py:44
  32.7 10.4 %collective-permute-start = (bf16[256,256]{1,0:T(8,128)(2,1)S(1)}, bf16[256,256]{1,0:T(8,128)(2,1)S(1)}, u32[]{:S(2)}, u32[]{:S(2)}) collective-permute-start(bf16[256,256]{1,0:T(8,128)(2,1)S(1)} %slice.16.fill_ref), channel_id=1, source_target_pairs={{0,32},{32,1},{1,33},{33,0},{2,34},{34,3},{3,35},{35,2},{4,36},{36... | collective-permute-start | bytes 393224 | tf_op jit(solution)/shard_map/ppermute | solution.py:51
  35.8 7.3 %collective-permute-start.5 = (bf16[384,256]{1,0:T(8,128)(2,1)S(1)}, bf16[384,256]{1,0:T(8,128)(2,1)S(1)}, u32[]{:S(2)}, u32[]{:S(2)}) collective-permute-start(bf16[384,256]{1,0:T(8,128)(2,1)S(1)} %pad_maximum_fusion.1), channel_id=1, source_target_pairs={{0,33},{32,0},{1,32},{33,1},{2,35},{34,2},{3,34},{35,3},{4,37},{36... | collective-permute-start | bytes 589832 | tf_op jit(solution)/shard_map/ppermute | solution.py:51
  38.0 5.8 %collective-permute-start.3 = (bf16[384,256]{1,0:T(8,128)(2,1)S(1)}, bf16[384,256]{1,0:T(8,128)(2,1)S(1)}, u32[]{:S(2)}, u32[]{:S(2)}) collective-permute-start(bf16[384,256]{1,0:T(8,128)(2,1)S(1)} %pad_maximum_fusion), channel_id=1, source_target_pairs={{0,32},{32,1},{1,33},{33,0},{2,34},{34,3},{3,35},{35,2},{4,36},{36... | collective-permute-start | bytes 589832 | tf_op jit(solution)/shard_map/ppermute | solution.py:51
  39.8 10.6 %copy-start = (bf16[1024,512]{1,0:T(8,128)(2,1)S(1)}, bf16[1024,512]{1,0:T(8,128)(2,1)}, u32[]{:S(2)}) copy-start(bf16[1024,512]{1,0:T(8,128)(2,1)} %residual_ref.1) | copy-start | bytes 3145732
  39.8 8.6 %collective-permute-start.10 = (bf16[512,256]{1,0:T(8,128)(2,1)S(1)}, bf16[512,256]{1,0:T(8,128)(2,1)S(1)}, u32[]{:S(2)}, u32[]{:S(2)}) collective-permute-start(bf16[512,256]{1,0:T(8,128)(2,1)S(1)} %constant_dynamic-update-slice_fusion.2.upper_ref), channel_id=1, source_target_pairs={{0,16},{16,0},{1,17},{17,1},{2,18},{18,2},{3,19},{19,3},{4,20},{20... | collective-permute-start | bytes 786440 | tf_op jit(solution)/shard_map/ppermute | solution.py:44
  43.0 5.3 %collective-permute-start.9 = (bf16[512,256]{1,0:T(8,128)(2,1)S(1)}, bf16[512,256]{1,0:T(8,128)(2,1)S(1)}, u32[]{:S(2)}, u32[]{:S(2)}) collective-permute-start(bf16[512,256]{1,0:T(8,128)(2,1)S(1)} %constant_dynamic-update-slice_fusion.lower_ref), channel_id=1, source_target_pairs={{0,16},{16,0},{1,17},{17,1},{2,18},{18,2},{3,19},{19,3},{4,20},{20... | collective-permute-start | bytes 786440 | tf_op jit(solution)/shard_map/ppermute | solution.py:44
  43.8 6.5 %collective-permute-start.7 = (bf16[384,256]{1,0:T(8,128)(2,1)S(1)}, bf16[384,256]{1,0:T(8,128)(2,1)S(1)}, u32[]{:S(2)}, u32[]{:S(2)}) collective-permute-start(bf16[384,256]{1,0:T(8,128)(2,1)S(1)} %collective-permute-done.3.rest_3_), channel_id=1, source_target_pairs={{0,16},{16,0},{1,17},{17,1},{2,18},{18,2},{3,19},{19,3},{4,20},{20... | collective-permute-start | bytes 589832 | tf_op jit(solution)/shard_map/ppermute | solution.py:44
  47.8 2.5 %collective-permute-start.8 = (bf16[384,256]{1,0:T(8,128)(2,1)S(1)}, bf16[384,256]{1,0:T(8,128)(2,1)S(1)}, u32[]{:S(2)}, u32[]{:S(2)}) collective-permute-start(bf16[384,256]{1,0:T(8,128)(2,1)S(1)} %collective-permute-done.5.rest_4_), channel_id=1, source_target_pairs={{0,16},{16,0},{1,17},{17,1},{2,18},{18,2},{3,19},{19,3},{4,20},{20... | collective-permute-start | bytes 589832 | tf_op jit(solution)/shard_map/ppermute | solution.py:44
  47.8 2.4 %collective-permute-start.6 = (bf16[256,256]{1,0:T(8,128)(2,1)S(1)}, bf16[256,256]{1,0:T(8,128)(2,1)S(1)}, u32[]{:S(2)}, u32[]{:S(2)}) collective-permute-start(bf16[256,256]{1,0:T(8,128)(2,1)S(1)} %collective-permute-done.rest_2_), channel_id=1, source_target_pairs={{0,16},{16,0},{1,17},{17,1},{2,18},{18,2},{3,19},{19,3},{4,20},{20... | collective-permute-start | bytes 393224 | tf_op jit(solution)/shard_map/ppermute | solution.py:44

commit v4 on v3

--- a/solution.py
+++ b/solution.py
@@ -56,11 +56,16 @@
     fill = jnp.broadcast_to(fill_ref[0:1, :HD], (HALF, HD))
     for at, (piece, first) in enumerate(pieces):
         start = pl.multiple_of(table_ref[PIECES_ALL + FIRST[group] + at], GRAN)
-        inside = row_in < table_ref[FIRST[group] + at]
+        live = table_ref[FIRST[group] + at]
         rows, now = pl.ds(start, HALF), slice(first, first + HALF)
-        k_buf[rows, :] = jnp.where(inside, piece[now, :HD], fill)
-        v_buf[rows, :HD] = jnp.where(inside, piece[now, HD:], jnp.zeros((HALF, HD), BF))
-        v_buf[rows, HD:] = jnp.where(inside, 1.0, 0.0).astype(BF)
+
+        @pl.when(live > 0)
+        def _():
+            inside = row_in < live
+            k_buf[rows, :] = jnp.where(inside, piece[now, :HD], fill)
+            v_buf[rows, :HD] = jnp.where(inside, piece[now, HD:], jnp.zeros((HALF, HD), BF))
+            v_buf[rows, HD:] = jnp.where(inside, 1.0, 0.0).astype(BF)
+
     end = pl.multiple_of(table_ref[2 * PIECES_ALL + group], GRAN)
     k_buf[pl.ds(end, TILE), :] = jnp.broadcast_to(fill_ref[0:1, :HD], (TILE, HD))
     v_buf[pl.ds(end, TILE), :] = jnp.zeros((TILE, 2 * HD), BF)
@@ -217,7 +222,6 @@
         in_specs=[SMEM] + [VMEM] * 3,
         out_specs=[VMEM] * 2,
         scratch_shapes=buffers(PIECES),
-        cost_estimate=SMALL,
         compiler_params=params(16),
     )(table, query_rows, lower, upper)
 

time: 53.1 us -> 52.6 us (level)
  Pallas kernels: 7.22 us -> 6.68 us
  transfers between devices with their start and end apart: 12 -> 12, of which waited for: 5 -> 5; matrix products, arithmetic and copies ran while one was open for 1% -> 1% of each run, Pallas kernels for 6% -> 5%
where the time goes in v4:
time: 52.6 us; the launch traced here: 52.3 us
  starting transfers between devices  24.8 us (47%)
  waiting for transfers between devices  19.2 us (37%)
  Pallas kernels  6.68 us (13%)
  local copies, waits for them, and re-layouts  0.85 us (2%)
    all_to_all x1, waiting for transfers between devices, shards(): sent = lax.all_to_all(sent, TP, split_axis=0, concat_axis=0, tiled=True)  13.6 us
    ppermute x8, starting transfers between devices, shift(): lax.ppermute(block, axis, [(i, (i + distance) % size) for i in range(size)])  12.4 us
    all_to_all x1, starting transfers between devices, shards(): sent = lax.all_to_all(sent, TP, split_axis=0, concat_axis=0, tiled=True)  11.6 us
    ppermute x8, waiting for transfers between devices, shift(): lax.ppermute(block, axis, [(i, (i + distance) % size) for i in range(size)])  4.77 us
    pallas_call x1, Pallas kernels, last_part(): pl.pallas_call(last_kernel, out_shape=jax.ShapeDtypeStruct((TOK_DEV, HEAD...  2.14 us
    pallas_call x1, Pallas kernels, sorted_part(): pl.pallas_call(sorted_kernel, out_shape=jax.ShapeDtypeStruct(shape, BF),...  1.69 us
    pallas_call x1, Pallas kernels, more_part(): pl.pallas_call(more_kernel, out_shape=STATE, in_specs=[SMEM] + [VMEM] * (...  1.6 us
    pallas_call x1, Pallas kernels, own_part(): pl.pallas_call(own_kernel, out_shape=STATE, in_specs=[SMEM] + [VMEM] * 3,...  1.25 us
  transfers between devices with their start and end apart: 12, of which 5 were waited for; matrix products, arithmetic and copies ran while one was open for 1% of the time, Pallas kernels for 5%

profile of v4, /device:TPU:1, one launch (start us, length us, event | category | flops | bytes accessed | tf_op | source)
XLA Modules:
  0.0 52.3 jit_solution(1718709128090187312)
XLA Ops:
  0.0 1.7 %shard_map.55 = bf16[16,16,768]{2,1,0:T(8,128)(2,1)} custom-call(bf16[1,16,8192]{2,1,0:T(8,128)(2,1)} %queries_ref.1, bf16[1,16,2048]{2,1,0:T(8,128)(2,1)} %pairs_ref.1), custom_call_target="tpu_custom_call" | custom-call | tf_op jit(solution)/shard_map/pallas_call | solution.py:202
  1.7 11.6 %all-to-all-start = ((bf16[16,16,768]{2,1,0:T(8,128)(2,1)}), bf16[16,16,768]{2,1,0:T(8,128)(2,1)S(1)}, u32[]{:S(2)}, u32[]{:S(2)}) async-start(bf16[16,16,768]{2,1,0:T(8,128)(2,1)} %shard_map.55), calls=%async_computation | async-start | bytes 786432 | tf_op jit(solution)/shard_map/all_to_all | solution.py:279
  13.3 0.0 copy-start.1
  13.3 0.0 copy-start.2
  13.4 0.7 %copy-done.2 = bf16[1,256]{1,0:T(2,128)(2,1)S(1)} copy-done((bf16[1,256]{1,0:T(2,128)(2,1)S(1)}, bf16[1,256]{1,0:T(2,128)(2,1)}, u32[]{:S(2)}) %copy-start.2) | copy-done | bytes 536
  14.0 0.1 convert_reduce_fusion
  14.2 0.1 select_reduce_fusion.1
  14.3 0.1 select_reduce_fusion
  14.4 0.1 pad_add_fusion.table_ref
  14.5 13.6 %all-to-all-done = bf16[16,16,768]{2,1,0:T(8,128)(2,1)S(1)} async-done(((bf16[16,16,768]{2,1,0:T(8,128)(2,1)}), bf16[16,16,768]{2,1,0:T(8,128)(2,1)S(1)}, u32[]{:S(2)}, u32[]{:S(2)}) %all-to-all-start) | async-done | bytes 393248 | tf_op jit(solution)/shard_map/all_to_all | solution.py:279
  28.1 0.1 broadcast_in_dim.53.router_ref
  28.2 3.0 %collective-permute-start.2 = (bf16[256,256]{1,0:T(8,128)(2,1)S(1)}, bf16[256,256]{1,0:T(8,128)(2,1)S(1)}, u32[]{:S(2)}, u32[]{:S(2)}) collective-permute-start(bf16[256,256]{1,0:T(8,128)(2,1)S(1)} %slice.16.fill_ref), channel_id=1, source_target_pairs={{0,128},{64,192},{128,0},{192,64},{1,129},{65,193},{129,1},{193,65... | collective-permute-start | bytes 393224 | tf_op jit(solution)/shard_map/ppermute | solution.py:44
  31.2 0.8 %collective-permute-start.4 = (bf16[256,256]{1,0:T(8,128)(2,1)S(1)}, bf16[256,256]{1,0:T(8,128)(2,1)S(1)}, u32[]{:S(2)}, u32[]{:S(2)}) collective-permute-start(bf16[256,256]{1,0:T(8,128)(2,1)S(1)} %slice.16.fill_ref), channel_id=1, source_target_pairs={{0,192},{64,0},{128,64},{192,128},{1,193},{65,1},{129,65},{193,129... | collective-permute-start | bytes 393224 | tf_op jit(solution)/shard_map/ppermute | solution.py:44
  32.0 0.7 %collective-permute-start.1 = (bf16[256,256]{1,0:T(8,128)(2,1)S(1)}, bf16[256,256]{1,0:T(8,128)(2,1)S(1)}, u32[]{:S(2)}, u32[]{:S(2)}) collective-permute-start(bf16[256,256]{1,0:T(8,128)(2,1)S(1)} %slice.16.fill_ref), channel_id=1, source_target_pairs={{0,64},{64,128},{128,192},{192,0},{1,65},{65,129},{129,193},{193,1... | collective-permute-start | bytes 393224 | tf_op jit(solution)/shard_map/ppermute | solution.py:44
  32.7 0.4 collective-permute-start
  33.1 0.5 collective-permute-done.2
  33.6 2.2 %collective-permute-done.4 = bf16[256,256]{1,0:T(8,128)(2,1)S(1)} collective-permute-done((bf16[256,256]{1,0:T(8,128)(2,1)S(1)}, bf16[256,256]{1,0:T(8,128)(2,1)S(1)}, u32[]{:S(2)}, u32[]{:S(2)}) %collective-permute-start.4) | collective-permute-done | bytes 131104 | tf_op jit(solution)/shard_map/ppermute | solution.py:44
  35.8 0.1 collective-permute-start.5
  35.9 2.1 %collective-permute-done.1 = bf16[256,256]{1,0:T(8,128)(2,1)S(1)} collective-permute-done((bf16[256,256]{1,0:T(8,128)(2,1)S(1)}, bf16[256,256]{1,0:T(8,128)(2,1)S(1)}, u32[]{:S(2)}, u32[]{:S(2)}) %collective-permute-start.1) | collective-permute-done | bytes 131104 | tf_op jit(solution)/shard_map/ppermute | solution.py:44
  38.0 0.4 collective-permute-start.3
  38.4 1.2 %shard_map.56 = (f32[1024,128]{1,0:T(8,128)S(1)}, f32[1024,256]{1,0:T(8,128)S(1)}) custom-call(s32[68]{0:T(128)S(1)} %pad_add_fusion.table_ref, bf16[256,512]{1,0:T(8,128)(2,1)S(1)} %slice.17.q_ref, bf16[512,256]{1,0:T(8,128)(2,1)S(1)} %constant_dynamic-update-slice_fusion.lower_ref, bf16[512,256]{1,0:T(8,128)(2,1)S(1)} %constant_dynamic-update-slice_fusion.2.upper_ref), custom_call_target="tpu_custom_call" | custom-call | tf_op jit(solution)/shard_map/pallas_call | solution.py:219
  39.7 0.0 copy-start
  39.7 3.2 %collective-permute-start.10 = (bf16[512,256]{1,0:T(8,128)(2,1)S(1)}, bf16[512,256]{1,0:T(8,128)(2,1)S(1)}, u32[]{:S(2)}, u32[]{:S(2)}) collective-permute-start(bf16[512,256]{1,0:T(8,128)(2,1)S(1)} %constant_dynamic-update-slice_fusion.2.upper_ref), channel_id=1, source_target_pairs={{0,16},{16,0},{1,17},{17,1},{2,18},{18,2},{3,19},{19,3},{4,20},{20... | collective-permute-start | bytes 786440 | tf_op jit(solution)/shard_map/ppermute | solution.py:44
  43.0 0.1 collective-permute-start.9
  43.1 0.0 collective-permute-done.rest_2_
  43.1 0.0 collective-permute-done.5.rest_4_
  43.1 0.7 %collective-permute-done.3.rest_3_ = bf16[384,256]{1,0:T(8,128)(2,1)S(1)} collective-permute-done((bf16[384,256]{1,0:T(8,128)(2,1)S(1)}, bf16[384,256]{1,0:T(8,128)(2,1)S(1)}, u32[]{:S(2)}, u32[]{:S(2)}) %collective-permute-start.3) | collective-permute-done | bytes 196640 | tf_op jit(solution)/shard_map/ppermute | solution.py:51
  43.8 4.0 %collective-permute-start.7 = (bf16[384,256]{1,0:T(8,128)(2,1)S(1)}, bf16[384,256]{1,0:T(8,128)(2,1)S(1)}, u32[]{:S(2)}, u32[]{:S(2)}) collective-permute-start(bf16[384,256]{1,0:T(8,128)(2,1)S(1)} %collective-permute-done.3.rest_3_), channel_id=1, source_target_pairs={{0,16},{16,0},{1,17},{17,1},{2,18},{18,2},{3,19},{19,3},{4,20},{20... | collective-permute-start | bytes 589832 | tf_op jit(solution)/shard_map/ppermute | solution.py:44
  47.8 0.0 collective-permute-start.8
  47.8 0.5 collective-permute-start.6
  48.4 1.6 %shard_map.57 = (f32[1024,128]{1,0:T(8,128)S(1)}, f32[1024,256]{1,0:T(8,128)S(1)}) custom-call(s32[68]{0:T(128)S(1)} %pad_add_fusion.table_ref, bf16[256,512]{1,0:T(8,128)(2,1)S(1)} %slice.17.q_ref, bf16[256,256]{1,0:T(8,128)(2,1)S(1)} %slice.16.fill_ref, bf16[512,256]{1,0:T(8,128)(2,1)S(1)} %collective-permute-done.9.rest_0_, ...), custom_call_target="tpu_custom_call" | custom-call | flops 1000000 | bytes 10000 | tf_op jit(solution)/shard_map/pallas_call | solution.py:230
  50.0 2.1 %shard_map.58 = bf16[1024,512]{1,0:T(8,128)(2,1)} custom-call(s32[68]{0:T(128)S(1)} %pad_add_fusion.table_ref, bf16[256,512]{1,0:T(8,128)(2,1)S(1)} %slice.17.q_ref, bf16[256,256]{1,0:T(8,128)(2,1)S(1)} %slice.16.fill_ref, bf16[256,256]{1,0:T(8,128)(2,1)S(1)} %collective-permute-done.6.own_ref, bf16[384,256]{1,0:T(8,128)(2,1)S(1)} %collective-permute-done.7.lower_ref, ...), custom_call_target="tpu_custom_call" | custom-call | tf_op jit(solution)/shard_map/pallas_call | solution.py:242
  (20 shorter events, 0.2 us)
Async XLA Ops:
  1.7 26.4 %all-to-all-start = ((bf16[16,16,768]{2,1,0:T(8,128)(2,1)}), bf16[16,16,768]{2,1,0:T(8,128)(2,1)S(1)}, u32[]{:S(2)}, u32[]{:S(2)}) async-start(bf16[16,16,768]{2,1,0:T(8,128)(2,1)} %shard_map.55), calls=%async_computation | async-start | bytes 786432 | tf_op jit(solution)/shard_map/all_to_all | solution.py:279
  13.3 0.7 %copy-start.1 = (s32[16,256]{1,0:T(8,128)S(1)}, s32[16,256]{1,0:T(8,128)}, u32[]{:S(2)}) copy-start(s32[16,256]{1,0:T(8,128)} %kept_ref.1) | copy-start | bytes 49156
  13.3 0.7 %copy-start.2 = (bf16[1,256]{1,0:T(2,128)(2,1)S(1)}, bf16[1,256]{1,0:T(2,128)(2,1)}, u32[]{:S(2)}) copy-start(bf16[1,256]{1,0:T(2,128)(2,1)} %param.9) | copy-start | bytes 1540
  28.2 5.4 %collective-permute-start.2 = (bf16[256,256]{1,0:T(8,128)(2,1)S(1)}, bf16[256,256]{1,0:T(8,128)(2,1)S(1)}, u32[]{:S(2)}, u32[]{:S(2)}) collective-permute-start(bf16[256,256]{1,0:T(8,128)(2,1)S(1)} %slice.16.fill_ref), channel_id=1, source_target_pairs={{0,128},{64,192},{128,0},{192,64},{1,129},{65,193},{129,1},{193,65... | collective-permute-start | bytes 393224 | tf_op jit(solution)/shard_map/ppermute | solution.py:44
  31.2 4.6 %collective-permute-start.4 = (bf16[256,256]{1,0:T(8,128)(2,1)S(1)}, bf16[256,256]{1,0:T(8,128)(2,1)S(1)}, u32[]{:S(2)}, u32[]{:S(2)}) collective-permute-start(bf16[256,256]{1,0:T(8,128)(2,1)S(1)} %slice.16.fill_ref), channel_id=1, source_target_pairs={{0,192},{64,0},{128,64},{192,128},{1,193},{65,1},{129,65},{193,129... | collective-permute-start | bytes 393224 | tf_op jit(solution)/shard_map/ppermute | solution.py:44
  32.0 6.0 %collective-permute-start.1 = (bf16[256,256]{1,0:T(8,128)(2,1)S(1)}, bf16[256,256]{1,0:T(8,128)(2,1)S(1)}, u32[]{:S(2)}, u32[]{:S(2)}) collective-permute-start(bf16[256,256]{1,0:T(8,128)(2,1)S(1)} %slice.16.fill_ref), channel_id=1, source_target_pairs={{0,64},{64,128},{128,192},{192,0},{1,65},{65,129},{129,193},{193,1... | collective-permute-start | bytes 393224 | tf_op jit(solution)/shard_map/ppermute | solution.py:44
  32.7 10.4 %collective-permute-start = (bf16[256,256]{1,0:T(8,128)(2,1)S(1)}, bf16[256,256]{1,0:T(8,128)(2,1)S(1)}, u32[]{:S(2)}, u32[]{:S(2)}) collective-permute-start(bf16[256,256]{1,0:T(8,128)(2,1)S(1)} %slice.16.fill_ref), channel_id=1, source_target_pairs={{0,32},{32,1},{1,33},{33,0},{2,34},{34,3},{3,35},{35,2},{4,36},{36... | collective-permute-start | bytes 393224 | tf_op jit(solution)/shard_map/ppermute | solution.py:51
  35.8 7.2 %collective-permute-start.5 = (bf16[384,256]{1,0:T(8,128)(2,1)S(1)}, bf16[384,256]{1,0:T(8,128)(2,1)S(1)}, u32[]{:S(2)}, u32[]{:S(2)}) collective-permute-start(bf16[384,256]{1,0:T(8,128)(2,1)S(1)} %pad_maximum_fusion.1), channel_id=1, source_target_pairs={{0,33},{32,0},{1,32},{33,1},{2,35},{34,2},{3,34},{35,3},{4,37},{36... | collective-permute-start | bytes 589832 | tf_op jit(solution)/shard_map/ppermute | solution.py:51
  38.0 5.8 %collective-permute-start.3 = (bf16[384,256]{1,0:T(8,128)(2,1)S(1)}, bf16[384,256]{1,0:T(8,128)(2,1)S(1)}, u32[]{:S(2)}, u32[]{:S(2)}) collective-permute-start(bf16[384,256]{1,0:T(8,128)(2,1)S(1)} %pad_maximum_fusion), channel_id=1, source_target_pairs={{0,32},{32,1},{1,33},{33,0},{2,34},{34,3},{3,35},{35,2},{4,36},{36... | collective-permute-start | bytes 589832 | tf_op jit(solution)/shard_map/ppermute | solution.py:51
  39.7 10.3 %copy-start = (bf16[1024,512]{1,0:T(8,128)(2,1)S(1)}, bf16[1024,512]{1,0:T(8,128)(2,1)}, u32[]{:S(2)}) copy-start(bf16[1024,512]{1,0:T(8,128)(2,1)} %residual_ref.1) | copy-start | bytes 3145732
  39.7 8.6 %collective-permute-start.10 = (bf16[512,256]{1,0:T(8,128)(2,1)S(1)}, bf16[512,256]{1,0:T(8,128)(2,1)S(1)}, u32[]{:S(2)}, u32[]{:S(2)}) collective-permute-start(bf16[512,256]{1,0:T(8,128)(2,1)S(1)} %constant_dynamic-update-slice_fusion.2.upper_ref), channel_id=1, source_target_pairs={{0,16},{16,0},{1,17},{17,1},{2,18},{18,2},{3,19},{19,3},{4,20},{20... | collective-permute-start | bytes 786440 | tf_op jit(solution)/shard_map/ppermute | solution.py:44
  43.0 5.4 %collective-permute-start.9 = (bf16[512,256]{1,0:T(8,128)(2,1)S(1)}, bf16[512,256]{1,0:T(8,128)(2,1)S(1)}, u32[]{:S(2)}, u32[]{:S(2)}) collective-permute-start(bf16[512,256]{1,0:T(8,128)(2,1)S(1)} %constant_dynamic-update-slice_fusion.lower_ref), channel_id=1, source_target_pairs={{0,16},{16,0},{1,17},{17,1},{2,18},{18,2},{3,19},{19,3},{4,20},{20... | collective-permute-start | bytes 786440 | tf_op jit(solution)/shard_map/ppermute | solution.py:44
  43.8 6.2 %collective-permute-start.7 = (bf16[384,256]{1,0:T(8,128)(2,1)S(1)}, bf16[384,256]{1,0:T(8,128)(2,1)S(1)}, u32[]{:S(2)}, u32[]{:S(2)}) collective-permute-start(bf16[384,256]{1,0:T(8,128)(2,1)S(1)} %collective-permute-done.3.rest_3_), channel_id=1, source_target_pairs={{0,16},{16,0},{1,17},{17,1},{2,18},{18,2},{3,19},{19,3},{4,20},{20... | collective-permute-start | bytes 589832 | tf_op jit(solution)/shard_map/ppermute | solution.py:44
  47.8 2.2 %collective-permute-start.8 = (bf16[384,256]{1,0:T(8,128)(2,1)S(1)}, bf16[384,256]{1,0:T(8,128)(2,1)S(1)}, u32[]{:S(2)}, u32[]{:S(2)}) collective-permute-start(bf16[384,256]{1,0:T(8,128)(2,1)S(1)} %collective-permute-done.5.rest_4_), channel_id=1, source_target_pairs={{0,16},{16,0},{1,17},{17,1},{2,18},{18,2},{3,19},{19,3},{4,20},{20... | collective-permute-start | bytes 589832 | tf_op jit(solution)/shard_map/ppermute | solution.py:44
  47.8 2.1 %collective-permute-start.6 = (bf16[256,256]{1,0:T(8,128)(2,1)S(1)}, bf16[256,256]{1,0:T(8,128)(2,1)S(1)}, u32[]{:S(2)}, u32[]{:S(2)}) collective-permute-start(bf16[256,256]{1,0:T(8,128)(2,1)S(1)} %collective-permute-done.rest_2_), channel_id=1, source_target_pairs={{0,16},{16,0},{1,17},{17,1},{2,18},{18,2},{3,19},{19,3},{4,20},{20... | collective-permute-start | bytes 393224 | tf_op jit(solution)/shard_map/ppermute | solution.py:44

commit v5 on v4

--- a/solution.py
+++ b/solution.py
@@ -53,7 +53,7 @@
 
 def compact(pieces, group, table_ref, fill_ref, k_buf, v_buf):
     row_in = lax.broadcasted_iota(jnp.int32, (HALF, HD), 0)
-    fill = jnp.broadcast_to(fill_ref[0:1, :HD], (HALF, HD))
+    fill = jnp.broadcast_to(fill_ref[:GRAN, :HD][0:1], (HALF, HD))
     for at, (piece, first) in enumerate(pieces):
         start = pl.multiple_of(table_ref[PIECES_ALL + FIRST[group] + at], GRAN)
         live = table_ref[FIRST[group] + at]
@@ -67,7 +67,7 @@
             v_buf[rows, HD:] = jnp.where(inside, 1.0, 0.0).astype(BF)
 
     end = pl.multiple_of(table_ref[2 * PIECES_ALL + group], GRAN)
-    k_buf[pl.ds(end, TILE), :] = jnp.broadcast_to(fill_ref[0:1, :HD], (TILE, HD))
+    k_buf[pl.ds(end, TILE), :] = jnp.concatenate([fill] * (TILE // HALF), axis=0)
     v_buf[pl.ds(end, TILE), :] = jnp.zeros((TILE, 2 * HD), BF)
     return (end + TILE - 1) // TILE
 

time: 52.6 us -> 52.6 us (level)
  no operation moved by 1% of the time
where the time goes in v5:
time: 52.6 us; the launch traced here: 52.4 us
  starting transfers between devices  24.8 us (47%)
  waiting for transfers between devices  19.2 us (37%)
  Pallas kernels  6.7 us (13%)
  local copies, waits for them, and re-layouts  0.85 us (2%)
    all_to_all x1, waiting for transfers between devices, shards(): sent = lax.all_to_all(sent, TP, split_axis=0, concat_axis=0, tiled=True)  13.6 us
    ppermute x8, starting transfers between devices, shift(): lax.ppermute(block, axis, [(i, (i + distance) % size) for i in range(size)])  12.4 us
    all_to_all x1, starting transfers between devices, shards(): sent = lax.all_to_all(sent, TP, split_axis=0, concat_axis=0, tiled=True)  11.6 us
    ppermute x8, waiting for transfers between devices, shift(): lax.ppermute(block, axis, [(i, (i + distance) % size) for i in range(size)])  4.77 us
    pallas_call x1, Pallas kernels, last_part(): pl.pallas_call(last_kernel, out_shape=jax.ShapeDtypeStruct((TOK_DEV, HEAD...  2.14 us
    pallas_call x1, Pallas kernels, sorted_part(): pl.pallas_call(sorted_kernel, out_shape=jax.ShapeDtypeStruct(shape, BF),...  1.69 us
    pallas_call x1, Pallas kernels, more_part(): pl.pallas_call(more_kernel, out_shape=STATE, in_specs=[SMEM] + [VMEM] * (...  1.62 us
    pallas_call x1, Pallas kernels, own_part(): pl.pallas_call(own_kernel, out_shape=STATE, in_specs=[SMEM] + [VMEM] * 3,...  1.24 us
  transfers between devices with their start and end apart: 12, of which 5 were waited for; matrix products, arithmetic and copies ran while one was open for 1% of the time, Pallas kernels for 5%

profile of v5, /device:TPU:1, one launch (start us, length us, event | category | flops | bytes accessed | tf_op | source)
XLA Modules:
  0.0 52.4 jit_solution(1092692023453700164)
XLA Ops:
  0.0 1.7 %shard_map.55 = bf16[16,16,768]{2,1,0:T(8,128)(2,1)} custom-call(bf16[1,16,8192]{2,1,0:T(8,128)(2,1)} %queries_ref.1, bf16[1,16,2048]{2,1,0:T(8,128)(2,1)} %pairs_ref.1), custom_call_target="tpu_custom_call" | custom-call | tf_op jit(solution)/shard_map/pallas_call | solution.py:202
  1.7 11.6 %all-to-all-start = ((bf16[16,16,768]{2,1,0:T(8,128)(2,1)}), bf16[16,16,768]{2,1,0:T(8,128)(2,1)S(1)}, u32[]{:S(2)}, u32[]{:S(2)}) async-start(bf16[16,16,768]{2,1,0:T(8,128)(2,1)} %shard_map.55), calls=%async_computation | async-start | bytes 786432 | tf_op jit(solution)/shard_map/all_to_all | solution.py:279
  13.3 0.0 copy-start.1
  13.3 0.0 copy-start.2
  13.4 0.7 %copy-done.2 = bf16[1,256]{1,0:T(2,128)(2,1)S(1)} copy-done((bf16[1,256]{1,0:T(2,128)(2,1)S(1)}, bf16[1,256]{1,0:T(2,128)(2,1)}, u32[]{:S(2)}) %copy-start.2) | copy-done | bytes 536
  14.0 0.1 convert_reduce_fusion
  14.2 0.1 select_reduce_fusion.1
  14.3 0.1 select_reduce_fusion
  14.4 0.1 pad_add_fusion.table_ref
  14.5 13.6 %all-to-all-done = bf16[16,16,768]{2,1,0:T(8,128)(2,1)S(1)} async-done(((bf16[16,16,768]{2,1,0:T(8,128)(2,1)}), bf16[16,16,768]{2,1,0:T(8,128)(2,1)S(1)}, u32[]{:S(2)}, u32[]{:S(2)}) %all-to-all-start) | async-done | bytes 393248 | tf_op jit(solution)/shard_map/all_to_all | solution.py:279
  28.1 0.1 broadcast_in_dim.53.router_ref
  28.2 3.0 %collective-permute-start.2 = (bf16[256,256]{1,0:T(8,128)(2,1)S(1)}, bf16[256,256]{1,0:T(8,128)(2,1)S(1)}, u32[]{:S(2)}, u32[]{:S(2)}) collective-permute-start(bf16[256,256]{1,0:T(8,128)(2,1)S(1)} %slice.16.fill_ref), channel_id=1, source_target_pairs={{0,128},{64,192},{128,0},{192,64},{1,129},{65,193},{129,1},{193,65... | collective-permute-start | bytes 393224 | tf_op jit(solution)/shard_map/ppermute | solution.py:44
  31.2 0.8 %collective-permute-start.4 = (bf16[256,256]{1,0:T(8,128)(2,1)S(1)}, bf16[256,256]{1,0:T(8,128)(2,1)S(1)}, u32[]{:S(2)}, u32[]{:S(2)}) collective-permute-start(bf16[256,256]{1,0:T(8,128)(2,1)S(1)} %slice.16.fill_ref), channel_id=1, source_target_pairs={{0,192},{64,0},{128,64},{192,128},{1,193},{65,1},{129,65},{193,129... | collective-permute-start | bytes 393224 | tf_op jit(solution)/shard_map/ppermute | solution.py:44
  32.0 0.7 %collective-permute-start.1 = (bf16[256,256]{1,0:T(8,128)(2,1)S(1)}, bf16[256,256]{1,0:T(8,128)(2,1)S(1)}, u32[]{:S(2)}, u32[]{:S(2)}) collective-permute-start(bf16[256,256]{1,0:T(8,128)(2,1)S(1)} %slice.16.fill_ref), channel_id=1, source_target_pairs={{0,64},{64,128},{128,192},{192,0},{1,65},{65,129},{129,193},{193,1... | collective-permute-start | bytes 393224 | tf_op jit(solution)/shard_map/ppermute | solution.py:44
  32.7 0.4 collective-permute-start
  33.1 0.5 collective-permute-done.2
  33.6 2.2 %collective-permute-done.4 = bf16[256,256]{1,0:T(8,128)(2,1)S(1)} collective-permute-done((bf16[256,256]{1,0:T(8,128)(2,1)S(1)}, bf16[256,256]{1,0:T(8,128)(2,1)S(1)}, u32[]{:S(2)}, u32[]{:S(2)}) %collective-permute-start.4) | collective-permute-done | bytes 131104 | tf_op jit(solution)/shard_map/ppermute | solution.py:44
  35.8 0.1 collective-permute-start.5
  35.9 2.1 %collective-permute-done.1 = bf16[256,256]{1,0:T(8,128)(2,1)S(1)} collective-permute-done((bf16[256,256]{1,0:T(8,128)(2,1)S(1)}, bf16[256,256]{1,0:T(8,128)(2,1)S(1)}, u32[]{:S(2)}, u32[]{:S(2)}) %collective-permute-start.1) | collective-permute-done | bytes 131104 | tf_op jit(solution)/shard_map/ppermute | solution.py:44
  38.0 0.4 collective-permute-start.3
  38.4 1.2 %shard_map.56 = (f32[1024,128]{1,0:T(8,128)S(1)}, f32[1024,256]{1,0:T(8,128)S(1)}) custom-call(s32[68]{0:T(128)S(1)} %pad_add_fusion.table_ref, bf16[256,512]{1,0:T(8,128)(2,1)S(1)} %slice.17.q_ref, bf16[512,256]{1,0:T(8,128)(2,1)S(1)} %constant_dynamic-update-slice_fusion.lower_ref, bf16[512,256]{1,0:T(8,128)(2,1)S(1)} %constant_dynamic-update-slice_fusion.2.upper_ref), custom_call_target="tpu_custom_call" | custom-call | tf_op jit(solution)/shard_map/pallas_call | solution.py:219
  39.7 0.0 copy-start
  39.7 3.2 %collective-permute-start.10 = (bf16[512,256]{1,0:T(8,128)(2,1)S(1)}, bf16[512,256]{1,0:T(8,128)(2,1)S(1)}, u32[]{:S(2)}, u32[]{:S(2)}) collective-permute-start(bf16[512,256]{1,0:T(8,128)(2,1)S(1)} %constant_dynamic-update-slice_fusion.2.upper_ref), channel_id=1, source_target_pairs={{0,16},{16,0},{1,17},{17,1},{2,18},{18,2},{3,19},{19,3},{4,20},{20... | collective-permute-start | bytes 786440 | tf_op jit(solution)/shard_map/ppermute | solution.py:44
  43.0 0.1 collective-permute-start.9
  43.1 0.0 collective-permute-done.rest_2_
  43.1 0.0 collective-permute-done.5.rest_4_
  43.1 0.7 %collective-permute-done.3.rest_3_ = bf16[384,256]{1,0:T(8,128)(2,1)S(1)} collective-permute-done((bf16[384,256]{1,0:T(8,128)(2,1)S(1)}, bf16[384,256]{1,0:T(8,128)(2,1)S(1)}, u32[]{:S(2)}, u32[]{:S(2)}) %collective-permute-start.3) | collective-permute-done | bytes 196640 | tf_op jit(solution)/shard_map/ppermute | solution.py:51
  43.8 4.0 %collective-permute-start.7 = (bf16[384,256]{1,0:T(8,128)(2,1)S(1)}, bf16[384,256]{1,0:T(8,128)(2,1)S(1)}, u32[]{:S(2)}, u32[]{:S(2)}) collective-permute-start(bf16[384,256]{1,0:T(8,128)(2,1)S(1)} %collective-permute-done.3.rest_3_), channel_id=1, source_target_pairs={{0,16},{16,0},{1,17},{17,1},{2,18},{18,2},{3,19},{19,3},{4,20},{20... | collective-permute-start | bytes 589832 | tf_op jit(solution)/shard_map/ppermute | solution.py:44
  47.8 0.0 collective-permute-start.8
  47.8 0.5 collective-permute-start.6
  48.4 1.6 %shard_map.57 = (f32[1024,128]{1,0:T(8,128)S(1)}, f32[1024,256]{1,0:T(8,128)S(1)}) custom-call(s32[68]{0:T(128)S(1)} %pad_add_fusion.table_ref, bf16[256,512]{1,0:T(8,128)(2,1)S(1)} %slice.17.q_ref, bf16[256,256]{1,0:T(8,128)(2,1)S(1)} %slice.16.fill_ref, bf16[512,256]{1,0:T(8,128)(2,1)S(1)} %collective-permute-done.9.rest_0_, ...), custom_call_target="tpu_custom_call" | custom-call | flops 1000000 | bytes 10000 | tf_op jit(solution)/shard_map/pallas_call | solution.py:230
  50.0 2.1 %shard_map.58 = bf16[1024,512]{1,0:T(8,128)(2,1)} custom-call(s32[68]{0:T(128)S(1)} %pad_add_fusion.table_ref, bf16[256,512]{1,0:T(8,128)(2,1)S(1)} %slice.17.q_ref, bf16[256,256]{1,0:T(8,128)(2,1)S(1)} %slice.16.fill_ref, bf16[256,256]{1,0:T(8,128)(2,1)S(1)} %collective-permute-done.6.own_ref, bf16[384,256]{1,0:T(8,128)(2,1)S(1)} %collective-permute-done.7.lower_ref, ...), custom_call_target="tpu_custom_call" | custom-call | tf_op jit(solution)/shard_map/pallas_call | solution.py:242
  (20 shorter events, 0.2 us)
Async XLA Ops:
  1.7 26.4 %all-to-all-start = ((bf16[16,16,768]{2,1,0:T(8,128)(2,1)}), bf16[16,16,768]{2,1,0:T(8,128)(2,1)S(1)}, u32[]{:S(2)}, u32[]{:S(2)}) async-start(bf16[16,16,768]{2,1,0:T(8,128)(2,1)} %shard_map.55), calls=%async_computation | async-start | bytes 786432 | tf_op jit(solution)/shard_map/all_to_all | solution.py:279
  13.3 0.7 %copy-start.1 = (s32[16,256]{1,0:T(8,128)S(1)}, s32[16,256]{1,0:T(8,128)}, u32[]{:S(2)}) copy-start(s32[16,256]{1,0:T(8,128)} %kept_ref.1) | copy-start | bytes 49156
  13.3 0.7 %copy-start.2 = (bf16[1,256]{1,0:T(2,128)(2,1)S(1)}, bf16[1,256]{1,0:T(2,128)(2,1)}, u32[]{:S(2)}) copy-start(bf16[1,256]{1,0:T(2,128)(2,1)} %param.9) | copy-start | bytes 1540
  28.2 5.4 %collective-permute-start.2 = (bf16[256,256]{1,0:T(8,128)(2,1)S(1)}, bf16[256,256]{1,0:T(8,128)(2,1)S(1)}, u32[]{:S(2)}, u32[]{:S(2)}) collective-permute-start(bf16[256,256]{1,0:T(8,128)(2,1)S(1)} %slice.16.fill_ref), channel_id=1, source_target_pairs={{0,128},{64,192},{128,0},{192,64},{1,129},{65,193},{129,1},{193,65... | collective-permute-start | bytes 393224 | tf_op jit(solution)/shard_map/ppermute | solution.py:44
  31.2 4.6 %collective-permute-start.4 = (bf16[256,256]{1,0:T(8,128)(2,1)S(1)}, bf16[256,256]{1,0:T(8,128)(2,1)S(1)}, u32[]{:S(2)}, u32[]{:S(2)}) collective-permute-start(bf16[256,256]{1,0:T(8,128)(2,1)S(1)} %slice.16.fill_ref), channel_id=1, source_target_pairs={{0,192},{64,0},{128,64},{192,128},{1,193},{65,1},{129,65},{193,129... | collective-permute-start | bytes 393224 | tf_op jit(solution)/shard_map/ppermute | solution.py:44
  32.0 6.0 %collective-permute-start.1 = (bf16[256,256]{1,0:T(8,128)(2,1)S(1)}, bf16[256,256]{1,0:T(8,128)(2,1)S(1)}, u32[]{:S(2)}, u32[]{:S(2)}) collective-permute-start(bf16[256,256]{1,0:T(8,128)(2,1)S(1)} %slice.16.fill_ref), channel_id=1, source_target_pairs={{0,64},{64,128},{128,192},{192,0},{1,65},{65,129},{129,193},{193,1... | collective-permute-start | bytes 393224 | tf_op jit(solution)/shard_map/ppermute | solution.py:44
  32.7 10.4 %collective-permute-start = (bf16[256,256]{1,0:T(8,128)(2,1)S(1)}, bf16[256,256]{1,0:T(8,128)(2,1)S(1)}, u32[]{:S(2)}, u32[]{:S(2)}) collective-permute-start(bf16[256,256]{1,0:T(8,128)(2,1)S(1)} %slice.16.fill_ref), channel_id=1, source_target_pairs={{0,32},{32,1},{1,33},{33,0},{2,34},{34,3},{3,35},{35,2},{4,36},{36... | collective-permute-start | bytes 393224 | tf_op jit(solution)/shard_map/ppermute | solution.py:51
  35.8 7.2 %collective-permute-start.5 = (bf16[384,256]{1,0:T(8,128)(2,1)S(1)}, bf16[384,256]{1,0:T(8,128)(2,1)S(1)}, u32[]{:S(2)}, u32[]{:S(2)}) collective-permute-start(bf16[384,256]{1,0:T(8,128)(2,1)S(1)} %pad_maximum_fusion.1), channel_id=1, source_target_pairs={{0,33},{32,0},{1,32},{33,1},{2,35},{34,2},{3,34},{35,3},{4,37},{36... | collective-permute-start | bytes 589832 | tf_op jit(solution)/shard_map/ppermute | solution.py:51
  38.0 5.8 %collective-permute-start.3 = (bf16[384,256]{1,0:T(8,128)(2,1)S(1)}, bf16[384,256]{1,0:T(8,128)(2,1)S(1)}, u32[]{:S(2)}, u32[]{:S(2)}) collective-permute-start(bf16[384,256]{1,0:T(8,128)(2,1)S(1)} %pad_maximum_fusion), channel_id=1, source_target_pairs={{0,32},{32,1},{1,33},{33,0},{2,34},{34,3},{3,35},{35,2},{4,36},{36... | collective-permute-start | bytes 589832 | tf_op jit(solution)/shard_map/ppermute | solution.py:51
  39.7 10.3 %copy-start = (bf16[1024,512]{1,0:T(8,128)(2,1)S(1)}, bf16[1024,512]{1,0:T(8,128)(2,1)}, u32[]{:S(2)}) copy-start(bf16[1024,512]{1,0:T(8,128)(2,1)} %residual_ref.1) | copy-start | bytes 3145732
  39.7 8.6 %collective-permute-start.10 = (bf16[512,256]{1,0:T(8,128)(2,1)S(1)}, bf16[512,256]{1,0:T(8,128)(2,1)S(1)}, u32[]{:S(2)}, u32[]{:S(2)}) collective-permute-start(bf16[512,256]{1,0:T(8,128)(2,1)S(1)} %constant_dynamic-update-slice_fusion.2.upper_ref), channel_id=1, source_target_pairs={{0,16},{16,0},{1,17},{17,1},{2,18},{18,2},{3,19},{19,3},{4,20},{20... | collective-permute-start | bytes 786440 | tf_op jit(solution)/shard_map/ppermute | solution.py:44
  43.0 5.4 %collective-permute-start.9 = (bf16[512,256]{1,0:T(8,128)(2,1)S(1)}, bf16[512,256]{1,0:T(8,128)(2,1)S(1)}, u32[]{:S(2)}, u32[]{:S(2)}) collective-permute-start(bf16[512,256]{1,0:T(8,128)(2,1)S(1)} %constant_dynamic-update-slice_fusion.lower_ref), channel_id=1, source_target_pairs={{0,16},{16,0},{1,17},{17,1},{2,18},{18,2},{3,19},{19,3},{4,20},{20... | collective-permute-start | bytes 786440 | tf_op jit(solution)/shard_map/ppermute | solution.py:44
  43.8 6.2 %collective-permute-start.7 = (bf16[384,256]{1,0:T(8,128)(2,1)S(1)}, bf16[384,256]{1,0:T(8,128)(2,1)S(1)}, u32[]{:S(2)}, u32[]{:S(2)}) collective-permute-start(bf16[384,256]{1,0:T(8,128)(2,1)S(1)} %collective-permute-done.3.rest_3_), channel_id=1, source_target_pairs={{0,16},{16,0},{1,17},{17,1},{2,18},{18,2},{3,19},{19,3},{4,20},{20... | collective-permute-start | bytes 589832 | tf_op jit(solution)/shard_map/ppermute | solution.py:44
  47.8 2.2 %collective-permute-start.8 = (bf16[384,256]{1,0:T(8,128)(2,1)S(1)}, bf16[384,256]{1,0:T(8,128)(2,1)S(1)}, u32[]{:S(2)}, u32[]{:S(2)}) collective-permute-start(bf16[384,256]{1,0:T(8,128)(2,1)S(1)} %collective-permute-done.5.rest_4_), channel_id=1, source_target_pairs={{0,16},{16,0},{1,17},{17,1},{2,18},{18,2},{3,19},{19,3},{4,20},{20... | collective-permute-start | bytes 589832 | tf_op jit(solution)/shard_map/ppermute | solution.py:44
  47.8 2.1 %collective-permute-start.6 = (bf16[256,256]{1,0:T(8,128)(2,1)S(1)}, bf16[256,256]{1,0:T(8,128)(2,1)S(1)}, u32[]{:S(2)}, u32[]{:S(2)}) collective-permute-start(bf16[256,256]{1,0:T(8,128)(2,1)S(1)} %collective-permute-done.rest_2_), channel_id=1, source_target_pairs={{0,16},{16,0},{1,17},{17,1},{2,18},{18,2},{3,19},{19,3},{4,20},{20... | collective-permute-start | bytes 393224 | tf_op jit(solution)/shard_map/ppermute | solution.py:44

commit v6 on v5

--- a/solution.py
+++ b/solution.py
@@ -94,6 +94,8 @@
         @pl.when(tiles == count)
         def _():
             if count == 0:
+                if old is new:
+                    return
                 top_new[...] = top_old[...]
                 sum_new[...] = sum_old[...]
                 return
@@ -139,12 +141,13 @@
     absorb(tiles, q_ref, k_buf, v_buf, state, (top_ref, sum_ref))
 
 
-def last_kernel(table_ref, q_ref, fill_ref, own_ref, lower_ref, upper_ref, top0, sum0, kept_ref, router_ref, residual_ref, out_ref, k_buf, v_buf, top_ref, sum_ref, residual_buf, out_buf, sems):
+def last_kernel(table_ref, q_ref, fill_ref, own_ref, lower_ref, upper_ref, top0, sum0, kept_ref, router_ref, residual_ref, out_ref, top_ref, sum_ref, k_buf, v_buf, residual_buf, out_buf, sems):
     fetch = pltpu.make_async_copy(residual_ref, residual_buf, sems.at[4])
     fetch.start()
     pieces = pieces_of(own_ref, lower_ref, upper_ref)
     tiles = compact(pieces, 2, table_ref, fill_ref, k_buf, v_buf)
-    absorb(tiles, q_ref, k_buf, v_buf, (top0, sum0), (top_ref, sum_ref))
+    state = (top_ref, sum_ref)
+    absorb(tiles, q_ref, k_buf, v_buf, state, state)
     updates = []
     for head in range(HEADS):
         now = slice(head * CAP, (head + 1) * CAP)
@@ -241,15 +244,15 @@
 def last_part(table, query_rows, fill, blocks, state, kept_local, router, residual):
     return pl.pallas_call(
         last_kernel,
-        out_shape=jax.ShapeDtypeStruct((TOK_DEV, HEADS * HD), BF),
+        out_shape=[jax.ShapeDtypeStruct((TOK_DEV, HEADS * HD), BF), *STATE],
         in_specs=[SMEM] + [VMEM] * 9 + [ANY],
-        out_specs=ANY,
+        out_specs=[ANY, VMEM, VMEM],
+        input_output_aliases={3 + len(blocks): 1, 4 + len(blocks): 2},
         scratch_shapes=buffers(PIECES)
-        + [pltpu.VMEM(s.shape, s.dtype) for s in STATE]
         + [pltpu.VMEM((TOK_DEV, HEADS * HD), BF)] * 2
         + [pltpu.SemaphoreType.DMA((5,))],
         compiler_params=params(16),
-    )(table, query_rows, fill, *blocks, *state, kept_local, router, residual)
+    )(table, query_rows, fill, *blocks, *state, kept_local, router, residual)[0]
 
 
 def tables(kept_local, y, xl, co):

time: 52.6 us -> 53.3 us (1.013); the launches traced: 52.4 us -> 52.4 us
  starting transfers between devices: 24.8 us -> 25.5 us
  waiting for transfers between devices: 19.2 us -> 18.6 us
    ppermute x3, starting transfers between devices: 0.86 us -> 3.14 us  [shift_x(): lax.ppermute(block, ('xl', 'xh'), [(at(x), at((x + distance) % 4)) for x...]
    ppermute x8, starting transfers between devices: 12.4 us -> 10.8 us  [shift(): lax.ppermute(block, axis, [(i, (i + distance) % size) for i in range(size)])]
    ppermute x3, waiting for transfers between devices: 0.75 us -> 0.01 us  [shift_x(): lax.ppermute(block, ('xl', 'xh'), [(at(x), at((x + distance) % 4)) for x...]
  transfers between devices with their start and end apart: 12 -> 12, of which waited for: 5 -> 3; matrix products, arithmetic and copies ran while one was open for 1% -> 1% of each run, Pallas kernels for 5% -> 5%
where the time goes in v6:
time: 53.3 us; the launch traced here: 52.4 us
  starting transfers between devices  25.5 us (48%)
  waiting for transfers between devices  18.6 us (35%)
  Pallas kernels  6.62 us (12%)
  local copies, waits for them, and re-layouts  0.85 us (2%)
    all_to_all x1, waiting for transfers between devices, shards(): sent = lax.all_to_all(sent, TP, split_axis=0, concat_axis=0, tiled=True)  13.6 us
    all_to_all x1, starting transfers between devices, shards(): sent = lax.all_to_all(sent, TP, split_axis=0, concat_axis=0, tiled=True)  11.6 us
    ppermute x8, starting transfers between devices, shift(): lax.ppermute(block, axis, [(i, (i + distance) % size) for i in range(size)])  10.8 us
    ppermute x8, waiting for transfers between devices, shift(): lax.ppermute(block, axis, [(i, (i + distance) % size) for i in range(size)])  4.92 us
    ppermute x3, starting transfers between devices, shift_x(): lax.ppermute(block, ('xl', 'xh'), [(at(x), at((x + distance) % 4)) for x...  3.14 us
    pallas_call x1, Pallas kernels, last_part(): pl.pallas_call(last_kernel, out_shape=[jax.ShapeDtypeStruct((TOK_DEV, HEA...  2.05 us
    pallas_call x1, Pallas kernels, sorted_part(): pl.pallas_call(sorted_kernel, out_shape=jax.ShapeDtypeStruct(shape, BF),...  1.69 us
    pallas_call x1, Pallas kernels, more_part(): pl.pallas_call(more_kernel, out_shape=STATE, in_specs=[SMEM] + [VMEM] * (...  1.63 us
  transfers between devices with their start and end apart: 12, of which 3 were waited for; matrix products, arithmetic and copies ran while one was open for 1% of the time, Pallas kernels for 5%

profile of v6, /device:TPU:1, one launch (start us, length us, event | category | flops | bytes accessed | tf_op | source)
XLA Modules:
  0.0 52.4 jit_solution(9556040532332880758)
XLA Ops:
  0.0 1.7 %shard_map.55 = bf16[16,16,768]{2,1,0:T(8,128)(2,1)} custom-call(bf16[1,16,8192]{2,1,0:T(8,128)(2,1)} %queries_ref.1, bf16[1,16,2048]{2,1,0:T(8,128)(2,1)} %pairs_ref.1), custom_call_target="tpu_custom_call" | custom-call | tf_op jit(solution)/shard_map/pallas_call | solution.py:205
  1.7 11.6 %all-to-all-start = ((bf16[16,16,768]{2,1,0:T(8,128)(2,1)}), bf16[16,16,768]{2,1,0:T(8,128)(2,1)S(1)}, u32[]{:S(2)}, u32[]{:S(2)}) async-start(bf16[16,16,768]{2,1,0:T(8,128)(2,1)} %shard_map.55), calls=%async_computation | async-start | bytes 786432 | tf_op jit(solution)/shard_map/all_to_all | solution.py:282
  13.3 0.0 copy-start.1
  13.3 0.0 copy-start.2
  13.4 0.7 %copy-done.2 = bf16[1,256]{1,0:T(2,128)(2,1)S(1)} copy-done((bf16[1,256]{1,0:T(2,128)(2,1)S(1)}, bf16[1,256]{1,0:T(2,128)(2,1)}, u32[]{:S(2)}) %copy-start.2) | copy-done | bytes 536
  14.0 0.1 convert_reduce_fusion
  14.2 0.1 select_reduce_fusion.1
  14.3 0.1 select_reduce_fusion
  14.4 0.1 pad_add_fusion.table_ref
  14.5 13.6 %all-to-all-done = bf16[16,16,768]{2,1,0:T(8,128)(2,1)S(1)} async-done(((bf16[16,16,768]{2,1,0:T(8,128)(2,1)}), bf16[16,16,768]{2,1,0:T(8,128)(2,1)S(1)}, u32[]{:S(2)}, u32[]{:S(2)}) %all-to-all-start) | async-done | bytes 393248 | tf_op jit(solution)/shard_map/all_to_all | solution.py:282
  28.1 0.1 broadcast_in_dim.53.router_ref
  28.2 3.0 %collective-permute-start.2 = (bf16[256,256]{1,0:T(8,128)(2,1)S(1)}, bf16[256,256]{1,0:T(8,128)(2,1)S(1)}, u32[]{:S(2)}, u32[]{:S(2)}) collective-permute-start(bf16[256,256]{1,0:T(8,128)(2,1)S(1)} %slice.16.fill_ref), channel_id=1, source_target_pairs={{0,128},{64,192},{128,0},{192,64},{1,129},{65,193},{129,1},{193,65... | collective-permute-start | bytes 393224 | tf_op jit(solution)/shard_map/ppermute | solution.py:44
  31.2 0.9 %collective-permute-start.4 = (bf16[256,256]{1,0:T(8,128)(2,1)S(1)}, bf16[256,256]{1,0:T(8,128)(2,1)S(1)}, u32[]{:S(2)}, u32[]{:S(2)}) collective-permute-start(bf16[256,256]{1,0:T(8,128)(2,1)S(1)} %slice.16.fill_ref), channel_id=1, source_target_pairs={{0,192},{64,0},{128,64},{192,128},{1,193},{65,1},{129,65},{193,129... | collective-permute-start | bytes 393224 | tf_op jit(solution)/shard_map/ppermute | solution.py:44
  32.1 0.7 %collective-permute-start.1 = (bf16[256,256]{1,0:T(8,128)(2,1)S(1)}, bf16[256,256]{1,0:T(8,128)(2,1)S(1)}, u32[]{:S(2)}, u32[]{:S(2)}) collective-permute-start(bf16[256,256]{1,0:T(8,128)(2,1)S(1)} %slice.16.fill_ref), channel_id=1, source_target_pairs={{0,64},{64,128},{128,192},{192,0},{1,65},{65,129},{129,193},{193,1... | collective-permute-start | bytes 393224 | tf_op jit(solution)/shard_map/ppermute | solution.py:44
  32.8 0.3 collective-permute-start
  33.1 0.5 collective-permute-done.2
  33.6 4.4 %collective-permute-done.1 = bf16[256,256]{1,0:T(8,128)(2,1)S(1)} collective-permute-done((bf16[256,256]{1,0:T(8,128)(2,1)S(1)}, bf16[256,256]{1,0:T(8,128)(2,1)S(1)}, u32[]{:S(2)}, u32[]{:S(2)}) %collective-permute-start.1) | collective-permute-done | bytes 131104 | tf_op jit(solution)/shard_map/ppermute | solution.py:44
  38.0 0.4 collective-permute-start.3
  38.4 0.0 collective-permute-done.4
  38.5 2.4 %collective-permute-start.5 = (bf16[384,256]{1,0:T(8,128)(2,1)S(1)}, bf16[384,256]{1,0:T(8,128)(2,1)S(1)}, u32[]{:S(2)}, u32[]{:S(2)}) collective-permute-start(bf16[384,256]{1,0:T(8,128)(2,1)S(1)} %pad_maximum_fusion.1), channel_id=1, source_target_pairs={{0,33},{32,0},{1,32},{33,1},{2,35},{34,2},{3,34},{35,3},{4,37},{36... | collective-permute-start | bytes 589832 | tf_op jit(solution)/shard_map/ppermute | solution.py:51
  40.9 1.2 %shard_map.56 = (f32[1024,128]{1,0:T(8,128)S(1)}, f32[1024,256]{1,0:T(8,128)S(1)}) custom-call(s32[68]{0:T(128)S(1)} %pad_add_fusion.table_ref, bf16[256,512]{1,0:T(8,128)(2,1)S(1)} %slice.17.q_ref, bf16[512,256]{1,0:T(8,128)(2,1)S(1)} %constant_dynamic-update-slice_fusion.lower_ref, bf16[512,256]{1,0:T(8,128)(2,1)S(1)} %constant_dynamic-update-slice_fusion.2.upper_ref), custom_call_target="tpu_custom_call" | custom-call | tf_op jit(solution)/shard_map/pallas_call | solution.py:222
  42.2 0.0 copy-start
  42.2 3.6 %collective-permute-start.9 = (bf16[512,256]{1,0:T(8,128)(2,1)S(1)}, bf16[512,256]{1,0:T(8,128)(2,1)S(1)}, u32[]{:S(2)}, u32[]{:S(2)}) collective-permute-start(bf16[512,256]{1,0:T(8,128)(2,1)S(1)} %constant_dynamic-update-slice_fusion.lower_ref), channel_id=1, source_target_pairs={{0,16},{16,0},{1,17},{17,1},{2,18},{18,2},{3,19},{19,3},{4,20},{20... | collective-permute-start | bytes 786440 | tf_op jit(solution)/shard_map/ppermute | solution.py:44
  45.8 0.1 collective-permute-start.10
  45.9 0.0 collective-permute-done.3.rest_3_
  45.9 0.0 collective-permute-done.5.rest_4_
  45.9 2.0 %collective-permute-start.7 = (bf16[384,256]{1,0:T(8,128)(2,1)S(1)}, bf16[384,256]{1,0:T(8,128)(2,1)S(1)}, u32[]{:S(2)}, u32[]{:S(2)}) collective-permute-start(bf16[384,256]{1,0:T(8,128)(2,1)S(1)} %collective-permute-done.3.rest_3_), channel_id=1, source_target_pairs={{0,16},{16,0},{1,17},{17,1},{2,18},{18,2},{3,19},{19,3},{4,20},{20... | collective-permute-start | bytes 589832 | tf_op jit(solution)/shard_map/ppermute | solution.py:44
  47.9 0.0 collective-permute-start.8
  48.0 0.5 collective-permute-start.6
  48.5 0.0 collective-permute-done.9.rest_0_
  48.5 1.6 %shard_map.57 = (f32[1024,128]{1,0:T(8,128)S(1)}, f32[1024,256]{1,0:T(8,128)S(1)}) custom-call(s32[68]{0:T(128)S(1)} %pad_add_fusion.table_ref, bf16[256,512]{1,0:T(8,128)(2,1)S(1)} %slice.17.q_ref, bf16[256,256]{1,0:T(8,128)(2,1)S(1)} %slice.16.fill_ref, bf16[512,256]{1,0:T(8,128)(2,1)S(1)} %collective-permute-done.9.rest_0_, ...), custom_call_target="tpu_custom_call" | custom-call | flops 1000000 | bytes 10000 | tf_op jit(solution)/shard_map/pallas_call | solution.py:233
  50.1 2.0 %shard_map.58 = (bf16[1024,512]{1,0:T(8,128)(2,1)}, f32[1024,128]{1,0:T(8,128)S(1)}, f32[1024,256]{1,0:T(8,128)S(1)}) custom-call(s32[68]{0:T(128)S(1)} %pad_add_fusion.table_ref, bf16[256,512]{1,0:T(8,128)(2,1)S(1)} %slice.17.q_ref, bf16[256,256]{1,0:T(8,128)(2,1)S(1)} %slice.16.fill_ref, ...), custom_call_target="tpu_custom_call", output_to_operand_aliasing={{1}: (6, {}), {2}: (7, {})} | custom-call | tf_op jit(solution)/shard_map/pallas_call | solution.py:245
  (20 shorter events, 0.2 us)
Async XLA Ops:
  1.7 26.4 %all-to-all-start = ((bf16[16,16,768]{2,1,0:T(8,128)(2,1)}), bf16[16,16,768]{2,1,0:T(8,128)(2,1)S(1)}, u32[]{:S(2)}, u32[]{:S(2)}) async-start(bf16[16,16,768]{2,1,0:T(8,128)(2,1)} %shard_map.55), calls=%async_computation | async-start | bytes 786432 | tf_op jit(solution)/shard_map/all_to_all | solution.py:282
  13.3 0.7 %copy-start.1 = (s32[16,256]{1,0:T(8,128)S(1)}, s32[16,256]{1,0:T(8,128)}, u32[]{:S(2)}) copy-start(s32[16,256]{1,0:T(8,128)} %kept_ref.1) | copy-start | bytes 49156
  13.3 0.7 %copy-start.2 = (bf16[1,256]{1,0:T(2,128)(2,1)S(1)}, bf16[1,256]{1,0:T(2,128)(2,1)}, u32[]{:S(2)}) copy-start(bf16[1,256]{1,0:T(2,128)(2,1)} %param.9) | copy-start | bytes 1540
  28.2 5.4 %collective-permute-start.2 = (bf16[256,256]{1,0:T(8,128)(2,1)S(1)}, bf16[256,256]{1,0:T(8,128)(2,1)S(1)}, u32[]{:S(2)}, u32[]{:S(2)}) collective-permute-start(bf16[256,256]{1,0:T(8,128)(2,1)S(1)} %slice.16.fill_ref), channel_id=1, source_target_pairs={{0,128},{64,192},{128,0},{192,64},{1,129},{65,193},{129,1},{193,65... | collective-permute-start | bytes 393224 | tf_op jit(solution)/shard_map/ppermute | solution.py:44
  31.2 7.2 %collective-permute-start.4 = (bf16[256,256]{1,0:T(8,128)(2,1)S(1)}, bf16[256,256]{1,0:T(8,128)(2,1)S(1)}, u32[]{:S(2)}, u32[]{:S(2)}) collective-permute-start(bf16[256,256]{1,0:T(8,128)(2,1)S(1)} %slice.16.fill_ref), channel_id=1, source_target_pairs={{0,192},{64,0},{128,64},{192,128},{1,193},{65,1},{129,65},{193,129... | collective-permute-start | bytes 393224 | tf_op jit(solution)/shard_map/ppermute | solution.py:44
  32.1 5.9 %collective-permute-start.1 = (bf16[256,256]{1,0:T(8,128)(2,1)S(1)}, bf16[256,256]{1,0:T(8,128)(2,1)S(1)}, u32[]{:S(2)}, u32[]{:S(2)}) collective-permute-start(bf16[256,256]{1,0:T(8,128)(2,1)S(1)} %slice.16.fill_ref), channel_id=1, source_target_pairs={{0,64},{64,128},{128,192},{192,0},{1,65},{65,129},{129,193},{193,1... | collective-permute-start | bytes 393224 | tf_op jit(solution)/shard_map/ppermute | solution.py:44
  32.8 13.1 %collective-permute-start = (bf16[256,256]{1,0:T(8,128)(2,1)S(1)}, bf16[256,256]{1,0:T(8,128)(2,1)S(1)}, u32[]{:S(2)}, u32[]{:S(2)}) collective-permute-start(bf16[256,256]{1,0:T(8,128)(2,1)S(1)} %slice.16.fill_ref), channel_id=1, source_target_pairs={{0,32},{32,1},{1,33},{33,0},{2,34},{34,3},{3,35},{35,2},{4,36},{36... | collective-permute-start | bytes 393224 | tf_op jit(solution)/shard_map/ppermute | solution.py:51
  38.0 7.9 %collective-permute-start.3 = (bf16[384,256]{1,0:T(8,128)(2,1)S(1)}, bf16[384,256]{1,0:T(8,128)(2,1)S(1)}, u32[]{:S(2)}, u32[]{:S(2)}) collective-permute-start(bf16[384,256]{1,0:T(8,128)(2,1)S(1)} %pad_maximum_fusion), channel_id=1, source_target_pairs={{0,32},{32,1},{1,33},{33,0},{2,34},{34,3},{3,35},{35,2},{4,36},{36... | collective-permute-start | bytes 589832 | tf_op jit(solution)/shard_map/ppermute | solution.py:51
  38.5 7.5 %collective-permute-start.5 = (bf16[384,256]{1,0:T(8,128)(2,1)S(1)}, bf16[384,256]{1,0:T(8,128)(2,1)S(1)}, u32[]{:S(2)}, u32[]{:S(2)}) collective-permute-start(bf16[384,256]{1,0:T(8,128)(2,1)S(1)} %pad_maximum_fusion.1), channel_id=1, source_target_pairs={{0,33},{32,0},{1,32},{33,1},{2,35},{34,2},{3,34},{35,3},{4,37},{36... | collective-permute-start | bytes 589832 | tf_op jit(solution)/shard_map/ppermute | solution.py:51
  42.2 7.9 %copy-start = (bf16[1024,512]{1,0:T(8,128)(2,1)S(1)}, bf16[1024,512]{1,0:T(8,128)(2,1)}, u32[]{:S(2)}) copy-start(bf16[1024,512]{1,0:T(8,128)(2,1)} %residual_ref.1) | copy-start | bytes 3145732
  42.2 6.2 %collective-permute-start.9 = (bf16[512,256]{1,0:T(8,128)(2,1)S(1)}, bf16[512,256]{1,0:T(8,128)(2,1)S(1)}, u32[]{:S(2)}, u32[]{:S(2)}) collective-permute-start(bf16[512,256]{1,0:T(8,128)(2,1)S(1)} %constant_dynamic-update-slice_fusion.lower_ref), channel_id=1, source_target_pairs={{0,16},{16,0},{1,17},{17,1},{2,18},{18,2},{3,19},{19,3},{4,20},{20... | collective-permute-start | bytes 786440 | tf_op jit(solution)/shard_map/ppermute | solution.py:44
  45.8 2.7 %collective-permute-start.10 = (bf16[512,256]{1,0:T(8,128)(2,1)S(1)}, bf16[512,256]{1,0:T(8,128)(2,1)S(1)}, u32[]{:S(2)}, u32[]{:S(2)}) collective-permute-start(bf16[512,256]{1,0:T(8,128)(2,1)S(1)} %constant_dynamic-update-slice_fusion.2.upper_ref), channel_id=1, source_target_pairs={{0,16},{16,0},{1,17},{17,1},{2,18},{18,2},{3,19},{19,3},{4,20},{20... | collective-permute-start | bytes 786440 | tf_op jit(solution)/shard_map/ppermute | solution.py:44
  45.9 4.2 %collective-permute-start.7 = (bf16[384,256]{1,0:T(8,128)(2,1)S(1)}, bf16[384,256]{1,0:T(8,128)(2,1)S(1)}, u32[]{:S(2)}, u32[]{:S(2)}) collective-permute-start(bf16[384,256]{1,0:T(8,128)(2,1)S(1)} %collective-permute-done.3.rest_3_), channel_id=1, source_target_pairs={{0,16},{16,0},{1,17},{17,1},{2,18},{18,2},{3,19},{19,3},{4,20},{20... | collective-permute-start | bytes 589832 | tf_op jit(solution)/shard_map/ppermute | solution.py:44
  47.9 2.2 %collective-permute-start.8 = (bf16[384,256]{1,0:T(8,128)(2,1)S(1)}, bf16[384,256]{1,0:T(8,128)(2,1)S(1)}, u32[]{:S(2)}, u32[]{:S(2)}) collective-permute-start(bf16[384,256]{1,0:T(8,128)(2,1)S(1)} %collective-permute-done.5.rest_4_), channel_id=1, source_target_pairs={{0,16},{16,0},{1,17},{17,1},{2,18},{18,2},{3,19},{19,3},{4,20},{20... | collective-permute-start | bytes 589832 | tf_op jit(solution)/shard_map/ppermute | solution.py:44
  48.0 2.2 %collective-permute-start.6 = (bf16[256,256]{1,0:T(8,128)(2,1)S(1)}, bf16[256,256]{1,0:T(8,128)(2,1)S(1)}, u32[]{:S(2)}, u32[]{:S(2)}) collective-permute-start(bf16[256,256]{1,0:T(8,128)(2,1)S(1)} %collective-permute-done.rest_2_), channel_id=1, source_target_pairs={{0,16},{16,0},{1,17},{17,1},{2,18},{18,2},{3,19},{19,3},{4,20},{20... | collective-permute-start | bytes 393224 | tf_op jit(solution)/shard_map/ppermute | solution.py:44

commit v7 on v5

--- a/solution.py
+++ b/solution.py
@@ -140,7 +140,7 @@
 
 
 def last_kernel(table_ref, q_ref, fill_ref, own_ref, lower_ref, upper_ref, top0, sum0, kept_ref, router_ref, residual_ref, out_ref, k_buf, v_buf, top_ref, sum_ref, residual_buf, out_buf, sems):
-    fetch = pltpu.make_async_copy(residual_ref, residual_buf, sems.at[4])
+    fetch = pltpu.make_async_copy(residual_ref, residual_buf, sems.at[8])
     fetch.start()
     pieces = pieces_of(own_ref, lower_ref, upper_ref)
     tiles = compact(pieces, 2, table_ref, fill_ref, k_buf, v_buf)
@@ -154,9 +154,9 @@
     kept = kept_ref[pl.ds(table_ref[2 * PIECES_ALL + 3], 1), :]
     fetch.wait()
     copies = []
-    for part, row in enumerate(range(0, TOK_DEV, CAP)):
-        now = slice(row, row + CAP)
-        place = lax.broadcasted_iota(jnp.int32, (CAP, CAP), 0) + row
+    for part, row in enumerate(range(0, TOK_DEV, HALF)):
+        now = slice(row, row + HALF)
+        place = lax.broadcasted_iota(jnp.int32, (HALF, CAP), 0) + row
         chosen = jnp.where(place == kept, 1.0, 0.0).astype(BF)
         added = jnp.dot(chosen, update, preferred_element_type=F32)
         out_buf[now, :] = (residual_buf[now, :].astype(F32) + added).astype(BF)
@@ -247,7 +247,7 @@
         scratch_shapes=buffers(PIECES)
         + [pltpu.VMEM(s.shape, s.dtype) for s in STATE]
         + [pltpu.VMEM((TOK_DEV, HEADS * HD), BF)] * 2
-        + [pltpu.SemaphoreType.DMA((5,))],
+        + [pltpu.SemaphoreType.DMA((9,))],
         compiler_params=params(16),
     )(table, query_rows, fill, *blocks, *state, kept_local, router, residual)
 

time: 52.6 us -> 52.6 us (level)
  no operation moved by 1% of the time
where the time goes in v7:
time: 52.6 us; the launch traced here: 52.3 us
  starting transfers between devices  24.8 us (47%)
  waiting for transfers between devices  19.2 us (37%)
  Pallas kernels  6.68 us (13%)
  local copies, waits for them, and re-layouts  0.85 us (2%)
    all_to_all x1, waiting for transfers between devices, shards(): sent = lax.all_to_all(sent, TP, split_axis=0, concat_axis=0, tiled=True)  13.6 us
    ppermute x8, starting transfers between devices, shift(): lax.ppermute(block, axis, [(i, (i + distance) % size) for i in range(size)])  12.4 us
    all_to_all x1, starting transfers between devices, shards(): sent = lax.all_to_all(sent, TP, split_axis=0, concat_axis=0, tiled=True)  11.6 us
    ppermute x8, waiting for transfers between devices, shift(): lax.ppermute(block, axis, [(i, (i + distance) % size) for i in range(size)])  4.77 us
    pallas_call x1, Pallas kernels, last_part(): pl.pallas_call(last_kernel, out_shape=jax.ShapeDtypeStruct((TOK_DEV, HEAD...  2.15 us
    pallas_call x1, Pallas kernels, sorted_part(): pl.pallas_call(sorted_kernel, out_shape=jax.ShapeDtypeStruct(shape, BF),...  1.69 us
    pallas_call x1, Pallas kernels, more_part(): pl.pallas_call(more_kernel, out_shape=STATE, in_specs=[SMEM] + [VMEM] * (...  1.6 us
    pallas_call x1, Pallas kernels, own_part(): pl.pallas_call(own_kernel, out_shape=STATE, in_specs=[SMEM] + [VMEM] * 3,...  1.24 us
  transfers between devices with their start and end apart: 12, of which 5 were waited for; matrix products, arithmetic and copies ran while one was open for 1% of the time, Pallas kernels for 5%

profile of v7, /device:TPU:1, one launch (start us, length us, event | category | flops | bytes accessed | tf_op | source)
XLA Modules:
  0.0 52.3 jit_solution(5808783975852330093)
XLA Ops:
  0.0 1.7 %shard_map.55 = bf16[16,16,768]{2,1,0:T(8,128)(2,1)} custom-call(bf16[1,16,8192]{2,1,0:T(8,128)(2,1)} %queries_ref.1, bf16[1,16,2048]{2,1,0:T(8,128)(2,1)} %pairs_ref.1), custom_call_target="tpu_custom_call" | custom-call | tf_op jit(solution)/shard_map/pallas_call | solution.py:202
  1.7 11.6 %all-to-all-start = ((bf16[16,16,768]{2,1,0:T(8,128)(2,1)}), bf16[16,16,768]{2,1,0:T(8,128)(2,1)S(1)}, u32[]{:S(2)}, u32[]{:S(2)}) async-start(bf16[16,16,768]{2,1,0:T(8,128)(2,1)} %shard_map.55), calls=%async_computation | async-start | bytes 786432 | tf_op jit(solution)/shard_map/all_to_all | solution.py:279
  13.3 0.0 copy-start.1
  13.3 0.0 copy-start.2
  13.4 0.7 %copy-done.2 = bf16[1,256]{1,0:T(2,128)(2,1)S(1)} copy-done((bf16[1,256]{1,0:T(2,128)(2,1)S(1)}, bf16[1,256]{1,0:T(2,128)(2,1)}, u32[]{:S(2)}) %copy-start.2) | copy-done | bytes 536
  14.0 0.1 convert_reduce_fusion
  14.2 0.1 select_reduce_fusion.1
  14.3 0.1 select_reduce_fusion
  14.4 0.1 pad_add_fusion.table_ref
  14.5 13.6 %all-to-all-done = bf16[16,16,768]{2,1,0:T(8,128)(2,1)S(1)} async-done(((bf16[16,16,768]{2,1,0:T(8,128)(2,1)}), bf16[16,16,768]{2,1,0:T(8,128)(2,1)S(1)}, u32[]{:S(2)}, u32[]{:S(2)}) %all-to-all-start) | async-done | bytes 393248 | tf_op jit(solution)/shard_map/all_to_all | solution.py:279
  28.1 0.1 broadcast_in_dim.53.router_ref
  28.2 3.0 %collective-permute-start.2 = (bf16[256,256]{1,0:T(8,128)(2,1)S(1)}, bf16[256,256]{1,0:T(8,128)(2,1)S(1)}, u32[]{:S(2)}, u32[]{:S(2)}) collective-permute-start(bf16[256,256]{1,0:T(8,128)(2,1)S(1)} %slice.16.fill_ref), channel_id=1, source_target_pairs={{0,128},{64,192},{128,0},{192,64},{1,129},{65,193},{129,1},{193,65... | collective-permute-start | bytes 393224 | tf_op jit(solution)/shard_map/ppermute | solution.py:44
  31.2 0.8 %collective-permute-start.4 = (bf16[256,256]{1,0:T(8,128)(2,1)S(1)}, bf16[256,256]{1,0:T(8,128)(2,1)S(1)}, u32[]{:S(2)}, u32[]{:S(2)}) collective-permute-start(bf16[256,256]{1,0:T(8,128)(2,1)S(1)} %slice.16.fill_ref), channel_id=1, source_target_pairs={{0,192},{64,0},{128,64},{192,128},{1,193},{65,1},{129,65},{193,129... | collective-permute-start | bytes 393224 | tf_op jit(solution)/shard_map/ppermute | solution.py:44
  32.0 0.7 %collective-permute-start.1 = (bf16[256,256]{1,0:T(8,128)(2,1)S(1)}, bf16[256,256]{1,0:T(8,128)(2,1)S(1)}, u32[]{:S(2)}, u32[]{:S(2)}) collective-permute-start(bf16[256,256]{1,0:T(8,128)(2,1)S(1)} %slice.16.fill_ref), channel_id=1, source_target_pairs={{0,64},{64,128},{128,192},{192,0},{1,65},{65,129},{129,193},{193,1... | collective-permute-start | bytes 393224 | tf_op jit(solution)/shard_map/ppermute | solution.py:44
  32.7 0.4 collective-permute-start
  33.1 0.5 collective-permute-done.2
  33.6 2.2 %collective-permute-done.4 = bf16[256,256]{1,0:T(8,128)(2,1)S(1)} collective-permute-done((bf16[256,256]{1,0:T(8,128)(2,1)S(1)}, bf16[256,256]{1,0:T(8,128)(2,1)S(1)}, u32[]{:S(2)}, u32[]{:S(2)}) %collective-permute-start.4) | collective-permute-done | bytes 131104 | tf_op jit(solution)/shard_map/ppermute | solution.py:44
  35.8 0.1 collective-permute-start.5
  35.9 2.1 %collective-permute-done.1 = bf16[256,256]{1,0:T(8,128)(2,1)S(1)} collective-permute-done((bf16[256,256]{1,0:T(8,128)(2,1)S(1)}, bf16[256,256]{1,0:T(8,128)(2,1)S(1)}, u32[]{:S(2)}, u32[]{:S(2)}) %collective-permute-start.1) | collective-permute-done | bytes 131104 | tf_op jit(solution)/shard_map/ppermute | solution.py:44
  38.0 0.4 collective-permute-start.3
  38.4 1.2 %shard_map.56 = (f32[1024,128]{1,0:T(8,128)S(1)}, f32[1024,256]{1,0:T(8,128)S(1)}) custom-call(s32[68]{0:T(128)S(1)} %pad_add_fusion.table_ref, bf16[256,512]{1,0:T(8,128)(2,1)S(1)} %slice.17.q_ref, bf16[512,256]{1,0:T(8,128)(2,1)S(1)} %constant_dynamic-update-slice_fusion.lower_ref, bf16[512,256]{1,0:T(8,128)(2,1)S(1)} %constant_dynamic-update-slice_fusion.2.upper_ref), custom_call_target="tpu_custom_call" | custom-call | tf_op jit(solution)/shard_map/pallas_call | solution.py:219
  39.7 0.0 copy-start
  39.7 3.2 %collective-permute-start.10 = (bf16[512,256]{1,0:T(8,128)(2,1)S(1)}, bf16[512,256]{1,0:T(8,128)(2,1)S(1)}, u32[]{:S(2)}, u32[]{:S(2)}) collective-permute-start(bf16[512,256]{1,0:T(8,128)(2,1)S(1)} %constant_dynamic-update-slice_fusion.2.upper_ref), channel_id=1, source_target_pairs={{0,16},{16,0},{1,17},{17,1},{2,18},{18,2},{3,19},{19,3},{4,20},{20... | collective-permute-start | bytes 786440 | tf_op jit(solution)/shard_map/ppermute | solution.py:44
  43.0 0.1 collective-permute-start.9
  43.1 0.0 collective-permute-done.rest_2_
  43.1 0.0 collective-permute-done.5.rest_4_
  43.1 0.7 %collective-permute-done.3.rest_3_ = bf16[384,256]{1,0:T(8,128)(2,1)S(1)} collective-permute-done((bf16[384,256]{1,0:T(8,128)(2,1)S(1)}, bf16[384,256]{1,0:T(8,128)(2,1)S(1)}, u32[]{:S(2)}, u32[]{:S(2)}) %collective-permute-start.3) | collective-permute-done | bytes 196640 | tf_op jit(solution)/shard_map/ppermute | solution.py:51
  43.8 4.0 %collective-permute-start.7 = (bf16[384,256]{1,0:T(8,128)(2,1)S(1)}, bf16[384,256]{1,0:T(8,128)(2,1)S(1)}, u32[]{:S(2)}, u32[]{:S(2)}) collective-permute-start(bf16[384,256]{1,0:T(8,128)(2,1)S(1)} %collective-permute-done.3.rest_3_), channel_id=1, source_target_pairs={{0,16},{16,0},{1,17},{17,1},{2,18},{18,2},{3,19},{19,3},{4,20},{20... | collective-permute-start | bytes 589832 | tf_op jit(solution)/shard_map/ppermute | solution.py:44
  47.8 0.0 collective-permute-start.8
  47.8 0.5 collective-permute-start.6
  48.4 1.6 %shard_map.57 = (f32[1024,128]{1,0:T(8,128)S(1)}, f32[1024,256]{1,0:T(8,128)S(1)}) custom-call(s32[68]{0:T(128)S(1)} %pad_add_fusion.table_ref, bf16[256,512]{1,0:T(8,128)(2,1)S(1)} %slice.17.q_ref, bf16[256,256]{1,0:T(8,128)(2,1)S(1)} %slice.16.fill_ref, bf16[512,256]{1,0:T(8,128)(2,1)S(1)} %collective-permute-done.9.rest_0_, ...), custom_call_target="tpu_custom_call" | custom-call | flops 1000000 | bytes 10000 | tf_op jit(solution)/shard_map/pallas_call | solution.py:230
  50.0 2.1 %shard_map.58 = bf16[1024,512]{1,0:T(8,128)(2,1)} custom-call(s32[68]{0:T(128)S(1)} %pad_add_fusion.table_ref, bf16[256,512]{1,0:T(8,128)(2,1)S(1)} %slice.17.q_ref, bf16[256,256]{1,0:T(8,128)(2,1)S(1)} %slice.16.fill_ref, bf16[256,256]{1,0:T(8,128)(2,1)S(1)} %collective-permute-done.6.own_ref, bf16[384,256]{1,0:T(8,128)(2,1)S(1)} %collective-permute-done.7.lower_ref, ...), custom_call_target="tpu_custom_call" | custom-call | tf_op jit(solution)/shard_map/pallas_call | solution.py:242
  (20 shorter events, 0.2 us)
Async XLA Ops:
  1.7 26.4 %all-to-all-start = ((bf16[16,16,768]{2,1,0:T(8,128)(2,1)}), bf16[16,16,768]{2,1,0:T(8,128)(2,1)S(1)}, u32[]{:S(2)}, u32[]{:S(2)}) async-start(bf16[16,16,768]{2,1,0:T(8,128)(2,1)} %shard_map.55), calls=%async_computation | async-start | bytes 786432 | tf_op jit(solution)/shard_map/all_to_all | solution.py:279
  13.3 0.7 %copy-start.1 = (s32[16,256]{1,0:T(8,128)S(1)}, s32[16,256]{1,0:T(8,128)}, u32[]{:S(2)}) copy-start(s32[16,256]{1,0:T(8,128)} %kept_ref.1) | copy-start | bytes 49156
  13.3 0.7 %copy-start.2 = (bf16[1,256]{1,0:T(2,128)(2,1)S(1)}, bf16[1,256]{1,0:T(2,128)(2,1)}, u32[]{:S(2)}) copy-start(bf16[1,256]{1,0:T(2,128)(2,1)} %param.9) | copy-start | bytes 1540
  28.2 5.4 %collective-permute-start.2 = (bf16[256,256]{1,0:T(8,128)(2,1)S(1)}, bf16[256,256]{1,0:T(8,128)(2,1)S(1)}, u32[]{:S(2)}, u32[]{:S(2)}) collective-permute-start(bf16[256,256]{1,0:T(8,128)(2,1)S(1)} %slice.16.fill_ref), channel_id=1, source_target_pairs={{0,128},{64,192},{128,0},{192,64},{1,129},{65,193},{129,1},{193,65... | collective-permute-start | bytes 393224 | tf_op jit(solution)/shard_map/ppermute | solution.py:44
  31.2 4.6 %collective-permute-start.4 = (bf16[256,256]{1,0:T(8,128)(2,1)S(1)}, bf16[256,256]{1,0:T(8,128)(2,1)S(1)}, u32[]{:S(2)}, u32[]{:S(2)}) collective-permute-start(bf16[256,256]{1,0:T(8,128)(2,1)S(1)} %slice.16.fill_ref), channel_id=1, source_target_pairs={{0,192},{64,0},{128,64},{192,128},{1,193},{65,1},{129,65},{193,129... | collective-permute-start | bytes 393224 | tf_op jit(solution)/shard_map/ppermute | solution.py:44
  32.0 6.0 %collective-permute-start.1 = (bf16[256,256]{1,0:T(8,128)(2,1)S(1)}, bf16[256,256]{1,0:T(8,128)(2,1)S(1)}, u32[]{:S(2)}, u32[]{:S(2)}) collective-permute-start(bf16[256,256]{1,0:T(8,128)(2,1)S(1)} %slice.16.fill_ref), channel_id=1, source_target_pairs={{0,64},{64,128},{128,192},{192,0},{1,65},{65,129},{129,193},{193,1... | collective-permute-start | bytes 393224 | tf_op jit(solution)/shard_map/ppermute | solution.py:44
  32.7 10.4 %collective-permute-start = (bf16[256,256]{1,0:T(8,128)(2,1)S(1)}, bf16[256,256]{1,0:T(8,128)(2,1)S(1)}, u32[]{:S(2)}, u32[]{:S(2)}) collective-permute-start(bf16[256,256]{1,0:T(8,128)(2,1)S(1)} %slice.16.fill_ref), channel_id=1, source_target_pairs={{0,32},{32,1},{1,33},{33,0},{2,34},{34,3},{3,35},{35,2},{4,36},{36... | collective-permute-start | bytes 393224 | tf_op jit(solution)/shard_map/ppermute | solution.py:51
  35.8 7.2 %collective-permute-start.5 = (bf16[384,256]{1,0:T(8,128)(2,1)S(1)}, bf16[384,256]{1,0:T(8,128)(2,1)S(1)}, u32[]{:S(2)}, u32[]{:S(2)}) collective-permute-start(bf16[384,256]{1,0:T(8,128)(2,1)S(1)} %pad_maximum_fusion.1), channel_id=1, source_target_pairs={{0,33},{32,0},{1,32},{33,1},{2,35},{34,2},{3,34},{35,3},{4,37},{36... | collective-permute-start | bytes 589832 | tf_op jit(solution)/shard_map/ppermute | solution.py:51
  38.0 5.8 %collective-permute-start.3 = (bf16[384,256]{1,0:T(8,128)(2,1)S(1)}, bf16[384,256]{1,0:T(8,128)(2,1)S(1)}, u32[]{:S(2)}, u32[]{:S(2)}) collective-permute-start(bf16[384,256]{1,0:T(8,128)(2,1)S(1)} %pad_maximum_fusion), channel_id=1, source_target_pairs={{0,32},{32,1},{1,33},{33,0},{2,34},{34,3},{3,35},{35,2},{4,36},{36... | collective-permute-start | bytes 589832 | tf_op jit(solution)/shard_map/ppermute | solution.py:51
  39.7 10.3 %copy-start = (bf16[1024,512]{1,0:T(8,128)(2,1)S(1)}, bf16[1024,512]{1,0:T(8,128)(2,1)}, u32[]{:S(2)}) copy-start(bf16[1024,512]{1,0:T(8,128)(2,1)} %residual_ref.1) | copy-start | bytes 3145732
  39.7 8.6 %collective-permute-start.10 = (bf16[512,256]{1,0:T(8,128)(2,1)S(1)}, bf16[512,256]{1,0:T(8,128)(2,1)S(1)}, u32[]{:S(2)}, u32[]{:S(2)}) collective-permute-start(bf16[512,256]{1,0:T(8,128)(2,1)S(1)} %constant_dynamic-update-slice_fusion.2.upper_ref), channel_id=1, source_target_pairs={{0,16},{16,0},{1,17},{17,1},{2,18},{18,2},{3,19},{19,3},{4,20},{20... | collective-permute-start | bytes 786440 | tf_op jit(solution)/shard_map/ppermute | solution.py:44
  43.0 5.4 %collective-permute-start.9 = (bf16[512,256]{1,0:T(8,128)(2,1)S(1)}, bf16[512,256]{1,0:T(8,128)(2,1)S(1)}, u32[]{:S(2)}, u32[]{:S(2)}) collective-permute-start(bf16[512,256]{1,0:T(8,128)(2,1)S(1)} %constant_dynamic-update-slice_fusion.lower_ref), channel_id=1, source_target_pairs={{0,16},{16,0},{1,17},{17,1},{2,18},{18,2},{3,19},{19,3},{4,20},{20... | collective-permute-start | bytes 786440 | tf_op jit(solution)/shard_map/ppermute | solution.py:44
  43.8 6.2 %collective-permute-start.7 = (bf16[384,256]{1,0:T(8,128)(2,1)S(1)}, bf16[384,256]{1,0:T(8,128)(2,1)S(1)}, u32[]{:S(2)}, u32[]{:S(2)}) collective-permute-start(bf16[384,256]{1,0:T(8,128)(2,1)S(1)} %collective-permute-done.3.rest_3_), channel_id=1, source_target_pairs={{0,16},{16,0},{1,17},{17,1},{2,18},{18,2},{3,19},{19,3},{4,20},{20... | collective-permute-start | bytes 589832 | tf_op jit(solution)/shard_map/ppermute | solution.py:44
  47.8 2.2 %collective-permute-start.8 = (bf16[384,256]{1,0:T(8,128)(2,1)S(1)}, bf16[384,256]{1,0:T(8,128)(2,1)S(1)}, u32[]{:S(2)}, u32[]{:S(2)}) collective-permute-start(bf16[384,256]{1,0:T(8,128)(2,1)S(1)} %collective-permute-done.5.rest_4_), channel_id=1, source_target_pairs={{0,16},{16,0},{1,17},{17,1},{2,18},{18,2},{3,19},{19,3},{4,20},{20... | collective-permute-start | bytes 589832 | tf_op jit(solution)/shard_map/ppermute | solution.py:44
  47.8 2.1 %collective-permute-start.6 = (bf16[256,256]{1,0:T(8,128)(2,1)S(1)}, bf16[256,256]{1,0:T(8,128)(2,1)S(1)}, u32[]{:S(2)}, u32[]{:S(2)}) collective-permute-start(bf16[256,256]{1,0:T(8,128)(2,1)S(1)} %collective-permute-done.rest_2_), channel_id=1, source_target_pairs={{0,16},{16,0},{1,17},{17,1},{2,18},{18,2},{3,19},{19,3},{4,20},{20... | collective-permute-start | bytes 393224 | tf_op jit(solution)/shard_map/ppermute | solution.py:44
